TPU v7x, 256 devices: a whole 4x4x8 slice. The times are simulated.
256 devices in a mesh: pair: 32 (over z, x), row: 8 (over y, core).
Axes of the slice: x: 4, y: 4, z: 8, core: 2. Of those that a mesh axis runs over, the one named last changes fastest.
Arguments:
- features: bfloat16 [64, 8, 32, 1024], P('pair', 'row'), may hold values from -6 to 6
- src_ids: int32 [64], replicated, may hold values from 0 to 63
- tgt_ids: int32 [64], replicated, may hold values from 0 to 63
- image_slot: int32 [64], replicated, may hold values from 0 to 63, each once
- w_first: bfloat16 [81, 16, 1], replicated, may hold values from -0.625 to 0.625
- w_mid: bfloat16 [81, 16, 16], replicated, may hold values from -0.15625 to 0.15625
- w_last: bfloat16 [81, 1, 16], replicated, may hold values from -0.15625 to 0.15625
Outputs:
- matches: bfloat16 [64, 8, 32, 256], P('pair', 'row')
All inputs are finite; a program needn't handle non-finite values.
Results may differ from a plain program's by a relative error of at most 0.012.
The roundings to bfloat16 on the way count: a program that leaves them out, or rounds other values in their place, can miss the bound.
Values may be sent and summed in bfloat16 or wider, within the bound.
No kernel may reach another device: no remote copies, remote signals or barrier semaphores. Data moves between devices by JAX's collectives and lax.ppermute only.
A program may use at most 64 MiB of HBM per device.

v0:
```python
import jax
import jax.numpy as jnp
from jax import lax
from jax.sharding import PartitionSpec as P

WID = 32


EPSILON = 1e-05
NORM_EPS = 1e-06


def with_halo(cells, sides, width):
    for axis, dim in sides:
        count = lax.axis_size(axis)
        ends = count - 1
        head = lax.slice_in_dim(cells, 0, width, axis=dim)
        tail = lax.slice_in_dim(cells, cells.shape[dim] - width, cells.shape[dim], axis=dim)
        cells = jnp.concatenate(
            [
                lax.ppermute(tail, axis, [(i, (i + 1) % count) for i in range(ends)]),
                cells,
                lax.ppermute(head, axis, [((i + 1) % count, i) for i in range(ends)]),
            ],
            axis=dim,
        )
    return cells


def slot_lookup(image_ids, image_slot):
    matches = image_ids[..., None] == jnp.arange(image_slot.shape[0], dtype=jnp.int32)
    return jnp.sum(jnp.where(matches, image_slot, 0), axis=-1)


def consensus_layer(tensor, weight, col_masks, is_last):
    group_pairs = tensor.shape[0]
    channels_in = tensor.shape[1]
    positions = tensor.shape[4]
    channels_out = weight.shape[1]
    rimmed = with_halo(tensor, (("row", 2),), 1)
    padded = jnp.pad(rimmed, ((0, 0), (0, 0), (0, 0), (1, 1), (0, 0)))
    matrix = (
        weight.reshape(9, 9, channels_out, channels_in)
        .transpose(1, 2, 0, 3)
        .reshape(9 * channels_out, 9 * channels_in)
    )
    results = []
    for member in range(group_pairs):
        stacked = jnp.stack(
            [padded[member, :, a, b : b + WID, :] for a in range(3) for b in range(3)]
        )
        product = jnp.dot(
            matrix,
            stacked.reshape(9 * channels_in, WID * positions),
            preferred_element_type=jnp.float32,
        )
        product = product.reshape(9, channels_out, WID, positions)
        summed = jnp.zeros((channels_out, WID, positions), jnp.float32)
        for c in range(3):
            for d in range(3):
                offset = (c - 1) * WID + (d - 1)
                widened = jnp.pad(product[c * 3 + d], ((0, 0), (0, 0), (WID + 1, WID + 1)))
                shifted = widened[:, :, WID + 1 + offset : WID + 1 + offset + positions]
                summed = summed + shifted * col_masks[d]
        outputs = [jax.nn.relu(summed)]
        results.append(jnp.stack(outputs, axis=1))
    result = jnp.stack(results, axis=0)
    if is_last:
        return result
    return result.astype(jnp.bfloat16)


def local(features, src_ids, tgt_ids, image_slot, w_first, w_mid, w_last):
    local_images, local_rows, columns, channels = features.shape
    block_rows = local_rows * columns
    flattened = features.reshape(local_images, block_rows, channels).astype(jnp.float32)
    scale = lax.rsqrt(jnp.sum(flattened * flattened, axis=-1, keepdims=True) + NORM_EPS)
    normed = (flattened * scale).astype(jnp.bfloat16)
    group_pairs = src_ids.shape[0] // lax.axis_size("pair")
    pair_index = lax.axis_index("pair")
    wanted_ids = jnp.stack([src_ids, tgt_ids], axis=1)
    pair_block = 2 * group_pairs * block_rows
    wanted = slot_lookup(wanted_ids, image_slot).reshape(-1, 2 * group_pairs)
    first_slot = pair_index * local_images
    one_hot = (wanted[..., None] == first_slot + jnp.arange(local_images, dtype=jnp.int32)).astype(
        jnp.bfloat16
    )
    contribution = jnp.einsum("gwk,krc->gwrc", one_hot, normed, preferred_element_type=jnp.float32)
    shares = lax.psum_scatter(
        contribution.reshape(pair_block * lax.axis_size("pair"), channels).astype(jnp.bfloat16),
        "pair",
        scatter_dimension=0,
        tiled=True,
    ).astype(jnp.float32)
    routed = shares.reshape(2 * group_pairs, block_rows, channels).astype(jnp.bfloat16)
    routed = routed.reshape(group_pairs, 2, block_rows, channels)
    sources = routed[:, 0]
    targets = routed[:, 1]
    correlation = jnp.einsum(
        "prc,ptc->prt",
        sources,
        lax.all_gather(targets, "row", axis=1, tiled=True),
        preferred_element_type=jnp.float32,
    )
    positions = correlation.shape[2]
    tensor = correlation.astype(jnp.bfloat16).reshape(
        group_pairs, 1, local_rows, columns, positions
    )
    target_col = jnp.arange(positions, dtype=jnp.int32) % WID
    col_masks = [
        ((target_col + d - 1 >= 0) & (target_col + d - 1 < WID)).astype(jnp.float32)
        for d in range(3)
    ]
    hidden_one = consensus_layer(tensor, w_first, col_masks, False)
    hidden_two = consensus_layer(hidden_one, w_mid, col_masks, False)
    consensus = consensus_layer(hidden_two, w_last, col_masks, True)[:, 0]
    target_best = jnp.max(consensus, axis=-1, keepdims=True)
    local_best = jnp.max(consensus, axis=(1, 2))
    source_best = lax.pmax(local_best, "row")
    matches = (
        consensus
        / (source_best[:, None, None, :] + EPSILON)
        * (consensus / (target_best + EPSILON))
    )
    return matches.astype(jnp.bfloat16)


def solution(mesh):
    placed = (P("pair", "row", None, None), P(), P(), P(), P(), P(), P())
    return jax.shard_map(
        local, mesh=mesh, in_specs=placed, out_specs=P("pair", "row", None, None), check_vma=False
    )
```

profile of v0, /device:TPU:1, one launch (start us, length us, event | category | flops | bytes accessed | tf_op | source)
XLA Modules:
  0.0 380.1 jit_solution(3491957866424239233)
XLA Ops:
  6.5 1.0 fusion.84
  7.6 1.0 fusion.85
  8.6 0.7 pad_add_fusion
  9.2 0.8 select_reduce_fusion
  10.3 4.8 %convolution_convert_fusion = bf16[32,4,32,1024]{3,0,2,1:T(8,128)(2,1)} fusion(bf16[2,32,1024]{2,1,0:T(8,128)(2,1)S(1)} %fusion.85, s32[32,4]{0,1:T(4,128)S(1)} %copy.25, s32[2]{0:T(128)S(1)} %iota_add_fusion), kind=kOutput, calls=%fused_computation.6 | convolution fusion | flops 20971776 | bytes 8520200 | tf_op jit(solution)/shard_map/gwk,krc->gwrc/dot_general | solution.py:88
  15.1 11.3 %copy.27 = bf16[32,4,32,1024]{3,2,1,0:T(8,128)(2,1)} copy(bf16[32,4,32,1024]{3,0,2,1:T(8,128)(2,1)} %convolution_convert_fusion) | data formatting | bytes 16777216 | tf_op jit(solution)/shard_map/convert_element_type | solution.py:90
  26.5 228.5 %reduce-scatter.2.cloned.1.call-done = bf16[128,1024]{1,0:T(8,128)(2,1)} async-done(((bf16[4096,1024]{1,0:T(8,128)(2,1)}), bf16[128,1024]{1,0:T(8,128)(2,1)}) %reduce-scatter.2.cloned.1.call-update) | async-done | bytes 262160 | tf_op jit(solution)/shard_map/reduce_scatter | solution.py:89
  255.0 1.6 slice_bitcast_fusion.32
  257.4 28.3 %all-gather.3.cloned.1.call-done = bf16[2,1,256,1024]{3,2,0,1:T(8,128)(2,1)} async-done(((bf16[2,1,32,1024]{3,2,0,1:T(8,128)(2,1)}), bf16[2,1,256,1024]{3,2,0,1:T(8,128)(2,1)}) %all-gather.3.cloned.1.call-update) | async-done | bytes 1048592 | tf_op jit(solution)/shard_map/all_gather | solution.py:102
  285.7 1.7 convolution_convert_fusion.1
  287.4 1.9 collective-permute-start
  289.4 2.9 collective-permute-start.1
  292.4 2.3 collective-permute-done.1
  295.4 0.8 convolution_bitcast_fusion.3
  297.7 0.9 copy.55
  298.6 1.0 copy.56
  299.6 1.0 copy.52
  301.9 0.6 copy.65
  302.5 0.6 copy.58
  303.8 2.0 stack.103
  305.8 0.8 convolution_bitcast_fusion.2
  309.2 1.2 fusion.22
  310.4 1.2 fusion.40
  311.6 1.9 collective-permute-start.2
  313.6 2.4 collective-permute-start.3
  316.9 2.8 collective-permute-done.2
  319.7 4.4 %collective-permute-done.3 = bf16[2,16,1,32,256]{4,3,1,2,0:T(8,128)(2,1)S(1)} collective-permute-done((bf16[2,16,1,32,256]{4,3,1,2,0:T(8,128)(2,1)S(1)}, bf16[2,16,1,32,256]{4,3,1,2,0:T(8,128)(2,1)S(1)}, u32[]{:S(2)}, u32[]{:S(2)}) %collective-permute-start.3) | collective-permute-done | bytes 524320 | tf_op jit(solution)/shard_map/ppermute | solution.py:23
  324.1 1.2 fusion.8
  325.9 1.6 copy.75
  327.5 0.8 convolution_bitcast_fusion.1
  330.4 1.6 copy.85
  332.0 0.8 convolution_bitcast_fusion
  334.7 1.2 fusion.58
  335.9 1.2 fusion.76
  337.1 1.9 collective-permute-start.4
  339.0 2.4 collective-permute-start.5
  341.7 3.4 collective-permute-done.4
  345.1 4.4 %collective-permute-done.5 = bf16[2,16,1,32,256]{4,3,1,2,0:T(8,128)(2,1)S(1)} collective-permute-done((bf16[2,16,1,32,256]{4,3,1,2,0:T(8,128)(2,1)S(1)}, bf16[2,16,1,32,256]{4,3,1,2,0:T(8,128)(2,1)S(1)}, u32[]{:S(2)}, u32[]{:S(2)}) %collective-permute-start.5) | collective-permute-done | bytes 524320 | tf_op jit(solution)/shard_map/ppermute | solution.py:23
  349.5 1.2 select_maximum_fusion
  351.4 1.4 copy-done
  352.8 1.6 copy.95
  354.8 0.7 slice_reduce_fusion.13
  355.8 0.7 fusion.87
  356.5 0.8 fusion.86
  357.3 3.3 copy.96
  361.0 0.7 slice_reduce_fusion.4
  362.3 10.0 %pmax.7 = f32[2,256]{1,0:T(2,128)S(1)} all-reduce(f32[2,256]{1,0:T(2,128)S(1)} %get-tuple-element.23), channel_id=1, replica_groups=mesh['pair'=32,'row'=8] {'row'}, use_global_device_ids=true, to_apply=%region_4.5 | all-reduce | flops 512 | bytes 4096 | tf_op jit(solution)/shard_map/pmax | solution.py:119
  372.3 0.7 fusion.127
  (149 shorter events, 15.2 us)
Async XLA Ops:
  6.5 248.5 %reduce-scatter.2.cloned.1.call-start = ((), (), s32[]{:S(2)}) async-start(), calls=%async_computation.1 | async-start | bytes 8650752 | tf_op jit(solution)/shard_map/reduce_scatter | solution.py:89
  26.4 230.2 %copy-start.7 = (bf16[81,16,1]{0,1,2:T(8,128)(2,1)S(1)}, bf16[81,16,1]{0,1,2:T(8,128)(2,1)}, u32[]{:S(2)}) copy-start(bf16[81,16,1]{0,1,2:T(8,128)(2,1)} %param.11) | copy-start | bytes 7780
  26.5 259.3 %all-gather.3.cloned.1.call-start = ((), (), s32[]{:S(2)}) async-start(), calls=%async_computation.2 | async-start | bytes 1179648 | tf_op jit(solution)/shard_map/all_gather | solution.py:102
  287.4 4.9 %collective-permute-start = (bf16[2,1,1,32,256]{4,3,0,2,1:T(8,128)(2,1)S(1)}, bf16[2,1,1,32,256]{4,3,0,2,1:T(8,128)(2,1)S(1)}, u32[]{:S(2)}, u32[]{:S(2)}) collective-permute-start(bf16[2,1,1,32,256]{4,3,0,2,1:T(8,128)(2,1)S(1)} %bitcast.487), channel_id=1, source_target_pairs={{0,1},{1,2},{2,3},{3,4},{4,5},{5,6},{6,7},{8,9},{9,10},{10,11},{11... | collective-permute-start | bytes 98312 | tf_op jit(solution)/shard_map/ppermute | solution.py:21
  289.4 5.2 %collective-permute-start.1 = (bf16[2,1,1,32,256]{4,3,0,2,1:T(8,128)(2,1)S(1)}, bf16[2,1,1,32,256]{4,3,0,2,1:T(8,128)(2,1)S(1)}, u32[]{:S(2)}, u32[]{:S(2)}) collective-permute-start(bf16[2,1,1,32,256]{4,3,0,2,1:T(8,128)(2,1)S(1)} %bitcast.488), channel_id=1, source_target_pairs={{1,0},{2,1},{3,2},{4,3},{5,4},{6,5},{7,6},{9,8},{10,9},{11,10},{12... | collective-permute-start | bytes 98312 | tf_op jit(solution)/shard_map/ppermute | solution.py:23
  307.9 1.0 copy-start.1
  307.9 1.2 copy-start.2
  307.9 1.3 copy-start.3
  307.9 1.3 copy-start.5
  310.4 5.6 %copy-start.4 = (bf16[81,16,16]{0,2,1:T(8,128)(2,1)S(1)}, bf16[81,16,16]{0,2,1:T(8,128)(2,1)}, u32[]{:S(2)}) copy-start(bf16[81,16,16]{0,2,1:T(8,128)(2,1)} %param.12) | copy-start | bytes 124420
  311.6 8.0 %collective-permute-start.2 = (bf16[2,16,1,32,256]{4,3,1,2,0:T(8,128)(2,1)S(1)}, bf16[2,16,1,32,256]{4,3,1,2,0:T(8,128)(2,1)S(1)}, u32[]{:S(2)}, u32[]{:S(2)}) collective-permute-start(bf16[2,16,1,32,256]{4,3,1,2,0:T(8,128)(2,1)S(1)} %pad_maximum_fusion), channel_id=1, source_target_pairs={{0,1},{1,2},{2,3},{3,4},{4,5},{5,6},{6,7},{8,9},{9,10},{10,11},{11... | collective-permute-start | bytes 1572872 | tf_op jit(solution)/shard_map/ppermute | solution.py:21
  313.6 10.5 %collective-permute-start.3 = (bf16[2,16,1,32,256]{4,3,1,2,0:T(8,128)(2,1)S(1)}, bf16[2,16,1,32,256]{4,3,1,2,0:T(8,128)(2,1)S(1)}, u32[]{:S(2)}, u32[]{:S(2)}) collective-permute-start(bf16[2,16,1,32,256]{4,3,1,2,0:T(8,128)(2,1)S(1)} %pad_maximum_fusion), channel_id=1, source_target_pairs={{1,0},{2,1},{3,2},{4,3},{5,4},{6,5},{7,6},{9,8},{10,9},{11,10},{12... | collective-permute-start | bytes 1572872 | tf_op jit(solution)/shard_map/ppermute | solution.py:23
  335.8 5.6 %copy-start.8 = (bf16[81,1,16]{0,2,1:T(8,128)(2,1)S(1)}, bf16[81,1,16]{0,2,1:T(8,128)(2,1)}, u32[]{:S(2)}) copy-start(bf16[81,1,16]{0,2,1:T(8,128)(2,1)} %param.13) | copy-start | bytes 7780
  337.1 8.0 %collective-permute-start.4 = (bf16[2,16,1,32,256]{4,3,1,2,0:T(8,128)(2,1)S(1)}, bf16[2,16,1,32,256]{4,3,1,2,0:T(8,128)(2,1)S(1)}, u32[]{:S(2)}, u32[]{:S(2)}) collective-permute-start(bf16[2,16,1,32,256]{4,3,1,2,0:T(8,128)(2,1)S(1)} %pad_maximum_fusion.1), channel_id=1, source_target_pairs={{0,1},{1,2},{2,3},{3,4},{4,5},{5,6},{6,7},{8,9},{9,10},{10,11},{11... | collective-permute-start | bytes 1572872 | tf_op jit(solution)/shard_map/ppermute | solution.py:21
  339.0 10.5 %collective-permute-start.5 = (bf16[2,16,1,32,256]{4,3,1,2,0:T(8,128)(2,1)S(1)}, bf16[2,16,1,32,256]{4,3,1,2,0:T(8,128)(2,1)S(1)}, u32[]{:S(2)}, u32[]{:S(2)}) collective-permute-start(bf16[2,16,1,32,256]{4,3,1,2,0:T(8,128)(2,1)S(1)} %pad_maximum_fusion.1), channel_id=1, source_target_pairs={{1,0},{2,1},{3,2},{4,3},{5,4},{6,5},{7,6},{9,8},{10,9},{11,10},{12... | collective-permute-start | bytes 1572872 | tf_op jit(solution)/shard_map/ppermute | solution.py:23
  351.4 1.4 copy-start
  360.6 1.4 copy-start.6
Sparse Core Ops, SparseCore 0:
  26.6 228.3 reduce-scatter.1
  257.0 28.6 all-gather.2
where the time goes:
time: 387 us; the launch traced here: 380 us
  waiting for transfers between devices  274 us (71%)
  local copies, waits for them, and re-layouts  44.8 us (12%)
  between operations  14.7 us (4%)
  starting transfers between devices  13.5 us (3%)
  other arithmetic  12.4 us (3%)
  matrix products  10.5 us (3%)
  blocking collectives  10 us (3%)
    reduce_scatter x1, waiting for transfers between devices, local(): lax.psum_scatter(contribution.reshape(pair_block * lax.axis_size('pair'),...  229 us
    all_gather x1, waiting for transfers between devices, local(): lax.all_gather(targets, 'row', axis=1, tiled=True)  28.3 us
    unnamed x106, local copies, waits for them, and re-layouts  25.7 us
    convert_element_type x1, local copies, waits for them, and re-layouts, local(): contribution.reshape(pair_block * lax.axis_size('pair'), channels)  11.3 us
    ppermute x3, waiting for transfers between devices, with_halo(): lax.ppermute(head, axis, [((i + 1) % count, i) for i in range(ends)])  11.1 us
    pmax x1, blocking collectives, local(): source_best = lax.pmax(local_best, 'row')  10 us
  transfers between devices with their start and end apart: 8, of which 7 were waited for; matrix products, arithmetic and copies ran while one was open for 1% of the time, Pallas kernels for 0%

commit v1 on v0

v1 whole, which is shorter than its diff:
```python
import functools

import jax
import jax.numpy as jnp
from jax import lax
from jax.experimental import pallas as pl
from jax.experimental.pallas import tpu as pltpu
from jax.sharding import PartitionSpec as P

WID = 32
HGT = 8
POS = HGT * WID
CONV = 16
EPSILON = 1e-05
NORM_EPS = 1e-06
BF16 = jnp.bfloat16
F32 = jnp.float32

CHIPS = 4
BLOCK = WID // CHIPS
COLS_IN, COLS_1, COLS_2 = BLOCK + 8, BLOCK + 4, BLOCK + 2
HALF = COLS_2 // 2
ROWS_1, ROWS_2 = COLS_1 * CONV, COLS_2 * CONV
K_1 = 27 * COLS_IN
K_PIECE = (HALF + 2) * CONV
K_2 = 9 * K_PIECE
M_2 = HALF * CONV


def whole(space=pltpu.VMEM):
    return pl.BlockSpec(memory_space=space)


def call(kernel, out_shape, inputs, scalars=(), scratch=()):
    return pl.pallas_call(
        kernel,
        out_shape=out_shape,
        in_specs=[whole(pltpu.SMEM)] * len(scalars) + [whole()] * len(inputs),
        out_specs=jax.tree.map(lambda _: whole(), out_shape),
        scratch_shapes=list(scratch),
        compiler_params=pltpu.CompilerParams(vmem_limit_bytes=40 * 1024 * 1024),
    )(*scalars, *inputs)


def spread_kernel(core_ref, own_ref, other_ref, out_ref, rows_ref):
    core = core_ref[0]
    images = own_ref.shape[0]
    for ref, place in ((own_ref, core), (other_ref, 1 - core)):
        for image in range(images):
            cells = ref[image, 0].astype(F32)
            scale = lax.rsqrt(jnp.sum(cells * cells, axis=-1, keepdims=True) + NORM_EPS)
            rows_ref[place, image] = (cells * scale).astype(BF16)
    for row in range(2):
        for half in range(2):
            for block in range(8):
                for image in range(images):
                    out_ref[(row * 2 + half) * 8 + block, image] = rows_ref[
                        row, image, half * 16 : half * 16 + 16, block * 128 : block * 128 + 128
                    ]


def select_kernel(core_ref, src_ref, tgt_ref, slot_ref, held_ref, out_ref):
    core = core_ref[0]
    for group in range(out_ref.shape[0]):
        pair = 2 * group + core
        out_ref[group, 0] = held_ref[slot_ref[src_ref[pair]]]
        out_ref[group, 1] = held_ref[slot_ref[tgt_ref[pair]]]


def pack_kernel(chip_ref, held_ref, out_0, out_1, out_2, out_3, windows_ref):
    chip = chip_ref[0]
    for row in range(2):
        for block in range(8):
            left = held_ref[row * 16 + block, 0].astype(F32)
            right = held_ref[row * 16 + 8 + block, 0].astype(F32)
            edge = jnp.zeros((4, 128), F32)
            line = jnp.concatenate([edge, left, right, edge], axis=0)
            for y in range(CHIPS):
                windows_ref[y, row * 8 + block] = line[y * BLOCK : y * BLOCK + 16].astype(BF16)
    for step, out_ref in enumerate((out_0, out_1, out_2, out_3)):
        for tile in range(32):
            out_ref[tile] = held_ref[tile, 1]
        out_ref[32:48] = windows_ref[lax.rem(chip + step, CHIPS)]


def shifted(values, offset):
    amount = (-offset) % POS
    return pltpu.roll(values, amount, values.ndim - 1) if amount else values


def consensus_kernel(
    chip_ref, got_0, got_1, got_2, got_3, z1_ref, z2_ref, z3_ref, out_ref, src, tgt, x1, x2, h2, w3s
):
    chip = chip_ref[0]
    for step, got in enumerate((got_0, got_1, got_2, got_3)):
        origin = lax.rem(chip + CHIPS - step, CHIPS)
        for quarter in range(4):
            rows = pl.ds(pl.multiple_of(origin * 64 + quarter * 16, 16), 16)
            for block in range(8):
                tgt[rows, block * 128 : block * 128 + 128] = got[quarter * 8 + block]
        for row in range(2):
            rows = pl.ds(pl.multiple_of(origin * 32 + row * 16, 16), 16)
            for block in range(8):
                src[rows, block * 128 : block * 128 + 128] = got[32 + row * 8 + block]
    corr = lax.dot_general(src[...], tgt[...], (((1,), (1,)), ((), ())), preferred_element_type=F32)
    corr = corr.astype(BF16).astype(F32)

    column = lax.broadcasted_iota(jnp.int32, (1, POS), 1)
    line = column // WID
    column = column % WID

    def col_mask(d):
        return ((column + d - 1 >= 0) & (column + d - 1 < WID)).astype(F32)

    def line_mask(c):
        return ((line + c - 1 >= 0) & (line + c - 1 < HGT)).astype(F32)

    has_left = (chip > 0).astype(F32)
    has_right = (chip < CHIPS - 1).astype(F32)

    z1 = z1_ref[...].astype(F32)
    w1 = jnp.concatenate([pltpu.roll(z1, j, 1) if j else z1 for j in range(COLS_1)], axis=0).astype(BF16)[:, :K_1]
    z2 = z2_ref[...].astype(F32)
    rolled = [pltpu.roll(z2, CONV * j, 1) if j else z2 for j in range(HALF)]
    w2 = jnp.concatenate(
        [rolled[j][c * CONV : c * CONV + CONV] for c in range(3) for j in range(HALF)], axis=0
    ).astype(BF16)[:, :K_2]
    z3 = z3_ref[...].astype(F32)
    for j in range(BLOCK):
        w3s[:, j, :] = pltpu.roll(z3, CONV * j, 1) if j else z3
    w3 = w3s[...].reshape(27 * BLOCK, 256).astype(BF16)[:, :ROWS_2]

    for c in range(3):
        for d in range(3):
            moved = shifted(corr, WID * (c - 1) + d - 1) * (line_mask(c) * col_mask(d))
            x1[c * 3 + d, 0:16] = jnp.zeros((16, POS), BF16)
            x1[c * 3 + d, 16 : 16 + 128] = moved.astype(BF16)
            x1[c * 3 + d, 144:160] = jnp.zeros((16, POS), BF16)
    for d in range(3):
        x2[d, 0:ROWS_1] = jnp.zeros((ROWS_1, POS), BF16)
        x2[d, (HGT + 1) * ROWS_1 :] = jnp.zeros((ROWS_1, POS), BF16)
    left_mask, right_mask = col_mask(0), col_mask(2)
    for i in range(HGT):
        cells = jnp.concatenate([x1[k, 16 * i : 16 * i + 48] for k in range(9)], axis=0)
        hidden = jnp.maximum(jnp.dot(w1, cells, preferred_element_type=F32), 0.0)
        edge = 2 * CONV
        hidden = jnp.concatenate(
            [hidden[:edge] * has_left, hidden[edge : ROWS_1 - edge], hidden[ROWS_1 - edge :] * has_right], axis=0
        )
        at = (i + 1) * ROWS_1
        x2[0, at : at + ROWS_1] = (shifted(hidden, -1) * left_mask).astype(BF16)
        x2[1, at : at + ROWS_1] = hidden.astype(BF16)
        x2[2, at : at + ROWS_1] = (shifted(hidden, 1) * right_mask).astype(BF16)

    up_mask, down_mask = line_mask(0), line_mask(2)
    for i in range(HGT):
        for half in range(2):
            first = half * HALF * CONV
            cells = jnp.concatenate(
                [x2[d, (i + a) * ROWS_1 + first : (i + a) * ROWS_1 + first + K_PIECE] for d in range(3) for a in range(3)],
                axis=0,
            )
            parts = jnp.dot(w2, cells, preferred_element_type=F32)
            total = parts[M_2 : 2 * M_2]
            total = total + shifted(parts[:M_2], -WID) * up_mask
            total = total + shifted(parts[2 * M_2 :], WID) * down_mask
            total = jnp.maximum(total, 0.0)
            if half == 0:
                total = jnp.concatenate([total[:CONV] * has_left, total[CONV:]], axis=0)
            else:
                total = jnp.concatenate([total[: M_2 - CONV], total[M_2 - CONV :] * has_right], axis=0)
            h2[i, first : first + M_2] = total.astype(BF16)

    sums = [None] * HGT
    for i in range(HGT):
        parts = jnp.dot(w3, h2[i], preferred_element_type=F32)
        for a in range(3):
            o = i + 1 - a
            if 0 <= o < HGT:
                part = parts[a * 9 * BLOCK : (a + 1) * 9 * BLOCK]
                sums[o] = part if sums[o] is None else sums[o] + part
    best = None
    scores = []
    for i in range(HGT):
        total = None
        for c in range(3):
            for d in range(3):
                k = (c * 3 + d) * BLOCK
                part = shifted(sums[i][k : k + BLOCK], WID * (c - 1) + d - 1) * (line_mask(c) * col_mask(d))
                total = part if total is None else total + part
        total = jnp.maximum(total, 0.0)
        top = jnp.max(total, axis=0, keepdims=True)
        best = top if best is None else jnp.maximum(best, top)
        target_best = jnp.max(total, axis=1, keepdims=True)
        scores.append(total * (total / (target_best + EPSILON)))
    pieces = []
    rest = best
    for _ in range(3):
        piece = rest.astype(BF16).astype(F32)
        pieces.append(piece)
        rest = rest - piece
    pieces.append(jnp.zeros((5, POS), F32))
    pieces = jnp.concatenate(pieces, axis=0)
    for i in range(HGT):
        out_ref[i] = jnp.concatenate([scores[i], pieces], axis=0).astype(BF16)


def finish_kernel(got_ref, out_ref):
    for pair in range(2):
        best = None
        for chip in range(CHIPS):
            top = got_ref[2 * chip + pair].astype(F32)
            top = top[8:9] + top[9:10] + top[10:11]
            best = top if best is None else jnp.maximum(best, top)
        best = best + EPSILON
        lines = [got_ref[2 * chip + pair].astype(F32)[:8] / best for chip in range(CHIPS)]
        out_ref[pair, 0] = jnp.concatenate(lines, axis=0).astype(BF16)


def row_moves(chips, cores):
    return [(2 * y + c, 2 * ((y + chips) % CHIPS) + (c ^ cores)) for y in range(CHIPS) for c in range(2)]


def local(features, src_ids, tgt_ids, image_slot, w_first, w_mid, w_last):
    groups = lax.axis_size("pair")
    images, _, _, channels = features.shape
    place = lax.axis_index("row").astype(jnp.int32)
    chip = (place // 2).reshape(1)
    core = (place % 2).reshape(1)

    taps = w_first.reshape(3, 3, 3, 3, CONV).transpose(4, 2, 3, 0, 1)
    z1 = jnp.pad(taps, ((0, 0),) * 4 + ((1, COLS_IN - 4),)).reshape(CONV, K_1)
    z1 = jnp.pad(z1, ((0, 0), (0, 512 - K_1)))
    taps = w_mid.reshape(3, 3, 3, 3, CONV, CONV).transpose(2, 4, 3, 0, 1, 5)
    z2 = jnp.pad(taps, ((0, 0),) * 4 + ((0, HALF - 1), (0, 0))).reshape(3 * CONV, K_2)
    z2 = jnp.pad(z2, ((0, 0), (0, 1024 - K_2)))
    z3 = w_last.reshape(3, 3, 3, 3, CONV).transpose(0, 2, 3, 1, 4).reshape(27, 3 * CONV)
    z3 = jnp.pad(z3, ((0, 0), (0, 256 - 3 * CONV)))

    other = lax.ppermute(features, "row", row_moves(0, 1))
    tiles = call(
        spread_kernel,
        jax.ShapeDtypeStruct((groups, images, 16, 128), BF16),
        (features, other),
        (core,),
        (pltpu.VMEM((2, images, WID, channels), BF16),),
    )
    held = lax.all_to_all(tiles, "pair", 0, 0, tiled=True).reshape(groups * images, 16, 128)
    wanted = call(
        select_kernel,
        jax.ShapeDtypeStruct((groups, 2, 16, 128), BF16),
        (held,),
        (core, src_ids, tgt_ids, image_slot),
    )
    routed = lax.all_to_all(wanted, "pair", 0, 0, tiled=True)
    message = jax.ShapeDtypeStruct((48, 16, 128), BF16)
    sends = call(
        pack_kernel, (message,) * 4, (routed,), (chip,), (pltpu.VMEM((CHIPS, 16, 16, 128), BF16),)
    )
    gots = [sends[0]] + [lax.ppermute(sends[k], "row", row_moves(k, 0)) for k in range(1, CHIPS)]
    scores = call(
        consensus_kernel,
        jax.ShapeDtypeStruct((HGT, 16, POS), BF16),
        (*gots, z1, z2, z3),
        (chip,),
        (
            pltpu.VMEM((HGT * COLS_IN, channels), BF16),
            pltpu.VMEM((POS, channels), BF16),
            pltpu.VMEM((9, 160, POS), BF16),
            pltpu.VMEM((3, (HGT + 2) * ROWS_1, POS), BF16),
            pltpu.VMEM((HGT, ROWS_2, POS), BF16),
            pltpu.VMEM((27, BLOCK, 256), F32),
        ),
    )
    swapped = lax.all_to_all(scores, "row", 0, 0, tiled=True)
    return call(finish_kernel, jax.ShapeDtypeStruct((2, 1, WID, POS), BF16), (swapped,))


def solution(mesh):
    placed = (P("pair", "row", None, None), P(), P(), P(), P(), P(), P())
    return jax.shard_map(
        local, mesh=mesh, in_specs=placed, out_specs=P("pair", "row", None, None), check_vma=False
    )
```

time: 387 us -> 70.7 us (0.18); the launches traced: 380 us -> 70.4 us
  waiting for transfers between devices: 274 us -> 12.3 us
  local copies, waits for them, and re-layouts: 44.8 us -> 5.13 us
  blocking collectives: 10 us -> 33.9 us
  between operations: 14.7 us -> 0.14 us
  other arithmetic: 12.4 us -> 0 us
  matrix products: 10.5 us -> 0 us
  Pallas kernels: 0 us -> 6.01 us
    reduce_scatter x1 -> x0, waiting for transfers between devices: 229 us -> none  [local(): lax.psum_scatter(contribution.reshape(pair_block * lax.axis_size('pair'),...]
    all_to_all x0 -> x2, blocking collectives: none -> 33.9 us  [the longest x1 20.7 us: local(): lax.all_to_all(tiles, 'pair', 0, 0, tiled=True)]
    all_gather x1 -> x0, waiting for transfers between devices: 28.3 us -> none  [local(): lax.all_gather(targets, 'row', axis=1, tiled=True)]
    unnamed x106 -> x19, local copies, waits for them, and re-layouts: 25.7 us -> 3.95 us
    ppermute x6 -> x4, waiting for transfers between devices: 17.2 us -> 1.86 us  [the longest x1 1.2 us: local(): other = lax.ppermute(features, 'row', row_moves(0, 1))]
    convert_element_type x1 -> x0, local copies, waits for them, and re-layouts: 11.3 us -> none  [local(): contribution.reshape(pair_block * lax.axis_size('pair'), channels)]
    dot_general x8 -> x0, matrix products: 10.5 us -> none  [the longest x1 4.8 us: local(): jnp.einsum('gwk,krc->gwrc', one_hot, normed, preferred_element_type=jnp.f...]
    all_to_all x0 -> x1, waiting for transfers between devices: none -> 10.4 us  [local(): routed = lax.all_to_all(wanted, 'pair', 0, 0, tiled=True)]
  transfers between devices with their start and end apart: 8 -> 5, of which waited for: 7 -> 3; matrix products, arithmetic and copies ran while one was open for 1% -> 3% of each run, Pallas kernels for 0% -> 0%
where the time goes in v1:
time: 70.7 us; the launch traced here: 70.4 us
  blocking collectives  33.9 us (48%)
  starting transfers between devices  12.9 us (18%)
  waiting for transfers between devices  12.3 us (17%)
  Pallas kernels  6.01 us (9%)
  local copies, waits for them, and re-layouts  5.13 us (7%)
    all_to_all x1, blocking collectives, local(): lax.all_to_all(tiles, 'pair', 0, 0, tiled=True)  20.7 us
    all_to_all x1, blocking collectives, local(): swapped = lax.all_to_all(scores, 'row', 0, 0, tiled=True)  13.2 us
    all_to_all x1, waiting for transfers between devices, local(): routed = lax.all_to_all(wanted, 'pair', 0, 0, tiled=True)  10.4 us
    pallas_call x5, Pallas kernels, call(): pl.pallas_call(kernel, out_shape=out_shape, in_specs=[whole(pltpu.SMEM)]...  6.01 us
    ppermute x3, starting transfers between devices, local(): lax.ppermute(sends[k], 'row', row_moves(k, 0))  5.06 us
    all_to_all x1, starting transfers between devices, local(): routed = lax.all_to_all(wanted, 'pair', 0, 0, tiled=True)  4.59 us
    unnamed x19, local copies, waits for them, and re-layouts  3.95 us
    ppermute x1, starting transfers between devices, local(): other = lax.ppermute(features, 'row', row_moves(0, 1))  3.24 us
  transfers between devices with their start and end apart: 5, of which 3 were waited for; matrix products, arithmetic and copies ran while one was open for 3% of the time, Pallas kernels for 0%

profile of v1, /device:TPU:1, one launch (start us, length us, event | category | flops | bytes accessed | tf_op | source)
XLA Modules:
  0.0 70.4 jit_solution(16781418746017127847)
XLA Ops:
  0.0 3.2 %collective-permute-start = (bf16[2,1,32,1024]{3,2,1,0:T(8,128)(2,1)}, bf16[2,1,32,1024]{3,2,1,0:T(8,128)(2,1)S(1)}, u32[]{:S(2)}, u32[]{:S(2)}) collective-permute-start(bf16[2,1,32,1024]{3,2,1,0:T(8,128)(2,1)} %own_ref.1), channel_id=1, source_target_pairs={{0,1},{1,0},{2,3},{3,2},{4,5},{5,4},{6,7},{7,6},{8,9},{9,8},{10,11... | collective-permute-start | bytes 393224 | tf_op jit(solution)/shard_map/ppermute | solution.py:240
  3.2 1.2 %collective-permute-done.other_ref = bf16[2,1,32,1024]{3,2,1,0:T(8,128)(2,1)S(1)} collective-permute-done((bf16[2,1,32,1024]{3,2,1,0:T(8,128)(2,1)}, bf16[2,1,32,1024]{3,2,1,0:T(8,128)(2,1)S(1)}, u32[]{:S(2)}, u32[]{:S(2)}) %collective-permute-start) | collective-permute-done | bytes 131104 | tf_op jit(solution)/shard_map/ppermute | solution.py:240
  4.4 0.0 copy-start
  4.4 0.9 %copy-done = bf16[2,1,32,1024]{3,2,1,0:T(8,128)(2,1)S(1)} copy-done((bf16[2,1,32,1024]{3,2,1,0:T(8,128)(2,1)S(1)}, bf16[2,1,32,1024]{3,2,1,0:T(8,128)(2,1)}, u32[]{:S(2)}) %copy-start) | copy-done | bytes 131096
  5.3 0.2 shard_map.73
  5.5 20.7 %all_to_all.15 = bf16[32,2,16,128]{3,2,1,0:T(8,128)(2,1)S(1)} all-to-all(bf16[32,2,16,128]{3,2,1,0:T(8,128)(2,1)S(1)} %shard_map.73), channel_id=1, replica_groups=mesh['pair'=32,'row'=8] {'pair'}, dimensions={0} | all-to-all | bytes 524288 | tf_op jit(solution)/shard_map/all_to_all | solution.py:248
  26.2 0.0 copy-start.1
  26.2 0.0 copy-start.2
  26.2 0.0 copy-start.3
  26.2 0.6 copy-done.1
  26.9 0.0 copy-done.2
  26.9 0.0 copy-done.3
  26.9 1.3 %shard_map.74 = bf16[32,2,16,128]{3,2,1,0:T(8,128)(2,1)} custom-call(s32[1]{0:T(128)} %bitcast.1.core_ref, s32[64]{0:T(128)S(1)} %copy-done.1, s32[64]{0:T(128)S(1)} %copy-done.2, s32[64]{0:T(128)S(1)} %copy-done.3, bf16[64,16,128]{2,1,0:T(8,128)(2,1)S(1)} %bitcast.12), custom_call_target="tpu_custom_call" | custom-call | tf_op jit(solution)/shard_map/pallas_call | solution.py:35
  28.2 4.6 %all-to-all-start.1 = ((bf16[32,2,16,128]{3,2,1,0:T(8,128)(2,1)}), bf16[32,2,16,128]{3,2,1,0:T(8,128)(2,1)S(1)}, u32[]{:S(2)}, u32[]{:S(2)}) async-start(bf16[32,2,16,128]{3,2,1,0:T(8,128)(2,1)} %shard_map.74), calls=%async_computation.1 | async-start | bytes 524288 | tf_op jit(solution)/shard_map/all_to_all | solution.py:255
  32.9 10.4 %all-to-all-done.1.held_ref = bf16[32,2,16,128]{3,2,1,0:T(8,128)(2,1)S(1)} async-done(((bf16[32,2,16,128]{3,2,1,0:T(8,128)(2,1)}), bf16[32,2,16,128]{3,2,1,0:T(8,128)(2,1)S(1)}, u32[]{:S(2)}, u32[]{:S(2)}) %all-to-all-start.1) | async-done | bytes 262176 | tf_op jit(solution)/shard_map/all_to_all | solution.py:255
  43.3 0.1 shard_map.75
  43.4 0.0 copy-start.5
  43.4 1.4 %collective-permute-start.1 = (bf16[48,16,128]{2,1,0:T(8,128)(2,1)S(1)}, bf16[48,16,128]{2,1,0:T(8,128)(2,1)S(1)}, u32[]{:S(2)}, u32[]{:S(2)}) collective-permute-start(bf16[48,16,128]{2,1,0:T(8,128)(2,1)S(1)} %get-tuple-element.10), channel_id=1, source_target_pairs={{0,2},{1,3},{2,4},{3,5},{4,6},{5,7},{6,0},{7,1},{8,10},{9,11},{10,... | collective-permute-start | bytes 589832 | tf_op jit(solution)/shard_map/ppermute | solution.py:260
  44.8 2.6 %collective-permute-start.2 = (bf16[48,16,128]{2,1,0:T(8,128)(2,1)S(1)}, bf16[48,16,128]{2,1,0:T(8,128)(2,1)S(1)}, u32[]{:S(2)}, u32[]{:S(2)}) collective-permute-start(bf16[48,16,128]{2,1,0:T(8,128)(2,1)S(1)} %get-tuple-element.11), channel_id=1, source_target_pairs={{0,4},{1,5},{2,6},{3,7},{4,0},{5,1},{6,2},{7,3},{8,12},{9,13},{10,... | collective-permute-start | bytes 589832 | tf_op jit(solution)/shard_map/ppermute | solution.py:260
  47.4 1.1 %collective-permute-start.3 = (bf16[48,16,128]{2,1,0:T(8,128)(2,1)S(1)}, bf16[48,16,128]{2,1,0:T(8,128)(2,1)S(1)}, u32[]{:S(2)}, u32[]{:S(2)}) collective-permute-start(bf16[48,16,128]{2,1,0:T(8,128)(2,1)S(1)} %get-tuple-element.12), channel_id=1, source_target_pairs={{0,6},{1,7},{2,0},{3,1},{4,2},{5,3},{6,4},{7,5},{8,14},{9,15},{10,... | collective-permute-start | bytes 589832 | tf_op jit(solution)/shard_map/ppermute | solution.py:260
  48.4 0.0 copy-done.5
  48.5 0.1 copy.11
  48.6 0.0 copy-start.6
  48.6 0.7 copy-done.6
  49.3 0.1 copy.15
  49.4 0.1 reshape.35
  49.5 0.3 copy.17
  49.8 0.2 pad.20.clone
  50.0 0.0 copy-start.4
  50.0 0.1 reshape.31
  50.1 0.7 copy-done.4
  50.8 0.3 copy.13
  51.2 0.2 copy.18
  51.3 0.2 pad.22.clone
  51.6 0.5 reshape.33
  52.1 0.0 collective-permute-done.1.got_1
  52.1 0.7 collective-permute-done.2.got_2
  52.7 0.0 collective-permute-done.3.got_3
  52.8 3.7 %shard_map.76 = bf16[8,16,256]{2,1,0:T(8,128)(2,1)S(1)} custom-call(s32[1]{0:T(128)} %bitcast.chip_ref, bf16[48,16,128]{2,1,0:T(8,128)(2,1)S(1)} %get-tuple-element.9.got_0, bf16[48,16,128]{2,1,0:T(8,128)(2,1)S(1)} %collective-permute-done.1.got_1, bf16[48,16,128]{2,1,0:T(8,128)(2,1)S(1)} %collective-permute-done.2.got_2, ...), custom_call_target="tpu_custom_call" | custom-call | tf_op jit(solution)/shard_map/pallas_call | solution.py:35
  56.5 13.2 %all_to_all.16.got_ref = bf16[8,16,256]{2,1,0:T(8,128)(2,1)S(1)} all-to-all(bf16[8,16,256]{2,1,0:T(8,128)(2,1)S(1)} %shard_map.76), channel_id=1, replica_groups=mesh['pair'=32,'row'=8] {'row'}, dimensions={0} | all-to-all | bytes 131072 | tf_op jit(solution)/shard_map/all_to_all | solution.py:275
  69.7 0.6 shard_map.77
  (6 shorter events, 0.1 us)
Async XLA Ops:
  0.0 4.4 %collective-permute-start = (bf16[2,1,32,1024]{3,2,1,0:T(8,128)(2,1)}, bf16[2,1,32,1024]{3,2,1,0:T(8,128)(2,1)S(1)}, u32[]{:S(2)}, u32[]{:S(2)}) collective-permute-start(bf16[2,1,32,1024]{3,2,1,0:T(8,128)(2,1)} %own_ref.1), channel_id=1, source_target_pairs={{0,1},{1,0},{2,3},{3,2},{4,5},{5,4},{6,7},{7,6},{8,9},{9,8},{10,11... | collective-permute-start | bytes 393224 | tf_op jit(solution)/shard_map/ppermute | solution.py:240
  4.4 0.9 %copy-start = (bf16[2,1,32,1024]{3,2,1,0:T(8,128)(2,1)S(1)}, bf16[2,1,32,1024]{3,2,1,0:T(8,128)(2,1)}, u32[]{:S(2)}) copy-start(bf16[2,1,32,1024]{3,2,1,0:T(8,128)(2,1)} %own_ref.1) | copy-start | bytes 393220
  26.2 0.7 copy-start.1
  26.2 0.7 copy-start.2
  26.2 0.7 copy-start.3
  28.2 15.0 %all-to-all-start.1 = ((bf16[32,2,16,128]{3,2,1,0:T(8,128)(2,1)}), bf16[32,2,16,128]{3,2,1,0:T(8,128)(2,1)S(1)}, u32[]{:S(2)}, u32[]{:S(2)}) async-start(bf16[32,2,16,128]{3,2,1,0:T(8,128)(2,1)} %shard_map.74), calls=%async_computation.1 | async-start | bytes 524288 | tf_op jit(solution)/shard_map/all_to_all | solution.py:255
  43.4 5.1 %copy-start.5 = (bf16[81,16,1]{0,1,2:T(8,128)(2,1)S(1)}, bf16[81,16,1]{0,1,2:T(8,128)(2,1)}, u32[]{:S(2)}) copy-start(bf16[81,16,1]{0,1,2:T(8,128)(2,1)} %param.11) | copy-start | bytes 7780
  43.4 8.7 %collective-permute-start.1 = (bf16[48,16,128]{2,1,0:T(8,128)(2,1)S(1)}, bf16[48,16,128]{2,1,0:T(8,128)(2,1)S(1)}, u32[]{:S(2)}, u32[]{:S(2)}) collective-permute-start(bf16[48,16,128]{2,1,0:T(8,128)(2,1)S(1)} %get-tuple-element.10), channel_id=1, source_target_pairs={{0,2},{1,3},{2,4},{3,5},{4,6},{5,7},{6,0},{7,1},{8,10},{9,11},{10,... | collective-permute-start | bytes 589832 | tf_op jit(solution)/shard_map/ppermute | solution.py:260
  44.8 8.0 %collective-permute-start.2 = (bf16[48,16,128]{2,1,0:T(8,128)(2,1)S(1)}, bf16[48,16,128]{2,1,0:T(8,128)(2,1)S(1)}, u32[]{:S(2)}, u32[]{:S(2)}) collective-permute-start(bf16[48,16,128]{2,1,0:T(8,128)(2,1)S(1)} %get-tuple-element.11), channel_id=1, source_target_pairs={{0,4},{1,5},{2,6},{3,7},{4,0},{5,1},{6,2},{7,3},{8,12},{9,13},{10,... | collective-permute-start | bytes 589832 | tf_op jit(solution)/shard_map/ppermute | solution.py:260
  47.4 5.4 %collective-permute-start.3 = (bf16[48,16,128]{2,1,0:T(8,128)(2,1)S(1)}, bf16[48,16,128]{2,1,0:T(8,128)(2,1)S(1)}, u32[]{:S(2)}, u32[]{:S(2)}) collective-permute-start(bf16[48,16,128]{2,1,0:T(8,128)(2,1)S(1)} %get-tuple-element.12), channel_id=1, source_target_pairs={{0,6},{1,7},{2,0},{3,1},{4,2},{5,3},{6,4},{7,5},{8,14},{9,15},{10,... | collective-permute-start | bytes 589832 | tf_op jit(solution)/shard_map/ppermute | solution.py:260
  48.6 0.7 copy-start.6
  50.0 0.8 %copy-start.4 = (bf16[81,16,16]{0,2,1:T(8,128)(2,1)S(1)}, bf16[81,16,16]{0,2,1:T(8,128)(2,1)}, u32[]{:S(2)}) copy-start(bf16[81,16,16]{0,2,1:T(8,128)(2,1)} %param.12) | copy-start | bytes 124420

commit v2 on v1

v2 whole, which is shorter than its diff:
```python
import jax
import jax.numpy as jnp
from jax import lax
from jax.experimental import pallas as pl
from jax.experimental.pallas import tpu as pltpu
from jax.sharding import PartitionSpec as P

WID = 32
HGT = 8
POS = HGT * WID
CONV = 16
EPSILON = 1e-05
NORM_EPS = 1e-06
BF16 = jnp.bfloat16
F32 = jnp.float32

CHIPS = 4
BLOCK = WID // 2
COLS_IN = 16
PART_1 = 10
COLS_1, COLS_2 = BLOCK + 4, BLOCK + 2
PART_2 = 6
PART_3 = 8
ROWS_1, ROWS_2 = COLS_1 * CONV, COLS_2 * CONV
K_1 = 27 * COLS_IN
K_PIECE = (PART_2 + 2) * CONV
K_2 = 9 * K_PIECE
M_1 = PART_1 * CONV
M_2 = PART_2 * CONV
K_3 = (PART_3 + 2) * CONV
FRAME = WID + 16


def whole(space=pltpu.VMEM):
    return pl.BlockSpec(memory_space=space)


def call(kernel, out_shape, inputs, scalars=(), scratch=(), out_specs=None):
    return pl.pallas_call(
        kernel,
        out_shape=out_shape,
        in_specs=[whole(pltpu.SMEM)] * len(scalars) + [whole()] * len(inputs),
        out_specs=jax.tree.map(lambda _: whole(), out_shape) if out_specs is None else out_specs,
        scratch_shapes=list(scratch),
        compiler_params=pltpu.CompilerParams(vmem_limit_bytes=48 * 1024 * 1024),
    )(*scalars, *inputs)


def spread_kernel(src_ref, tgt_ref, slot_ref, own_ref, out_ref, slots_ref):
    for pair in range(src_ref.shape[0]):
        slots_ref[2 * pair] = slot_ref[src_ref[pair]]
        slots_ref[2 * pair + 1] = slot_ref[tgt_ref[pair]]
    rows = []
    for image in range(2):
        cells = own_ref[image, 0].astype(F32)
        scale = lax.rsqrt(jnp.sum(cells * cells, axis=-1, keepdims=True) + NORM_EPS)
        rows.append(cells * scale)
    for part in range(4):
        for block in range(8):
            at = slice(part * 8, part * 8 + 8), slice(block * 128, block * 128 + 128)
            out_ref[part * 8 + block] = jnp.concatenate([rows[0][at], rows[1][at]], axis=0).astype(BF16)


def select_kernel(slots_ref, held_ref, out_ref, pieces):
    groups = held_ref.shape[0]
    for group in range(groups):
        both = held_ref[group].astype(F32)
        pieces[2 * group] = both[:8]
        pieces[2 * group + 1] = both[8:]
    for group in range(groups):
        for pair in range(2):
            at = 4 * group + 2 * pair
            out_ref[group, pair] = jnp.concatenate(
                [pieces[slots_ref[at]], pieces[slots_ref[at + 1]]], axis=0
            ).astype(BF16)


def pack_kernel(chip_ref, held_ref, out_0, out_1, out_2, out_3):
    chip = chip_ref[0]
    for step, out_ref in enumerate((out_0, out_1, out_2, out_3)):
        pair = lax.rem(chip + step, CHIPS) // (CHIPS // 2)
        for group in range(held_ref.shape[0]):
            out_ref[group] = held_ref[group, pair]


def shifted(values, offset):
    amount = (-offset) % POS
    return pltpu.roll(values, amount, values.ndim - 1) if amount else values


def consensus_kernel(
    chip_ref, core_ref, own_0, own_1, own_2, own_3, oth_0, oth_1, oth_2, oth_3, z1_ref, z2_ref, z3_ref,
    keep_ref, give_ref, frame, src, tgt, x1, x2, h2, w3s, kept,
):
    chip = chip_ref[0]
    core = core_ref[0]
    for row in range(HGT):
        frame[row * FRAME : row * FRAME + 8] = jnp.zeros((8, frame.shape[1]), F32)
        frame[row * FRAME + 8 + WID : (row + 1) * FRAME] = jnp.zeros((8, frame.shape[1]), F32)
    for parity, gots in ((core, (own_0, own_1, own_2, own_3)), (1 - core, (oth_0, oth_1, oth_2, oth_3))):
        for step, got in enumerate(gots):
            row = 2 * lax.rem(chip + CHIPS - step, CHIPS) + parity
            for part in range(4):
                to_src = pl.ds(pl.multiple_of(row * FRAME + 8 + part * 8, 8), 8)
                to_tgt = pl.ds(pl.multiple_of(row * WID + part * 8, 8), 8)
                for block in range(8):
                    both = got[part * 8 + block].astype(F32)
                    frame[to_src, block * 128 : block * 128 + 128] = both[:8]
                    tgt[to_tgt, block * 128 : block * 128 + 128] = both[8:]
    for row in range(HGT):
        line = frame[pl.ds(pl.multiple_of(row * FRAME + BLOCK * core, 8), 32), :]
        src[row * 16 : row * 16 + 16] = line[4:20].astype(BF16)
        src[128 + row * 16 : 128 + row * 16 + 16] = line[12:28].astype(BF16)
    corr = lax.dot_general(
        src[...], tgt[...].astype(BF16), (((1,), (1,)), ((), ())), preferred_element_type=F32
    )
    corr = corr.astype(BF16).astype(F32)

    column = lax.broadcasted_iota(jnp.int32, (1, POS), 1)
    line = column // WID
    column = column % WID

    def col_mask(d):
        return ((column + d - 1 >= 0) & (column + d - 1 < WID)).astype(F32)

    def line_mask(c):
        return ((line + c - 1 >= 0) & (line + c - 1 < HGT)).astype(F32)

    has_left = (core > 0).astype(F32)
    has_right = (core < 1).astype(F32)

    z1 = z1_ref[...].astype(F32)
    w1 = [
        jnp.concatenate([pltpu.roll(z1, j + 2 * w, 1) if j + w else z1 for j in range(PART_1)], axis=0).astype(BF16)[:, :K_1]
        for w in range(2)
    ]
    z2 = z2_ref[...].astype(F32)
    rolled = [pltpu.roll(z2, CONV * j, 1) if j else z2 for j in range(PART_2)]
    w2 = jnp.concatenate(
        [rolled[j][c * CONV : c * CONV + CONV] for c in range(3) for j in range(PART_2)], axis=0
    ).astype(BF16)
    z3 = z3_ref[...].astype(F32)
    for j in range(PART_3):
        w3s[:, j, :] = pltpu.roll(z3, CONV * j, 1) if j else z3
    w3 = w3s[...].reshape(27 * PART_3, 256).astype(BF16)[:, :K_3]

    for c in range(3):
        for d in range(3):
            moved = (shifted(corr, WID * (c - 1) + d - 1) * (line_mask(c) * col_mask(d))).astype(BF16)
            for w in range(2):
                at = w * 160
                x1[c * 3 + d, at : at + 16] = jnp.zeros((16, POS), BF16)
                x1[c * 3 + d, at + 16 : at + 144] = moved[w * 128 : w * 128 + 128]
                x1[c * 3 + d, at + 144 : at + 160] = jnp.zeros((16, POS), BF16)
    for d in range(3):
        x2[d, 0:ROWS_1] = jnp.zeros((ROWS_1, POS), BF16)
        x2[d, (HGT + 1) * ROWS_1 :] = jnp.zeros((ROWS_1, POS), BF16)
    left_mask, right_mask = col_mask(0), col_mask(2)
    for i in range(HGT):
        for w in range(2):
            at = w * 160 + 16 * i
            cells = jnp.concatenate([x1[k, at : at + 48] for k in range(9)], axis=0)
            hidden = jnp.maximum(jnp.dot(w1[w], cells, preferred_element_type=F32), 0.0)
            edge = 2 * CONV
            if w == 0:
                hidden = jnp.concatenate([hidden[:edge] * has_left, hidden[edge:]], axis=0)
            else:
                hidden = jnp.concatenate([hidden[: M_1 - edge], hidden[M_1 - edge :] * has_right], axis=0)
            at = (i + 1) * ROWS_1 + w * M_1
            x2[0, at : at + M_1] = (shifted(hidden, -1) * left_mask).astype(BF16)
            x2[1, at : at + M_1] = hidden.astype(BF16)
            x2[2, at : at + M_1] = (shifted(hidden, 1) * right_mask).astype(BF16)

    up_mask, down_mask = line_mask(0), line_mask(2)
    for i in range(HGT):
        for part in range(3):
            first = part * M_2
            cells = jnp.concatenate(
                [x2[d, (i + a) * ROWS_1 + first : (i + a) * ROWS_1 + first + K_PIECE] for d in range(3) for a in range(3)],
                axis=0,
            )
            parts = jnp.dot(w2, cells, preferred_element_type=F32)
            total = parts[M_2 : 2 * M_2]
            total = total + shifted(parts[:M_2], -WID) * up_mask
            total = total + shifted(parts[2 * M_2 :], WID) * down_mask
            total = jnp.maximum(total, 0.0)
            if part == 0:
                total = jnp.concatenate([total[:CONV] * has_left, total[CONV:]], axis=0)
            if part == 2:
                total = jnp.concatenate([total[: M_2 - CONV], total[M_2 - CONV :] * has_right], axis=0)
            h2[i, first : first + M_2] = total.astype(BF16)

    best = None
    sums = [[None] * HGT for _ in range(2)]
    for part in range(2):
        for i in range(HGT):
            parts = jnp.dot(w3, h2[i, part * 128 : part * 128 + K_3], preferred_element_type=F32)
            for a in range(3):
                o = i + 1 - a
                if 0 <= o < HGT:
                    piece = parts[a * 9 * PART_3 : (a + 1) * 9 * PART_3]
                    sums[part][o] = piece if sums[part][o] is None else sums[part][o] + piece
    for i in range(HGT):
        halves = []
        for part in range(2):
            total = None
            for c in range(3):
                for d in range(3):
                    k = (c * 3 + d) * PART_3
                    moved = shifted(sums[part][i][k : k + PART_3], WID * (c - 1) + d - 1) * (line_mask(c) * col_mask(d))
                    total = moved if total is None else total + moved
            halves.append(jnp.maximum(total, 0.0))
        total = jnp.concatenate(halves, axis=0)
        top = jnp.max(total, axis=0, keepdims=True)
        best = top if best is None else jnp.maximum(best, top)
        target_best = jnp.max(total, axis=1, keepdims=True)
        kept[i] = (total * (total / (target_best + EPSILON))).astype(BF16)
    pieces = []
    rest = best
    for _ in range(3):
        piece = rest.astype(BF16).astype(F32)
        pieces.append(piece)
        rest = rest - piece
    pieces = jnp.concatenate(pieces + [jnp.zeros((13, POS), F32)], axis=0).astype(BF16)
    far = CHIPS - 1 - chip
    for ref, parity in ((keep_ref, core), (give_ref, 1 - core)):
        ref[0] = kept[2 * chip + parity]
        ref[1] = kept[2 * far + parity]
        ref[2] = pieces


def finish_kernel(core_ref, keep_ref, got_ref, near_ref, far_ref, lines):
    core = core_ref[0]

    def largest(ref):
        top = ref[2].astype(F32)
        return top[0:1] + top[1:2] + top[2:3]

    best = jnp.maximum(largest(keep_ref), largest(got_ref)) + EPSILON
    for line in range(2):
        lines[line, core] = (keep_ref[line].astype(F32) / best).astype(BF16)
        lines[line, 1 - core] = (got_ref[line].astype(F32) / best).astype(BF16)
    near_ref[...] = lines[0]
    far_ref[...] = lines[1]


def place_kernel(chip_ref, near_ref, far_ref, out_ref):
    pair = chip_ref[0] // (CHIPS // 2)
    for half in range(2):
        out_ref[pair, 0, half * BLOCK : half * BLOCK + BLOCK] = near_ref[half]
        out_ref[1 - pair, 0, half * BLOCK : half * BLOCK + BLOCK] = far_ref[half]


def row_moves(chips, cores):
    return [(2 * y + c, 2 * ((y + chips) % CHIPS) + (c ^ cores)) for y in range(CHIPS) for c in range(2)]


def local(features, src_ids, tgt_ids, image_slot, w_first, w_mid, w_last):
    groups = lax.axis_size("pair")
    channels = features.shape[3]
    place = lax.axis_index("row").astype(jnp.int32)
    chip = (place // 2).reshape(1)
    core = (place % 2).reshape(1)

    taps = w_first.reshape(3, 3, 3, 3, CONV).transpose(4, 2, 3, 0, 1)
    z1 = jnp.pad(taps, ((0, 0),) * 4 + ((1, COLS_IN - 4),)).reshape(CONV, K_1)
    z1 = jnp.pad(z1, ((0, 0), (0, 512 - K_1)))
    taps = w_mid.reshape(3, 3, 3, 3, CONV, CONV).transpose(2, 4, 3, 0, 1, 5)
    z2 = jnp.pad(taps, ((0, 0),) * 4 + ((0, PART_2 - 1), (0, 0))).reshape(3 * CONV, K_2)
    z3 = w_last.reshape(3, 3, 3, 3, CONV).transpose(0, 2, 3, 1, 4).reshape(27, 3 * CONV)
    z3 = jnp.pad(z3, ((0, 0), (0, 256 - 3 * CONV)))

    tiles, slots = call(
        spread_kernel,
        (jax.ShapeDtypeStruct((groups, 16, 128), BF16), jax.ShapeDtypeStruct((2 * src_ids.shape[0],), jnp.int32)),
        (features,),
        (src_ids, tgt_ids, image_slot),
        out_specs=(whole(), whole(pltpu.SMEM)),
    )
    held = lax.all_to_all(tiles, "pair", 0, 0, tiled=True)
    wanted = call(
        select_kernel,
        jax.ShapeDtypeStruct((groups, 2, 16, 128), BF16),
        (held,),
        (slots,),
        (pltpu.VMEM((2 * groups, 8, 128), F32),),
    )
    routed = lax.all_to_all(wanted, "pair", 0, 0, tiled=True)
    sends = call(pack_kernel, (jax.ShapeDtypeStruct((groups, 16, 128), BF16),) * 4, (routed,), (chip,))
    own = [sends[0]] + [lax.ppermute(sends[k], "row", row_moves(k, 0)) for k in range(1, CHIPS)]
    other = [lax.ppermute(block, "row", row_moves(0, 1)) for block in own]
    message = jax.ShapeDtypeStruct((3, 16, POS), BF16)
    keep, give = call(
        consensus_kernel,
        (message, message),
        (*own, *other, z1, z2, z3),
        (chip, core),
        (
            pltpu.VMEM((HGT * FRAME, channels), F32),
            pltpu.VMEM((2 * HGT * COLS_IN, channels), BF16),
            pltpu.VMEM((POS, channels), F32),
            pltpu.VMEM((9, 320, POS), BF16),
            pltpu.VMEM((3, (HGT + 2) * ROWS_1, POS), BF16),
            pltpu.VMEM((HGT, ROWS_2, POS), BF16),
            pltpu.VMEM((27, PART_3, 256), F32),
            pltpu.VMEM((HGT, 16, POS), BF16),
        ),
    )
    got = lax.ppermute(give, "row", row_moves(0, 1))
    lines = jax.ShapeDtypeStruct((2, BLOCK, POS), BF16)
    near, far = call(finish_kernel, (lines, lines), (keep, got), (core,), (pltpu.VMEM((2, 2, BLOCK, POS), BF16),))
    far = lax.ppermute(far, "row", [(2 * y + c, 2 * (CHIPS - 1 - y) + c) for y in range(CHIPS) for c in range(2)])
    return call(place_kernel, jax.ShapeDtypeStruct((2, 1, WID, POS), BF16), (near, far), (chip,))


def solution(mesh):
    placed = (P("pair", "row", None, None), P(), P(), P(), P(), P(), P())
    return jax.shard_map(
        local, mesh=mesh, in_specs=placed, out_specs=P("pair", "row", None, None), check_vma=False
    )
```

time: 70.7 us -> 70.4 us (level)
  blocking collectives: 33.9 us -> 21 us
  starting transfers between devices: 12.9 us -> 19.3 us
  Pallas kernels: 6.01 us -> 10.4 us
  waiting for transfers between devices: 12.3 us -> 13.3 us
  local copies, waits for them, and re-layouts: 5.13 us -> 5.93 us
    all_to_all x2 -> x1, blocking collectives: 33.9 us -> 21 us  [local(): held = lax.all_to_all(tiles, 'pair', 0, 0, tiled=True)]
    ppermute x1 -> x6, starting transfers between devices: 3.24 us -> 10.4 us  [the longest x4 7.94 us: local(): other = [lax.ppermute(block, 'row', row_moves(0, 1)) for block in own]]
    pallas_call x5 -> x6, Pallas kernels: 6.01 us -> 10.4 us  [call(): pl.pallas_call(kernel, out_shape=out_shape, in_specs=[whole(pltpu.SMEM)]...]
    ppermute x1 -> x6, waiting for transfers between devices: 1.2 us -> 2.71 us  [the longest x1 1.52 us: local(): lax.ppermute(far, 'row', [(2 * y + c, 2 * (CHIPS - 1 - y) + c) for y in r...]
    all_to_all x1, starting transfers between devices: 4.59 us -> 3.87 us  [local(): routed = lax.all_to_all(wanted, 'pair', 0, 0, tiled=True)]
    unnamed x19, local copies, waits for them, and re-layouts: 3.95 us -> 4.66 us
  transfers between devices with their start and end apart: 5 -> 10, of which waited for: 3 -> 3; matrix products, arithmetic and copies ran while one was open for 3% -> 3% of each run, Pallas kernels for 0% -> 0%
where the time goes in v2:
time: 70.4 us; the launch traced here: 70.1 us
  blocking collectives  21 us (30%)
  starting transfers between devices  19.3 us (27%)
  waiting for transfers between devices  13.3 us (19%)
  Pallas kernels  10.4 us (15%)
  local copies, waits for them, and re-layouts  5.93 us (8%)
    all_to_all x1, blocking collectives, local(): held = lax.all_to_all(tiles, 'pair', 0, 0, tiled=True)  21 us
    all_to_all x1, waiting for transfers between devices, local(): routed = lax.all_to_all(wanted, 'pair', 0, 0, tiled=True)  10.6 us
    pallas_call x6, Pallas kernels, call(): pl.pallas_call(kernel, out_shape=out_shape, in_specs=[whole(pltpu.SMEM)]...  10.4 us
    ppermute x4, starting transfers between devices, local(): other = [lax.ppermute(block, 'row', row_moves(0, 1)) for block in own]  7.94 us
    ppermute x3, starting transfers between devices, local(): lax.ppermute(sends[k], 'row', row_moves(k, 0))  5.06 us
    unnamed x19, local copies, waits for them, and re-layouts  4.66 us
    all_to_all x1, starting transfers between devices, local(): routed = lax.all_to_all(wanted, 'pair', 0, 0, tiled=True)  3.87 us
    ppermute x1, starting transfers between devices, local(): lax.ppermute(far, 'row', [(2 * y + c, 2 * (CHIPS - 1 - y) + c) for y in r...  2.36 us
  transfers between devices with their start and end apart: 10, of which 3 were waited for; matrix products, arithmetic and copies ran while one was open for 3% of the time, Pallas kernels for 0%

profile of v2, /device:TPU:1, one launch (start us, length us, event | category | flops | bytes accessed | tf_op | source)
XLA Modules:
  0.0 70.1 jit_solution(7987992195747581351)
XLA Ops:
  0.0 0.0 copy-start
  0.0 0.9 %copy-done = bf16[2,1,32,1024]{3,2,1,0:T(8,128)(2,1)S(1)} copy-done((bf16[2,1,32,1024]{3,2,1,0:T(8,128)(2,1)S(1)}, bf16[2,1,32,1024]{3,2,1,0:T(8,128)(2,1)}, u32[]{:S(2)}) %copy-start) | copy-done | bytes 131096
  0.9 0.0 copy-start.1
  0.9 0.7 copy-done.1
  1.6 0.0 copy-start.2
  1.6 0.7 copy-done.2
  2.2 0.0 copy-start.3
  2.2 0.7 copy-done.3
  2.9 1.3 %shard_map.73 = (bf16[32,16,128]{2,1,0:T(8,128)(2,1)S(1)}, s32[128]{0:T(128)S(1)}) custom-call(s32[64]{0:T(128)S(1)} %copy-done.1, s32[64]{0:T(128)S(1)} %copy-done.2, s32[64]{0:T(128)S(1)} %copy-done.3, bf16[2,1,32,1024]{3,2,1,0:T(8,128)(2,1)S(1)} %copy-done), custom_call_target="tpu_custom_call" | custom-call | tf_op jit(solution)/shard_map/pallas_call | solution.py:39
  4.2 21.0 %all_to_all.10.held_ref = bf16[32,16,128]{2,1,0:T(8,128)(2,1)S(1)} all-to-all(bf16[32,16,128]{2,1,0:T(8,128)(2,1)S(1)} %get-tuple-element.16), channel_id=1, replica_groups=mesh['pair'=32,'row'=8] {'pair'}, dimensions={0} | all-to-all | bytes 262144 | tf_op jit(solution)/shard_map/all_to_all | solution.py:280
  25.2 1.3 %shard_map.74 = bf16[32,2,16,128]{3,2,1,0:T(8,128)(2,1)} custom-call(s32[128]{0:T(128)S(1)} %get-tuple-element.15.slots_ref, bf16[32,16,128]{2,1,0:T(8,128)(2,1)S(1)} %all_to_all.10.held_ref), custom_call_target="tpu_custom_call" | custom-call | tf_op jit(solution)/shard_map/pallas_call | solution.py:39
  26.5 3.9 %all-to-all-start.1 = ((bf16[32,2,16,128]{3,2,1,0:T(8,128)(2,1)}), bf16[32,2,16,128]{3,2,1,0:T(8,128)(2,1)S(1)}, u32[]{:S(2)}, u32[]{:S(2)}) async-start(bf16[32,2,16,128]{3,2,1,0:T(8,128)(2,1)} %shard_map.74), calls=%async_computation.1 | async-start | bytes 524288 | tf_op jit(solution)/shard_map/all_to_all | solution.py:288
  30.4 10.6 %all-to-all-done.1.held_ref = bf16[32,2,16,128]{3,2,1,0:T(8,128)(2,1)S(1)} async-done(((bf16[32,2,16,128]{3,2,1,0:T(8,128)(2,1)}), bf16[32,2,16,128]{3,2,1,0:T(8,128)(2,1)S(1)}, u32[]{:S(2)}, u32[]{:S(2)}) %all-to-all-start.1) | async-done | bytes 262176 | tf_op jit(solution)/shard_map/all_to_all | solution.py:288
  41.0 1.4 %collective-permute-start = (bf16[32,16,128]{2,1,0:T(8,128)(2,1)S(1)}, bf16[32,16,128]{2,1,0:T(8,128)(2,1)S(1)}, u32[]{:S(2)}, u32[]{:S(2)}) collective-permute-start(bf16[32,16,128]{2,1,0:T(8,128)(2,1)S(1)} %get-tuple-element.18), channel_id=1, source_target_pairs={{0,2},{1,3},{2,4},{3,5},{4,6},{5,7},{6,0},{7,1},{8,10},{9,11},{10,... | collective-permute-start | bytes 393224 | tf_op jit(solution)/shard_map/ppermute | solution.py:290
  42.4 2.6 %collective-permute-start.1 = (bf16[32,16,128]{2,1,0:T(8,128)(2,1)S(1)}, bf16[32,16,128]{2,1,0:T(8,128)(2,1)S(1)}, u32[]{:S(2)}, u32[]{:S(2)}) collective-permute-start(bf16[32,16,128]{2,1,0:T(8,128)(2,1)S(1)} %get-tuple-element.19), channel_id=1, source_target_pairs={{0,4},{1,5},{2,6},{3,7},{4,0},{5,1},{6,2},{7,3},{8,12},{9,13},{10,... | collective-permute-start | bytes 393224 | tf_op jit(solution)/shard_map/ppermute | solution.py:290
  45.0 1.1 %collective-permute-start.2 = (bf16[32,16,128]{2,1,0:T(8,128)(2,1)S(1)}, bf16[32,16,128]{2,1,0:T(8,128)(2,1)S(1)}, u32[]{:S(2)}, u32[]{:S(2)}) collective-permute-start(bf16[32,16,128]{2,1,0:T(8,128)(2,1)S(1)} %get-tuple-element.20), channel_id=1, source_target_pairs={{0,6},{1,7},{2,0},{3,1},{4,2},{5,3},{6,4},{7,5},{8,14},{9,15},{10,... | collective-permute-start | bytes 393224 | tf_op jit(solution)/shard_map/ppermute | solution.py:290
  46.1 4.3 %collective-permute-start.3 = (bf16[32,16,128]{2,1,0:T(8,128)(2,1)S(1)}, bf16[32,16,128]{2,1,0:T(8,128)(2,1)S(1)}, u32[]{:S(2)}, u32[]{:S(2)}) collective-permute-start(bf16[32,16,128]{2,1,0:T(8,128)(2,1)S(1)} %get-tuple-element.17.own_0), channel_id=1, source_target_pairs={{0,1},{1,0},{2,3},{3,2},{4,5},{5,4},{6,7},{7,6},{8,9},{9,8},{10,11... | collective-permute-start | bytes 393224 | tf_op jit(solution)/shard_map/ppermute | solution.py:291
  50.4 0.0 collective-permute-done.own_1
  50.4 0.4 collective-permute-start.4
  50.9 0.0 collective-permute-done.1.own_2
  50.9 2.5 %collective-permute-start.5 = (bf16[32,16,128]{2,1,0:T(8,128)(2,1)S(1)}, bf16[32,16,128]{2,1,0:T(8,128)(2,1)S(1)}, u32[]{:S(2)}, u32[]{:S(2)}) collective-permute-start(bf16[32,16,128]{2,1,0:T(8,128)(2,1)S(1)} %collective-permute-done.1.own_2), channel_id=1, source_target_pairs={{0,1},{1,0},{2,3},{3,2},{4,5},{5,4},{6,7},{7,6},{8,9},{9,8},{10,11... | collective-permute-start | bytes 393224 | tf_op jit(solution)/shard_map/ppermute | solution.py:291
  53.4 0.0 collective-permute-done.2.own_3
  53.4 0.6 collective-permute-start.6
  54.0 0.0 copy-done.4
  54.0 0.3 copy.13
  54.4 0.2 copy.18
  54.5 0.2 pad.18.clone
  54.8 0.0 copy-start.5
  54.8 0.6 reshape.29.z2_ref
  55.4 0.1 copy-done.5
  55.5 0.1 copy.11
  55.6 0.3 copy.17
  55.9 0.2 pad.16.clone
  56.1 0.1 reshape.27
  56.2 0.0 copy-start.6
  56.2 0.7 copy-done.6
  56.9 0.1 copy.15
  57.1 0.1 reshape.31
  57.2 0.0 collective-permute-done.3.oth_0
  57.2 0.0 collective-permute-done.4.oth_1
  57.2 0.0 collective-permute-done.5.oth_2
  57.2 0.0 collective-permute-done.6.oth_3
  57.2 7.1 %shard_map.76 = (bf16[3,16,256]{2,1,0:T(8,128)(2,1)S(1)}, bf16[3,16,256]{2,1,0:T(8,128)(2,1)S(1)}) custom-call(s32[1]{0:T(128)} %bitcast.chip_ref, s32[1]{0:T(128)} %bitcast.1.core_ref, bf16[32,16,128]{2,1,0:T(8,128)(2,1)S(1)} %get-tuple-element.17.own_0, bf16[32,16,128]{2,1,0:T(8,128)(2,1)S(1)} %collective-permute-done.own_1, ...), custom_call_target="tpu_custom_call" | custom-call | tf_op jit(solution)/shard_map/pallas_call | solution.py:39
  64.3 0.1 collective-permute-start.7
  64.4 1.2 %collective-permute-done.7.got_ref = bf16[3,16,256]{2,1,0:T(8,128)(2,1)S(1)} collective-permute-done((bf16[3,16,256]{2,1,0:T(8,128)(2,1)S(1)}, bf16[3,16,256]{2,1,0:T(8,128)(2,1)S(1)}, u32[]{:S(2)}, u32[]{:S(2)}) %collective-permute-start.7) | collective-permute-done | bytes 24608 | tf_op jit(solution)/shard_map/ppermute | solution.py:309
  65.6 2.4 %collective-permute-start.8 = (bf16[2,16,256]{2,1,0:T(8,128)(2,1)S(1)}, bf16[2,16,256]{2,1,0:T(8,128)(2,1)S(1)}, u32[]{:S(2)}, u32[]{:S(2)}) collective-permute-start(bf16[2,16,256]{2,1,0:T(8,128)(2,1)S(1)} %get-tuple-element.24), channel_id=1, source_target_pairs={{0,6},{1,7},{2,4},{3,5},{4,2},{5,3},{6,0},{7,1},{8,14},{9,15},{10,... | collective-permute-start | bytes 49160 | tf_op jit(solution)/shard_map/ppermute | solution.py:312
  68.0 1.5 %collective-permute-done.8.far_ref = bf16[2,16,256]{2,1,0:T(8,128)(2,1)S(1)} collective-permute-done((bf16[2,16,256]{2,1,0:T(8,128)(2,1)S(1)}, bf16[2,16,256]{2,1,0:T(8,128)(2,1)S(1)}, u32[]{:S(2)}, u32[]{:S(2)}) %collective-permute-start.8) | collective-permute-done | bytes 16416 | tf_op jit(solution)/shard_map/ppermute | solution.py:312
  69.5 0.6 shard_map.78
  (8 shorter events, 0.1 us)
Async XLA Ops:
  0.0 0.9 %copy-start = (bf16[2,1,32,1024]{3,2,1,0:T(8,128)(2,1)S(1)}, bf16[2,1,32,1024]{3,2,1,0:T(8,128)(2,1)}, u32[]{:S(2)}) copy-start(bf16[2,1,32,1024]{3,2,1,0:T(8,128)(2,1)} %own_ref.1) | copy-start | bytes 393220
  0.9 0.7 copy-start.1
  1.6 0.7 copy-start.2
  2.2 0.7 copy-start.3
  26.5 14.5 %all-to-all-start.1 = ((bf16[32,2,16,128]{3,2,1,0:T(8,128)(2,1)}), bf16[32,2,16,128]{3,2,1,0:T(8,128)(2,1)S(1)}, u32[]{:S(2)}, u32[]{:S(2)}) async-start(bf16[32,2,16,128]{3,2,1,0:T(8,128)(2,1)} %shard_map.74), calls=%async_computation.1 | async-start | bytes 524288 | tf_op jit(solution)/shard_map/all_to_all | solution.py:288
  41.0 13.1 %copy-start.4 = (bf16[81,16,16]{0,2,1:T(8,128)(2,1)S(1)}, bf16[81,16,16]{0,2,1:T(8,128)(2,1)}, u32[]{:S(2)}) copy-start(bf16[81,16,16]{0,2,1:T(8,128)(2,1)} %param.12) | copy-start | bytes 124420
  41.0 9.4 %collective-permute-start = (bf16[32,16,128]{2,1,0:T(8,128)(2,1)S(1)}, bf16[32,16,128]{2,1,0:T(8,128)(2,1)S(1)}, u32[]{:S(2)}, u32[]{:S(2)}) collective-permute-start(bf16[32,16,128]{2,1,0:T(8,128)(2,1)S(1)} %get-tuple-element.18), channel_id=1, source_target_pairs={{0,2},{1,3},{2,4},{3,5},{4,6},{5,7},{6,0},{7,1},{8,10},{9,11},{10,... | collective-permute-start | bytes 393224 | tf_op jit(solution)/shard_map/ppermute | solution.py:290
  42.4 8.5 %collective-permute-start.1 = (bf16[32,16,128]{2,1,0:T(8,128)(2,1)S(1)}, bf16[32,16,128]{2,1,0:T(8,128)(2,1)S(1)}, u32[]{:S(2)}, u32[]{:S(2)}) collective-permute-start(bf16[32,16,128]{2,1,0:T(8,128)(2,1)S(1)} %get-tuple-element.19), channel_id=1, source_target_pairs={{0,4},{1,5},{2,6},{3,7},{4,0},{5,1},{6,2},{7,3},{8,12},{9,13},{10,... | collective-permute-start | bytes 393224 | tf_op jit(solution)/shard_map/ppermute | solution.py:290
  45.0 8.4 %collective-permute-start.2 = (bf16[32,16,128]{2,1,0:T(8,128)(2,1)S(1)}, bf16[32,16,128]{2,1,0:T(8,128)(2,1)S(1)}, u32[]{:S(2)}, u32[]{:S(2)}) collective-permute-start(bf16[32,16,128]{2,1,0:T(8,128)(2,1)S(1)} %get-tuple-element.20), channel_id=1, source_target_pairs={{0,6},{1,7},{2,0},{3,1},{4,2},{5,3},{6,4},{7,5},{8,14},{9,15},{10,... | collective-permute-start | bytes 393224 | tf_op jit(solution)/shard_map/ppermute | solution.py:290
  46.1 11.1 %collective-permute-start.3 = (bf16[32,16,128]{2,1,0:T(8,128)(2,1)S(1)}, bf16[32,16,128]{2,1,0:T(8,128)(2,1)S(1)}, u32[]{:S(2)}, u32[]{:S(2)}) collective-permute-start(bf16[32,16,128]{2,1,0:T(8,128)(2,1)S(1)} %get-tuple-element.17.own_0), channel_id=1, source_target_pairs={{0,1},{1,0},{2,3},{3,2},{4,5},{5,4},{6,7},{7,6},{8,9},{9,8},{10,11... | collective-permute-start | bytes 393224 | tf_op jit(solution)/shard_map/ppermute | solution.py:291
  50.4 6.8 %collective-permute-start.4 = (bf16[32,16,128]{2,1,0:T(8,128)(2,1)S(1)}, bf16[32,16,128]{2,1,0:T(8,128)(2,1)S(1)}, u32[]{:S(2)}, u32[]{:S(2)}) collective-permute-start(bf16[32,16,128]{2,1,0:T(8,128)(2,1)S(1)} %collective-permute-done.own_1), channel_id=1, source_target_pairs={{0,1},{1,0},{2,3},{3,2},{4,5},{5,4},{6,7},{7,6},{8,9},{9,8},{10,11... | collective-permute-start | bytes 393224 | tf_op jit(solution)/shard_map/ppermute | solution.py:291
  50.9 6.3 %collective-permute-start.5 = (bf16[32,16,128]{2,1,0:T(8,128)(2,1)S(1)}, bf16[32,16,128]{2,1,0:T(8,128)(2,1)S(1)}, u32[]{:S(2)}, u32[]{:S(2)}) collective-permute-start(bf16[32,16,128]{2,1,0:T(8,128)(2,1)S(1)} %collective-permute-done.1.own_2), channel_id=1, source_target_pairs={{0,1},{1,0},{2,3},{3,2},{4,5},{5,4},{6,7},{7,6},{8,9},{9,8},{10,11... | collective-permute-start | bytes 393224 | tf_op jit(solution)/shard_map/ppermute | solution.py:291
  53.4 3.8 %collective-permute-start.6 = (bf16[32,16,128]{2,1,0:T(8,128)(2,1)S(1)}, bf16[32,16,128]{2,1,0:T(8,128)(2,1)S(1)}, u32[]{:S(2)}, u32[]{:S(2)}) collective-permute-start(bf16[32,16,128]{2,1,0:T(8,128)(2,1)S(1)} %collective-permute-done.2.own_3), channel_id=1, source_target_pairs={{0,1},{1,0},{2,3},{3,2},{4,5},{5,4},{6,7},{7,6},{8,9},{9,8},{10,11... | collective-permute-start | bytes 393224 | tf_op jit(solution)/shard_map/ppermute | solution.py:291
  54.8 0.7 copy-start.5
  56.2 0.7 copy-start.6
  64.3 1.3 %collective-permute-start.7 = (bf16[3,16,256]{2,1,0:T(8,128)(2,1)S(1)}, bf16[3,16,256]{2,1,0:T(8,128)(2,1)S(1)}, u32[]{:S(2)}, u32[]{:S(2)}) collective-permute-start(bf16[3,16,256]{2,1,0:T(8,128)(2,1)S(1)} %get-tuple-element.22), channel_id=1, source_target_pairs={{0,1},{1,0},{2,3},{3,2},{4,5},{5,4},{6,7},{7,6},{8,9},{9,8},{10,11... | collective-permute-start | bytes 73736 | tf_op jit(solution)/shard_map/ppermute | solution.py:309
  65.6 3.9 %collective-permute-start.8 = (bf16[2,16,256]{2,1,0:T(8,128)(2,1)S(1)}, bf16[2,16,256]{2,1,0:T(8,128)(2,1)S(1)}, u32[]{:S(2)}, u32[]{:S(2)}) collective-permute-start(bf16[2,16,256]{2,1,0:T(8,128)(2,1)S(1)} %get-tuple-element.24), channel_id=1, source_target_pairs={{0,6},{1,7},{2,4},{3,5},{4,2},{5,3},{6,0},{7,1},{8,14},{9,15},{10,... | collective-permute-start | bytes 49160 | tf_op jit(solution)/shard_map/ppermute | solution.py:312

commit v3 on v2

--- a/solution.py
+++ b/solution.py
@@ -46,19 +46,38 @@
     )(*scalars, *inputs)
 
 
-def spread_kernel(src_ref, tgt_ref, slot_ref, own_ref, out_ref, slots_ref):
+def spread_kernel(own_ref, out_ref, rows_ref, sems):
+    copies = [
+        [
+            pltpu.make_async_copy(
+                own_ref.at[image, 0, half * 16 : half * 16 + 16], rows_ref.at[image, half], sems.at[image, half]
+            )
+            for half in range(2)
+        ]
+        for image in range(2)
+    ]
+    for half in range(2):
+        for image in range(2):
+            copies[image][half].start()
+    for half in range(2):
+        rows = []
+        for image in range(2):
+            copies[image][half].wait()
+            cells = rows_ref[image, half].astype(F32)
+            scale = lax.rsqrt(jnp.sum(cells * cells, axis=-1, keepdims=True) + NORM_EPS)
+            rows.append(cells * scale)
+        for part in range(2):
+            for block in range(8):
+                at = slice(part * 8, part * 8 + 8), slice(block * 128, block * 128 + 128)
+                out_ref[(half * 2 + part) * 8 + block] = jnp.concatenate(
+                    [rows[0][at], rows[1][at]], axis=0
+                ).astype(BF16)
+
+
+def slots_kernel(src_ref, tgt_ref, slot_ref, slots_ref):
     for pair in range(src_ref.shape[0]):
         slots_ref[2 * pair] = slot_ref[src_ref[pair]]
         slots_ref[2 * pair + 1] = slot_ref[tgt_ref[pair]]
-    rows = []
-    for image in range(2):
-        cells = own_ref[image, 0].astype(F32)
-        scale = lax.rsqrt(jnp.sum(cells * cells, axis=-1, keepdims=True) + NORM_EPS)
-        rows.append(cells * scale)
-    for part in range(4):
-        for block in range(8):
-            at = slice(part * 8, part * 8 + 8), slice(block * 128, block * 128 + 128)
-            out_ref[part * 8 + block] = jnp.concatenate([rows[0][at], rows[1][at]], axis=0).astype(BF16)
 
 
 def select_kernel(slots_ref, held_ref, out_ref, pieces):
@@ -270,12 +289,19 @@
     z3 = w_last.reshape(3, 3, 3, 3, CONV).transpose(0, 2, 3, 1, 4).reshape(27, 3 * CONV)
     z3 = jnp.pad(z3, ((0, 0), (0, 256 - 3 * CONV)))
 
-    tiles, slots = call(
+    tiles = pl.pallas_call(
         spread_kernel,
-        (jax.ShapeDtypeStruct((groups, 16, 128), BF16), jax.ShapeDtypeStruct((2 * src_ids.shape[0],), jnp.int32)),
-        (features,),
+        out_shape=jax.ShapeDtypeStruct((groups, 16, 128), BF16),
+        in_specs=[whole(pl.ANY)],
+        out_specs=whole(),
+        scratch_shapes=[pltpu.VMEM((2, 2, 16, channels), BF16), pltpu.SemaphoreType.DMA((2, 2))],
+    )(features)
+    slots = call(
+        slots_kernel,
+        jax.ShapeDtypeStruct((2 * src_ids.shape[0],), jnp.int32),
+        (),
         (src_ids, tgt_ids, image_slot),
-        out_specs=(whole(), whole(pltpu.SMEM)),
+        out_specs=whole(pltpu.SMEM),
     )
     held = lax.all_to_all(tiles, "pair", 0, 0, tiled=True)
     wanted = call(
@@ -286,6 +312,7 @@
         (pltpu.VMEM((2 * groups, 8, 128), F32),),
     )
     routed = lax.all_to_all(wanted, "pair", 0, 0, tiled=True)
+    routed, z1, z2, z3 = lax.optimization_barrier((routed, z1, z2, z3))
     sends = call(pack_kernel, (jax.ShapeDtypeStruct((groups, 16, 128), BF16),) * 4, (routed,), (chip,))
     own = [sends[0]] + [lax.ppermute(sends[k], "row", row_moves(k, 0)) for k in range(1, CHIPS)]
     other = [lax.ppermute(block, "row", row_moves(0, 1)) for block in own]

time: 70.4 us -> 66.5 us (0.945)
  blocking collectives: 21 us -> 0 us
  starting transfers between devices: 19.3 us -> 31.8 us
  waiting for transfers between devices: 13.3 us -> 18.8 us
  local copies, waits for them, and re-layouts: 5.93 us -> 3.08 us
  Pallas kernels: 10.4 us -> 12.2 us
    all_to_all x1 -> x0, blocking collectives: 21 us -> none  [local(): held = lax.all_to_all(tiles, 'pair', 0, 0, tiled=True)]
    all_to_all x0 -> x1, starting transfers between devices: none -> 12 us  [local(): held = lax.all_to_all(tiles, 'pair', 0, 0, tiled=True)]
    all_to_all x0 -> x1, waiting for transfers between devices: none -> 8.02 us  [local(): held = lax.all_to_all(tiles, 'pair', 0, 0, tiled=True)]
    all_to_all x1, waiting for transfers between devices: 10.6 us -> 7.41 us  [local(): routed = lax.all_to_all(wanted, 'pair', 0, 0, tiled=True)]
    unnamed x19 -> x17, local copies, waits for them, and re-layouts: 4.66 us -> 1.81 us
    pallas_call x0 -> x1, Pallas kernels: none -> 1.82 us  [local(): pl.pallas_call(spread_kernel, out_shape=jax.ShapeDtypeStruct((groups, 16,...]
    ppermute x4, waiting for transfers between devices: 0.01 us -> 0.98 us  [local(): other = [lax.ppermute(block, 'row', row_moves(0, 1)) for block in own]]
  transfers between devices with their start and end apart: 10 -> 11, of which waited for: 3 -> 6; matrix products, arithmetic and copies ran while one was open for 3% -> 3% of each run, Pallas kernels for 0% -> 2%
where the time goes in v3:
time: 66.5 us; the launch traced here: 66.1 us
  starting transfers between devices  31.8 us (48%)
  waiting for transfers between devices  18.8 us (28%)
  Pallas kernels  12.2 us (18%)
  local copies, waits for them, and re-layouts  3.08 us (5%)
    all_to_all x1, starting transfers between devices, local(): held = lax.all_to_all(tiles, 'pair', 0, 0, tiled=True)  12 us
    pallas_call x6, Pallas kernels, call(): pl.pallas_call(kernel, out_shape=out_shape, in_specs=[whole(pltpu.SMEM)]...  10.4 us
    all_to_all x1, waiting for transfers between devices, local(): held = lax.all_to_all(tiles, 'pair', 0, 0, tiled=True)  8.02 us
    ppermute x4, starting transfers between devices, local(): other = [lax.ppermute(block, 'row', row_moves(0, 1)) for block in own]  7.94 us
    all_to_all x1, waiting for transfers between devices, local(): routed = lax.all_to_all(wanted, 'pair', 0, 0, tiled=True)  7.41 us
    ppermute x3, starting transfers between devices, local(): lax.ppermute(sends[k], 'row', row_moves(k, 0))  5.06 us
    all_to_all x1, starting transfers between devices, local(): routed = lax.all_to_all(wanted, 'pair', 0, 0, tiled=True)  4 us
    ppermute x1, starting transfers between devices, local(): lax.ppermute(far, 'row', [(2 * y + c, 2 * (CHIPS - 1 - y) + c) for y in r...  2.36 us
  transfers between devices with their start and end apart: 11, of which 6 were waited for; matrix products, arithmetic and copies ran while one was open for 3% of the time, Pallas kernels for 2%

profile of v3, /device:TPU:1, one launch (start us, length us, event | category | flops | bytes accessed | tf_op | source)
XLA Modules:
  0.0 66.1 jit_solution(1404089352732424092)
XLA Ops:
  0.0 1.8 %shard_map.74 = bf16[32,16,128]{2,1,0:T(8,128)(2,1)} custom-call(bf16[2,1,32,1024]{3,2,1,0:T(8,128)(2,1)} %own_ref.1), custom_call_target="tpu_custom_call" | custom-call | tf_op jit(solution)/shard_map/pallas_call | solution.py:292
  1.8 0.0 copy-start
  1.8 0.0 copy-start.1
  1.9 0.0 copy-start.2
  1.9 12.0 %all-to-all-start = ((bf16[32,16,128]{2,1,0:T(8,128)(2,1)}), bf16[32,16,128]{2,1,0:T(8,128)(2,1)S(1)}, u32[]{:S(2)}, u32[]{:S(2)}) async-start(bf16[32,16,128]{2,1,0:T(8,128)(2,1)} %shard_map.74), calls=%async_computation | async-start | bytes 262144 | tf_op jit(solution)/shard_map/all_to_all | solution.py:306
  13.9 0.0 copy-done
  13.9 0.0 copy-done.1
  13.9 0.0 copy-done.2
  13.9 1.3 %shard_map.73.slots_ref = s32[128]{0:T(128)S(1)} custom-call(s32[64]{0:T(128)S(1)} %copy-done, s32[64]{0:T(128)S(1)} %copy-done.1, s32[64]{0:T(128)S(1)} %copy-done.2), custom_call_target="tpu_custom_call" | custom-call | tf_op jit(solution)/shard_map/pallas_call | solution.py:39
  15.2 8.0 %all-to-all-done.held_ref = bf16[32,16,128]{2,1,0:T(8,128)(2,1)S(1)} async-done(((bf16[32,16,128]{2,1,0:T(8,128)(2,1)}), bf16[32,16,128]{2,1,0:T(8,128)(2,1)S(1)}, u32[]{:S(2)}, u32[]{:S(2)}) %all-to-all-start) | async-done | bytes 131104 | tf_op jit(solution)/shard_map/all_to_all | solution.py:306
  23.2 1.3 %shard_map.75 = bf16[32,2,16,128]{3,2,1,0:T(8,128)(2,1)} custom-call(s32[128]{0:T(128)S(1)} %shard_map.73.slots_ref, bf16[32,16,128]{2,1,0:T(8,128)(2,1)S(1)} %all-to-all-done.held_ref), custom_call_target="tpu_custom_call" | custom-call | tf_op jit(solution)/shard_map/pallas_call | solution.py:39
  24.6 4.0 %all-to-all-start.1 = ((bf16[32,2,16,128]{3,2,1,0:T(8,128)(2,1)}), bf16[32,2,16,128]{3,2,1,0:T(8,128)(2,1)S(1)}, u32[]{:S(2)}, u32[]{:S(2)}) async-start(bf16[32,2,16,128]{3,2,1,0:T(8,128)(2,1)} %shard_map.75), calls=%async_computation.1 | async-start | bytes 524288 | tf_op jit(solution)/shard_map/all_to_all | solution.py:314
  28.6 0.0 copy-done.3
  28.6 0.3 copy.13
  28.9 0.2 copy.18
  29.1 0.2 pad.18.clone
  29.4 0.0 copy-start.4
  29.4 0.6 reshape.29.z2_ref
  29.9 0.1 copy-done.4
  30.0 0.1 copy.11
  30.2 0.3 copy.17
  30.5 0.2 pad.16.clone
  30.6 0.1 reshape.27
  30.8 0.0 copy-start.5
  30.8 0.7 %copy-done.5 = bf16[81,1,16]{0,2,1:T(8,128)(2,1)S(1)} copy-done((bf16[81,1,16]{0,2,1:T(8,128)(2,1)S(1)}, bf16[81,1,16]{0,2,1:T(8,128)(2,1)}, u32[]{:S(2)}) %copy-start.5) | copy-done | bytes 2616
  31.5 0.1 copy.15
  31.6 0.1 reshape.31
  31.8 7.4 %all-to-all-done.1.held_ref = bf16[32,2,16,128]{3,2,1,0:T(8,128)(2,1)S(1)} async-done(((bf16[32,2,16,128]{3,2,1,0:T(8,128)(2,1)}), bf16[32,2,16,128]{3,2,1,0:T(8,128)(2,1)S(1)}, u32[]{:S(2)}, u32[]{:S(2)}) %all-to-all-start.1) | async-done | bytes 262176 | tf_op jit(solution)/shard_map/all_to_all | solution.py:314
  39.2 1.4 %collective-permute-start = (bf16[32,16,128]{2,1,0:T(8,128)(2,1)S(1)}, bf16[32,16,128]{2,1,0:T(8,128)(2,1)S(1)}, u32[]{:S(2)}, u32[]{:S(2)}) collective-permute-start(bf16[32,16,128]{2,1,0:T(8,128)(2,1)S(1)} %get-tuple-element.19), channel_id=1, source_target_pairs={{0,2},{1,3},{2,4},{3,5},{4,6},{5,7},{6,0},{7,1},{8,10},{9,11},{10,... | collective-permute-start | bytes 393224 | tf_op jit(solution)/shard_map/ppermute | solution.py:317
  40.6 2.6 %collective-permute-start.1 = (bf16[32,16,128]{2,1,0:T(8,128)(2,1)S(1)}, bf16[32,16,128]{2,1,0:T(8,128)(2,1)S(1)}, u32[]{:S(2)}, u32[]{:S(2)}) collective-permute-start(bf16[32,16,128]{2,1,0:T(8,128)(2,1)S(1)} %get-tuple-element.20), channel_id=1, source_target_pairs={{0,4},{1,5},{2,6},{3,7},{4,0},{5,1},{6,2},{7,3},{8,12},{9,13},{10,... | collective-permute-start | bytes 393224 | tf_op jit(solution)/shard_map/ppermute | solution.py:317
  43.2 1.1 %collective-permute-start.2 = (bf16[32,16,128]{2,1,0:T(8,128)(2,1)S(1)}, bf16[32,16,128]{2,1,0:T(8,128)(2,1)S(1)}, u32[]{:S(2)}, u32[]{:S(2)}) collective-permute-start(bf16[32,16,128]{2,1,0:T(8,128)(2,1)S(1)} %get-tuple-element.21), channel_id=1, source_target_pairs={{0,6},{1,7},{2,0},{3,1},{4,2},{5,3},{6,4},{7,5},{8,14},{9,15},{10,... | collective-permute-start | bytes 393224 | tf_op jit(solution)/shard_map/ppermute | solution.py:317
  44.3 4.3 %collective-permute-start.3 = (bf16[32,16,128]{2,1,0:T(8,128)(2,1)S(1)}, bf16[32,16,128]{2,1,0:T(8,128)(2,1)S(1)}, u32[]{:S(2)}, u32[]{:S(2)}) collective-permute-start(bf16[32,16,128]{2,1,0:T(8,128)(2,1)S(1)} %get-tuple-element.18.own_0), channel_id=1, source_target_pairs={{0,1},{1,0},{2,3},{3,2},{4,5},{5,4},{6,7},{7,6},{8,9},{9,8},{10,11... | collective-permute-start | bytes 393224 | tf_op jit(solution)/shard_map/ppermute | solution.py:318
  48.6 0.0 collective-permute-done.own_1
  48.6 0.4 collective-permute-start.4
  49.1 0.0 collective-permute-done.1.own_2
  49.1 2.5 %collective-permute-start.5 = (bf16[32,16,128]{2,1,0:T(8,128)(2,1)S(1)}, bf16[32,16,128]{2,1,0:T(8,128)(2,1)S(1)}, u32[]{:S(2)}, u32[]{:S(2)}) collective-permute-start(bf16[32,16,128]{2,1,0:T(8,128)(2,1)S(1)} %collective-permute-done.1.own_2), channel_id=1, source_target_pairs={{0,1},{1,0},{2,3},{3,2},{4,5},{5,4},{6,7},{7,6},{8,9},{9,8},{10,11... | collective-permute-start | bytes 393224 | tf_op jit(solution)/shard_map/ppermute | solution.py:318
  51.6 0.0 collective-permute-done.2.own_3
  51.6 0.6 collective-permute-start.6
  52.2 0.0 collective-permute-done.3.oth_0
  52.2 0.0 collective-permute-done.4.oth_1
  52.2 0.4 collective-permute-done.5.oth_2
  52.6 0.6 collective-permute-done.6.oth_3
  53.2 7.1 %shard_map.77 = (bf16[3,16,256]{2,1,0:T(8,128)(2,1)S(1)}, bf16[3,16,256]{2,1,0:T(8,128)(2,1)S(1)}) custom-call(s32[1]{0:T(128)} %bitcast.chip_ref, s32[1]{0:T(128)} %bitcast.1.core_ref, bf16[32,16,128]{2,1,0:T(8,128)(2,1)S(1)} %get-tuple-element.18.own_0, bf16[32,16,128]{2,1,0:T(8,128)(2,1)S(1)} %collective-permute-done.own_1, ...), custom_call_target="tpu_custom_call" | custom-call | tf_op jit(solution)/shard_map/pallas_call | solution.py:39
  60.3 0.4 collective-permute-start.7
  60.8 0.8 %collective-permute-done.7.got_ref = bf16[3,16,256]{2,1,0:T(8,128)(2,1)S(1)} collective-permute-done((bf16[3,16,256]{2,1,0:T(8,128)(2,1)S(1)}, bf16[3,16,256]{2,1,0:T(8,128)(2,1)S(1)}, u32[]{:S(2)}, u32[]{:S(2)}) %collective-permute-start.7) | collective-permute-done | bytes 24608 | tf_op jit(solution)/shard_map/ppermute | solution.py:336
  61.6 2.4 %collective-permute-start.8 = (bf16[2,16,256]{2,1,0:T(8,128)(2,1)S(1)}, bf16[2,16,256]{2,1,0:T(8,128)(2,1)S(1)}, u32[]{:S(2)}, u32[]{:S(2)}) collective-permute-start(bf16[2,16,256]{2,1,0:T(8,128)(2,1)S(1)} %get-tuple-element.28), channel_id=1, source_target_pairs={{0,6},{1,7},{2,4},{3,5},{4,2},{5,3},{6,0},{7,1},{8,14},{9,15},{10,... | collective-permute-start | bytes 49160 | tf_op jit(solution)/shard_map/ppermute | solution.py:339
  64.0 1.5 %collective-permute-done.8.far_ref = bf16[2,16,256]{2,1,0:T(8,128)(2,1)S(1)} collective-permute-done((bf16[2,16,256]{2,1,0:T(8,128)(2,1)S(1)}, bf16[2,16,256]{2,1,0:T(8,128)(2,1)S(1)}, u32[]{:S(2)}, u32[]{:S(2)}) %collective-permute-start.8) | collective-permute-done | bytes 16416 | tf_op jit(solution)/shard_map/ppermute | solution.py:339
  65.5 0.6 shard_map.79
  (8 shorter events, 0.1 us)
Async XLA Ops:
  1.8 12.1 %copy-start = (s32[64]{0:T(128)S(1)}, s32[64]{0:T(128)}, u32[]{:S(2)}) copy-start(s32[64]{0:T(128)} %src_ref.1) | copy-start | bytes 772
  1.8 12.1 %copy-start.1 = (s32[64]{0:T(128)S(1)}, s32[64]{0:T(128)}, u32[]{:S(2)}) copy-start(s32[64]{0:T(128)} %tgt_ref.1) | copy-start | bytes 772
  1.9 12.1 %copy-start.2 = (s32[64]{0:T(128)S(1)}, s32[64]{0:T(128)}, u32[]{:S(2)}) copy-start(s32[64]{0:T(128)} %slot_ref.1) | copy-start | bytes 772
  1.9 21.4 %all-to-all-start = ((bf16[32,16,128]{2,1,0:T(8,128)(2,1)}), bf16[32,16,128]{2,1,0:T(8,128)(2,1)S(1)}, u32[]{:S(2)}, u32[]{:S(2)}) async-start(bf16[32,16,128]{2,1,0:T(8,128)(2,1)} %shard_map.74), calls=%async_computation | async-start | bytes 262144 | tf_op jit(solution)/shard_map/all_to_all | solution.py:306
  24.6 4.0 %copy-start.3 = (bf16[81,16,16]{0,2,1:T(8,128)(2,1)S(1)}, bf16[81,16,16]{0,2,1:T(8,128)(2,1)}, u32[]{:S(2)}) copy-start(bf16[81,16,16]{0,2,1:T(8,128)(2,1)} %param.12) | copy-start | bytes 124420
  24.6 14.6 %all-to-all-start.1 = ((bf16[32,2,16,128]{3,2,1,0:T(8,128)(2,1)}), bf16[32,2,16,128]{3,2,1,0:T(8,128)(2,1)S(1)}, u32[]{:S(2)}, u32[]{:S(2)}) async-start(bf16[32,2,16,128]{3,2,1,0:T(8,128)(2,1)} %shard_map.75), calls=%async_computation.1 | async-start | bytes 524288 | tf_op jit(solution)/shard_map/all_to_all | solution.py:314
  29.4 0.7 %copy-start.4 = (bf16[81,16,1]{0,1,2:T(8,128)(2,1)S(1)}, bf16[81,16,1]{0,1,2:T(8,128)(2,1)}, u32[]{:S(2)}) copy-start(bf16[81,16,1]{0,1,2:T(8,128)(2,1)} %param.11) | copy-start | bytes 7780
  30.8 0.7 %copy-start.5 = (bf16[81,1,16]{0,2,1:T(8,128)(2,1)S(1)}, bf16[81,1,16]{0,2,1:T(8,128)(2,1)}, u32[]{:S(2)}) copy-start(bf16[81,1,16]{0,2,1:T(8,128)(2,1)} %param.13) | copy-start | bytes 7780
  39.2 9.4 %collective-permute-start = (bf16[32,16,128]{2,1,0:T(8,128)(2,1)S(1)}, bf16[32,16,128]{2,1,0:T(8,128)(2,1)S(1)}, u32[]{:S(2)}, u32[]{:S(2)}) collective-permute-start(bf16[32,16,128]{2,1,0:T(8,128)(2,1)S(1)} %get-tuple-element.19), channel_id=1, source_target_pairs={{0,2},{1,3},{2,4},{3,5},{4,6},{5,7},{6,0},{7,1},{8,10},{9,11},{10,... | collective-permute-start | bytes 393224 | tf_op jit(solution)/shard_map/ppermute | solution.py:317
  40.6 8.5 %collective-permute-start.1 = (bf16[32,16,128]{2,1,0:T(8,128)(2,1)S(1)}, bf16[32,16,128]{2,1,0:T(8,128)(2,1)S(1)}, u32[]{:S(2)}, u32[]{:S(2)}) collective-permute-start(bf16[32,16,128]{2,1,0:T(8,128)(2,1)S(1)} %get-tuple-element.20), channel_id=1, source_target_pairs={{0,4},{1,5},{2,6},{3,7},{4,0},{5,1},{6,2},{7,3},{8,12},{9,13},{10,... | collective-permute-start | bytes 393224 | tf_op jit(solution)/shard_map/ppermute | solution.py:317
  43.2 8.4 %collective-permute-start.2 = (bf16[32,16,128]{2,1,0:T(8,128)(2,1)S(1)}, bf16[32,16,128]{2,1,0:T(8,128)(2,1)S(1)}, u32[]{:S(2)}, u32[]{:S(2)}) collective-permute-start(bf16[32,16,128]{2,1,0:T(8,128)(2,1)S(1)} %get-tuple-element.21), channel_id=1, source_target_pairs={{0,6},{1,7},{2,0},{3,1},{4,2},{5,3},{6,4},{7,5},{8,14},{9,15},{10,... | collective-permute-start | bytes 393224 | tf_op jit(solution)/shard_map/ppermute | solution.py:317
  44.3 8.0 %collective-permute-start.3 = (bf16[32,16,128]{2,1,0:T(8,128)(2,1)S(1)}, bf16[32,16,128]{2,1,0:T(8,128)(2,1)S(1)}, u32[]{:S(2)}, u32[]{:S(2)}) collective-permute-start(bf16[32,16,128]{2,1,0:T(8,128)(2,1)S(1)} %get-tuple-element.18.own_0), channel_id=1, source_target_pairs={{0,1},{1,0},{2,3},{3,2},{4,5},{5,4},{6,7},{7,6},{8,9},{9,8},{10,11... | collective-permute-start | bytes 393224 | tf_op jit(solution)/shard_map/ppermute | solution.py:318
  48.6 3.6 %collective-permute-start.4 = (bf16[32,16,128]{2,1,0:T(8,128)(2,1)S(1)}, bf16[32,16,128]{2,1,0:T(8,128)(2,1)S(1)}, u32[]{:S(2)}, u32[]{:S(2)}) collective-permute-start(bf16[32,16,128]{2,1,0:T(8,128)(2,1)S(1)} %collective-permute-done.own_1), channel_id=1, source_target_pairs={{0,1},{1,0},{2,3},{3,2},{4,5},{5,4},{6,7},{7,6},{8,9},{9,8},{10,11... | collective-permute-start | bytes 393224 | tf_op jit(solution)/shard_map/ppermute | solution.py:318
  49.1 3.5 %collective-permute-start.5 = (bf16[32,16,128]{2,1,0:T(8,128)(2,1)S(1)}, bf16[32,16,128]{2,1,0:T(8,128)(2,1)S(1)}, u32[]{:S(2)}, u32[]{:S(2)}) collective-permute-start(bf16[32,16,128]{2,1,0:T(8,128)(2,1)S(1)} %collective-permute-done.1.own_2), channel_id=1, source_target_pairs={{0,1},{1,0},{2,3},{3,2},{4,5},{5,4},{6,7},{7,6},{8,9},{9,8},{10,11... | collective-permute-start | bytes 393224 | tf_op jit(solution)/shard_map/ppermute | solution.py:318
  51.6 1.6 %collective-permute-start.6 = (bf16[32,16,128]{2,1,0:T(8,128)(2,1)S(1)}, bf16[32,16,128]{2,1,0:T(8,128)(2,1)S(1)}, u32[]{:S(2)}, u32[]{:S(2)}) collective-permute-start(bf16[32,16,128]{2,1,0:T(8,128)(2,1)S(1)} %collective-permute-done.2.own_3), channel_id=1, source_target_pairs={{0,1},{1,0},{2,3},{3,2},{4,5},{5,4},{6,7},{7,6},{8,9},{9,8},{10,11... | collective-permute-start | bytes 393224 | tf_op jit(solution)/shard_map/ppermute | solution.py:318
  60.3 1.3 %collective-permute-start.7 = (bf16[3,16,256]{2,1,0:T(8,128)(2,1)S(1)}, bf16[3,16,256]{2,1,0:T(8,128)(2,1)S(1)}, u32[]{:S(2)}, u32[]{:S(2)}) collective-permute-start(bf16[3,16,256]{2,1,0:T(8,128)(2,1)S(1)} %get-tuple-element.26), channel_id=1, source_target_pairs={{0,1},{1,0},{2,3},{3,2},{4,5},{5,4},{6,7},{7,6},{8,9},{9,8},{10,11... | collective-permute-start | bytes 73736 | tf_op jit(solution)/shard_map/ppermute | solution.py:336
  61.6 3.9 %collective-permute-start.8 = (bf16[2,16,256]{2,1,0:T(8,128)(2,1)S(1)}, bf16[2,16,256]{2,1,0:T(8,128)(2,1)S(1)}, u32[]{:S(2)}, u32[]{:S(2)}) collective-permute-start(bf16[2,16,256]{2,1,0:T(8,128)(2,1)S(1)} %get-tuple-element.28), channel_id=1, source_target_pairs={{0,6},{1,7},{2,4},{3,5},{4,2},{5,3},{6,0},{7,1},{8,14},{9,15},{10,... | collective-permute-start | bytes 49160 | tf_op jit(solution)/shard_map/ppermute | solution.py:339

commit v4 on v2

--- a/solution.py
+++ b/solution.py
@@ -19,12 +19,12 @@
 COLS_IN = 16
 PART_1 = 10
 COLS_1, COLS_2 = BLOCK + 4, BLOCK + 2
-PART_2 = 6
+PART_2 = 3
 PART_3 = 8
 ROWS_1, ROWS_2 = COLS_1 * CONV, COLS_2 * CONV
 K_1 = 27 * COLS_IN
 K_PIECE = (PART_2 + 2) * CONV
-K_2 = 9 * K_PIECE
+K_2 = 3 * K_PIECE
 M_1 = PART_1 * CONV
 M_2 = PART_2 * CONV
 K_3 = (PART_3 + 2) * CONV
@@ -46,10 +46,7 @@
     )(*scalars, *inputs)
 
 
-def spread_kernel(src_ref, tgt_ref, slot_ref, own_ref, out_ref, slots_ref):
-    for pair in range(src_ref.shape[0]):
-        slots_ref[2 * pair] = slot_ref[src_ref[pair]]
-        slots_ref[2 * pair + 1] = slot_ref[tgt_ref[pair]]
+def spread_kernel(own_ref, out_ref):
     rows = []
     for image in range(2):
         cells = own_ref[image, 0].astype(F32)
@@ -59,6 +56,12 @@
         for block in range(8):
             at = slice(part * 8, part * 8 + 8), slice(block * 128, block * 128 + 128)
             out_ref[part * 8 + block] = jnp.concatenate([rows[0][at], rows[1][at]], axis=0).astype(BF16)
+
+
+def slots_kernel(src_ref, tgt_ref, slot_ref, slots_ref):
+    for pair in range(src_ref.shape[0]):
+        slots_ref[2 * pair] = slot_ref[src_ref[pair]]
+        slots_ref[2 * pair + 1] = slot_ref[tgt_ref[pair]]
 
 
 def select_kernel(slots_ref, held_ref, out_ref, pieces):
@@ -137,8 +140,8 @@
     z2 = z2_ref[...].astype(F32)
     rolled = [pltpu.roll(z2, CONV * j, 1) if j else z2 for j in range(PART_2)]
     w2 = jnp.concatenate(
-        [rolled[j][c * CONV : c * CONV + CONV] for c in range(3) for j in range(PART_2)], axis=0
-    ).astype(BF16)
+        [rolled[j][k * CONV : k * CONV + CONV] for k in range(9) for j in range(PART_2)], axis=0
+    ).astype(BF16)[:, :K_2]
     z3 = z3_ref[...].astype(F32)
     for j in range(PART_3):
         w3s[:, j, :] = pltpu.roll(z3, CONV * j, 1) if j else z3
@@ -152,9 +155,6 @@
                 x1[c * 3 + d, at : at + 16] = jnp.zeros((16, POS), BF16)
                 x1[c * 3 + d, at + 16 : at + 144] = moved[w * 128 : w * 128 + 128]
                 x1[c * 3 + d, at + 144 : at + 160] = jnp.zeros((16, POS), BF16)
-    for d in range(3):
-        x2[d, 0:ROWS_1] = jnp.zeros((ROWS_1, POS), BF16)
-        x2[d, (HGT + 1) * ROWS_1 :] = jnp.zeros((ROWS_1, POS), BF16)
     left_mask, right_mask = col_mask(0), col_mask(2)
     for i in range(HGT):
         for w in range(2):
@@ -166,29 +166,36 @@
                 hidden = jnp.concatenate([hidden[:edge] * has_left, hidden[edge:]], axis=0)
             else:
                 hidden = jnp.concatenate([hidden[: M_1 - edge], hidden[M_1 - edge :] * has_right], axis=0)
-            at = (i + 1) * ROWS_1 + w * M_1
+            at = i * ROWS_1 + w * M_1
             x2[0, at : at + M_1] = (shifted(hidden, -1) * left_mask).astype(BF16)
             x2[1, at : at + M_1] = hidden.astype(BF16)
             x2[2, at : at + M_1] = (shifted(hidden, 1) * right_mask).astype(BF16)
 
     up_mask, down_mask = line_mask(0), line_mask(2)
-    for i in range(HGT):
-        for part in range(3):
-            first = part * M_2
-            cells = jnp.concatenate(
-                [x2[d, (i + a) * ROWS_1 + first : (i + a) * ROWS_1 + first + K_PIECE] for d in range(3) for a in range(3)],
-                axis=0,
-            )
-            parts = jnp.dot(w2, cells, preferred_element_type=F32)
-            total = parts[M_2 : 2 * M_2]
-            total = total + shifted(parts[:M_2], -WID) * up_mask
-            total = total + shifted(parts[2 * M_2 :], WID) * down_mask
-            total = jnp.maximum(total, 0.0)
-            if part == 0:
-                total = jnp.concatenate([total[:CONV] * has_left, total[CONV:]], axis=0)
-            if part == 2:
-                total = jnp.concatenate([total[: M_2 - CONV], total[M_2 - CONV :] * has_right], axis=0)
-            h2[i, first : first + M_2] = total.astype(BF16)
+    for part in range(COLS_2 // PART_2):
+        first = part * M_2
+        rows = [None] * HGT
+        for i in range(HGT):
+            cells = jnp.concatenate([x2[d, i * ROWS_1 + first : i * ROWS_1 + first + K_PIECE] for d in range(3)], axis=0)
+            low, high = (0 if i < HGT - 1 else 1), (3 if i > 0 else 2)
+            parts = jnp.dot(w2[low * 3 * M_2 : high * 3 * M_2], cells, preferred_element_type=F32)
+            for a in range(low, high):
+                piece = parts[(a - low) * 3 * M_2 : (a - low + 1) * 3 * M_2]
+                o = i + 1 - a
+                rows[o] = piece if rows[o] is None else rows[o] + piece
+            done = [i - 1] if i < HGT - 1 else [i - 1, i]
+            for o in done:
+                if o < 0:
+                    continue
+                total = rows[o][M_2 : 2 * M_2]
+                total = total + shifted(rows[o][:M_2], -WID) * up_mask
+                total = total + shifted(rows[o][2 * M_2 :], WID) * down_mask
+                total = jnp.maximum(total, 0.0)
+                if part == 0:
+                    total = jnp.concatenate([total[:CONV] * has_left, total[CONV:]], axis=0)
+                if part == COLS_2 // PART_2 - 1:
+                    total = jnp.concatenate([total[: M_2 - CONV], total[M_2 - CONV :] * has_right], axis=0)
+                h2[o, first : first + M_2] = total.astype(BF16)
 
     best = None
     sums = [[None] * HGT for _ in range(2)]
@@ -229,6 +236,19 @@
         ref[2] = pieces
 
 
+def consensus_scratch(channels):
+    return (
+        pltpu.VMEM((HGT * FRAME, channels), F32),
+        pltpu.VMEM((2 * HGT * COLS_IN, channels), BF16),
+        pltpu.VMEM((POS, channels), F32),
+        pltpu.VMEM((9, 320, POS), BF16),
+        pltpu.VMEM((3, HGT * ROWS_1, POS), BF16),
+        pltpu.VMEM((HGT, ROWS_2, POS), BF16),
+        pltpu.VMEM((27, PART_3, 256), F32),
+        pltpu.VMEM((HGT, 16, POS), BF16),
+    )
+
+
 def finish_kernel(core_ref, keep_ref, got_ref, near_ref, far_ref, lines):
     core = core_ref[0]
 
@@ -265,17 +285,19 @@
     taps = w_first.reshape(3, 3, 3, 3, CONV).transpose(4, 2, 3, 0, 1)
     z1 = jnp.pad(taps, ((0, 0),) * 4 + ((1, COLS_IN - 4),)).reshape(CONV, K_1)
     z1 = jnp.pad(z1, ((0, 0), (0, 512 - K_1)))
-    taps = w_mid.reshape(3, 3, 3, 3, CONV, CONV).transpose(2, 4, 3, 0, 1, 5)
-    z2 = jnp.pad(taps, ((0, 0),) * 4 + ((0, PART_2 - 1), (0, 0))).reshape(3 * CONV, K_2)
+    taps = w_mid.reshape(3, 3, 3, 3, CONV, CONV).transpose(0, 2, 4, 3, 1, 5)
+    z2 = jnp.pad(taps, ((0, 0),) * 4 + ((0, PART_2 - 1), (0, 0))).reshape(9 * CONV, K_2)
+    z2 = jnp.pad(z2, ((0, 0), (0, 256 - K_2)))
     z3 = w_last.reshape(3, 3, 3, 3, CONV).transpose(0, 2, 3, 1, 4).reshape(27, 3 * CONV)
     z3 = jnp.pad(z3, ((0, 0), (0, 256 - 3 * CONV)))
 
-    tiles, slots = call(
-        spread_kernel,
-        (jax.ShapeDtypeStruct((groups, 16, 128), BF16), jax.ShapeDtypeStruct((2 * src_ids.shape[0],), jnp.int32)),
-        (features,),
+    tiles = call(spread_kernel, jax.ShapeDtypeStruct((groups, 16, 128), BF16), (features,))
+    slots = call(
+        slots_kernel,
+        jax.ShapeDtypeStruct((2 * src_ids.shape[0],), jnp.int32),
+        (),
         (src_ids, tgt_ids, image_slot),
-        out_specs=(whole(), whole(pltpu.SMEM)),
+        out_specs=whole(pltpu.SMEM),
     )
     held = lax.all_to_all(tiles, "pair", 0, 0, tiled=True)
     wanted = call(
@@ -286,6 +308,7 @@
         (pltpu.VMEM((2 * groups, 8, 128), F32),),
     )
     routed = lax.all_to_all(wanted, "pair", 0, 0, tiled=True)
+    routed, z1, z2, z3 = lax.optimization_barrier((routed, z1, z2, z3))
     sends = call(pack_kernel, (jax.ShapeDtypeStruct((groups, 16, 128), BF16),) * 4, (routed,), (chip,))
     own = [sends[0]] + [lax.ppermute(sends[k], "row", row_moves(k, 0)) for k in range(1, CHIPS)]
     other = [lax.ppermute(block, "row", row_moves(0, 1)) for block in own]
@@ -295,16 +318,7 @@
         (message, message),
         (*own, *other, z1, z2, z3),
         (chip, core),
-        (
-            pltpu.VMEM((HGT * FRAME, channels), F32),
-            pltpu.VMEM((2 * HGT * COLS_IN, channels), BF16),
-            pltpu.VMEM((POS, channels), F32),
-            pltpu.VMEM((9, 320, POS), BF16),
-            pltpu.VMEM((3, (HGT + 2) * ROWS_1, POS), BF16),
-            pltpu.VMEM((HGT, ROWS_2, POS), BF16),
-            pltpu.VMEM((27, PART_3, 256), F32),
-            pltpu.VMEM((HGT, 16, POS), BF16),
-        ),
+        consensus_scratch(channels),
     )
     got = lax.ppermute(give, "row", row_moves(0, 1))
     lines = jax.ShapeDtypeStruct((2, BLOCK, POS), BF16)

time: 70.4 us -> 64.2 us (0.912)
  blocking collectives: 21 us -> 0 us
  starting transfers between devices: 19.3 us -> 31.8 us
  waiting for transfers between devices: 13.3 us -> 18.4 us
  local copies, waits for them, and re-layouts: 5.93 us -> 4.4 us
  Pallas kernels: 10.4 us -> 9.14 us
    all_to_all x1 -> x0, blocking collectives: 21 us -> none  [local(): held = lax.all_to_all(tiles, 'pair', 0, 0, tiled=True)]
    all_to_all x0 -> x1, starting transfers between devices: none -> 12 us  [local(): held = lax.all_to_all(tiles, 'pair', 0, 0, tiled=True)]
    all_to_all x0 -> x1, waiting for transfers between devices: none -> 8.02 us  [local(): held = lax.all_to_all(tiles, 'pair', 0, 0, tiled=True)]
    all_to_all x1, waiting for transfers between devices: 10.6 us -> 6.97 us  [local(): routed = lax.all_to_all(wanted, 'pair', 0, 0, tiled=True)]
    unnamed x19, local copies, waits for them, and re-layouts: 4.66 us -> 3.27 us
    pallas_call x6 -> x7, Pallas kernels: 10.4 us -> 9.14 us  [call(): pl.pallas_call(kernel, out_shape=out_shape, in_specs=[whole(pltpu.SMEM)]...]
    ppermute x4, waiting for transfers between devices: 0.01 us -> 0.98 us  [local(): other = [lax.ppermute(block, 'row', row_moves(0, 1)) for block in own]]
  transfers between devices with their start and end apart: 10 -> 11, of which waited for: 3 -> 6; matrix products, arithmetic and copies ran while one was open for 3% -> 3% of each run, Pallas kernels for 0% -> 2%
where the time goes in v4:
time: 64.2 us; the launch traced here: 63.9 us
  starting transfers between devices  31.8 us (50%)
  waiting for transfers between devices  18.4 us (29%)
  Pallas kernels  9.14 us (14%)
  local copies, waits for them, and re-layouts  4.4 us (7%)
    all_to_all x1, starting transfers between devices, local(): held = lax.all_to_all(tiles, 'pair', 0, 0, tiled=True)  12 us
    pallas_call x7, Pallas kernels, call(): pl.pallas_call(kernel, out_shape=out_shape, in_specs=[whole(pltpu.SMEM)]...  9.14 us
    all_to_all x1, waiting for transfers between devices, local(): held = lax.all_to_all(tiles, 'pair', 0, 0, tiled=True)  8.02 us
    ppermute x4, starting transfers between devices, local(): other = [lax.ppermute(block, 'row', row_moves(0, 1)) for block in own]  7.94 us
    all_to_all x1, waiting for transfers between devices, local(): routed = lax.all_to_all(wanted, 'pair', 0, 0, tiled=True)  6.97 us
    ppermute x3, starting transfers between devices, local(): lax.ppermute(sends[k], 'row', row_moves(k, 0))  5.06 us
    all_to_all x1, starting transfers between devices, local(): routed = lax.all_to_all(wanted, 'pair', 0, 0, tiled=True)  4 us
    unnamed x19, local copies, waits for them, and re-layouts  3.27 us
  transfers between devices with their start and end apart: 11, of which 6 were waited for; matrix products, arithmetic and copies ran while one was open for 3% of the time, Pallas kernels for 2%

profile of v4, /device:TPU:1, one launch (start us, length us, event | category | flops | bytes accessed | tf_op | source)
XLA Modules:
  0.0 63.9 jit_solution(4169187327969555098)
XLA Ops:
  0.0 0.0 copy-start
  0.0 0.9 %copy-done = bf16[2,1,32,1024]{3,2,1,0:T(8,128)(2,1)S(1)} copy-done((bf16[2,1,32,1024]{3,2,1,0:T(8,128)(2,1)S(1)}, bf16[2,1,32,1024]{3,2,1,0:T(8,128)(2,1)}, u32[]{:S(2)}) %copy-start) | copy-done | bytes 131096
  0.9 0.8 %shard_map.74 = bf16[32,16,128]{2,1,0:T(8,128)(2,1)} custom-call(bf16[2,1,32,1024]{3,2,1,0:T(8,128)(2,1)S(1)} %copy-done), custom_call_target="tpu_custom_call" | custom-call | tf_op jit(solution)/shard_map/pallas_call | solution.py:39
  1.7 0.0 copy-start.1
  1.7 12.0 %all-to-all-start = ((bf16[32,16,128]{2,1,0:T(8,128)(2,1)}), bf16[32,16,128]{2,1,0:T(8,128)(2,1)S(1)}, u32[]{:S(2)}, u32[]{:S(2)}) async-start(bf16[32,16,128]{2,1,0:T(8,128)(2,1)} %shard_map.74), calls=%async_computation | async-start | bytes 262144 | tf_op jit(solution)/shard_map/all_to_all | solution.py:302
  13.7 0.0 copy-done.1
  13.7 0.0 copy-done.2
  13.7 0.0 copy-done.3
  13.7 1.3 %shard_map.73.slots_ref = s32[128]{0:T(128)S(1)} custom-call(s32[64]{0:T(128)S(1)} %copy-done.1, s32[64]{0:T(128)S(1)} %copy-done.2, s32[64]{0:T(128)S(1)} %copy-done.3), custom_call_target="tpu_custom_call" | custom-call | tf_op jit(solution)/shard_map/pallas_call | solution.py:39
  15.0 8.0 %all-to-all-done.held_ref = bf16[32,16,128]{2,1,0:T(8,128)(2,1)S(1)} async-done(((bf16[32,16,128]{2,1,0:T(8,128)(2,1)}), bf16[32,16,128]{2,1,0:T(8,128)(2,1)S(1)}, u32[]{:S(2)}, u32[]{:S(2)}) %all-to-all-start) | async-done | bytes 131104 | tf_op jit(solution)/shard_map/all_to_all | solution.py:302
  23.0 1.3 %shard_map.75 = bf16[32,2,16,128]{3,2,1,0:T(8,128)(2,1)} custom-call(s32[128]{0:T(128)S(1)} %shard_map.73.slots_ref, bf16[32,16,128]{2,1,0:T(8,128)(2,1)S(1)} %all-to-all-done.held_ref), custom_call_target="tpu_custom_call" | custom-call | tf_op jit(solution)/shard_map/pallas_call | solution.py:39
  24.4 4.0 %all-to-all-start.1 = ((bf16[32,2,16,128]{3,2,1,0:T(8,128)(2,1)}), bf16[32,2,16,128]{3,2,1,0:T(8,128)(2,1)S(1)}, u32[]{:S(2)}, u32[]{:S(2)}) async-start(bf16[32,2,16,128]{3,2,1,0:T(8,128)(2,1)} %shard_map.75), calls=%async_computation.1 | async-start | bytes 524288 | tf_op jit(solution)/shard_map/all_to_all | solution.py:310
  28.4 0.0 copy-done.4
  28.4 0.3 copy.13
  28.7 0.2 copy.21
  28.9 0.2 pad.22.clone
  29.2 0.4 reshape.32
  29.6 0.0 copy-start.5
  29.6 0.7 %copy-done.5 = bf16[81,16,1]{0,1,2:T(8,128)(2,1)S(1)} copy-done((bf16[81,16,1]{0,1,2:T(8,128)(2,1)S(1)}, bf16[81,16,1]{0,1,2:T(8,128)(2,1)}, u32[]{:S(2)}) %copy-start.5) | copy-done | bytes 2616
  30.3 0.1 copy.11
  30.4 0.3 copy.20
  30.7 0.2 pad.20.clone
  30.9 0.1 reshape.27
  31.0 0.0 copy-start.6
  31.0 0.7 %copy-done.6 = bf16[81,1,16]{0,2,1:T(8,128)(2,1)S(1)} copy-done((bf16[81,1,16]{0,2,1:T(8,128)(2,1)S(1)}, bf16[81,1,16]{0,2,1:T(8,128)(2,1)}, u32[]{:S(2)}) %copy-start.6) | copy-done | bytes 2616
  31.7 0.1 copy.16
  31.9 0.1 reshape.31
  32.0 7.0 %all-to-all-done.1.held_ref = bf16[32,2,16,128]{3,2,1,0:T(8,128)(2,1)S(1)} async-done(((bf16[32,2,16,128]{3,2,1,0:T(8,128)(2,1)}), bf16[32,2,16,128]{3,2,1,0:T(8,128)(2,1)S(1)}, u32[]{:S(2)}, u32[]{:S(2)}) %all-to-all-start.1) | async-done | bytes 262176 | tf_op jit(solution)/shard_map/all_to_all | solution.py:310
  39.0 1.4 %collective-permute-start = (bf16[32,16,128]{2,1,0:T(8,128)(2,1)S(1)}, bf16[32,16,128]{2,1,0:T(8,128)(2,1)S(1)}, u32[]{:S(2)}, u32[]{:S(2)}) collective-permute-start(bf16[32,16,128]{2,1,0:T(8,128)(2,1)S(1)} %get-tuple-element.19), channel_id=1, source_target_pairs={{0,2},{1,3},{2,4},{3,5},{4,6},{5,7},{6,0},{7,1},{8,10},{9,11},{10,... | collective-permute-start | bytes 393224 | tf_op jit(solution)/shard_map/ppermute | solution.py:313
  40.4 2.6 %collective-permute-start.1 = (bf16[32,16,128]{2,1,0:T(8,128)(2,1)S(1)}, bf16[32,16,128]{2,1,0:T(8,128)(2,1)S(1)}, u32[]{:S(2)}, u32[]{:S(2)}) collective-permute-start(bf16[32,16,128]{2,1,0:T(8,128)(2,1)S(1)} %get-tuple-element.20), channel_id=1, source_target_pairs={{0,4},{1,5},{2,6},{3,7},{4,0},{5,1},{6,2},{7,3},{8,12},{9,13},{10,... | collective-permute-start | bytes 393224 | tf_op jit(solution)/shard_map/ppermute | solution.py:313
  43.0 1.1 %collective-permute-start.2 = (bf16[32,16,128]{2,1,0:T(8,128)(2,1)S(1)}, bf16[32,16,128]{2,1,0:T(8,128)(2,1)S(1)}, u32[]{:S(2)}, u32[]{:S(2)}) collective-permute-start(bf16[32,16,128]{2,1,0:T(8,128)(2,1)S(1)} %get-tuple-element.21), channel_id=1, source_target_pairs={{0,6},{1,7},{2,0},{3,1},{4,2},{5,3},{6,4},{7,5},{8,14},{9,15},{10,... | collective-permute-start | bytes 393224 | tf_op jit(solution)/shard_map/ppermute | solution.py:313
  44.1 4.3 %collective-permute-start.3 = (bf16[32,16,128]{2,1,0:T(8,128)(2,1)S(1)}, bf16[32,16,128]{2,1,0:T(8,128)(2,1)S(1)}, u32[]{:S(2)}, u32[]{:S(2)}) collective-permute-start(bf16[32,16,128]{2,1,0:T(8,128)(2,1)S(1)} %get-tuple-element.18.own_0), channel_id=1, source_target_pairs={{0,1},{1,0},{2,3},{3,2},{4,5},{5,4},{6,7},{7,6},{8,9},{9,8},{10,11... | collective-permute-start | bytes 393224 | tf_op jit(solution)/shard_map/ppermute | solution.py:314
  48.4 0.0 collective-permute-done.own_1
  48.4 0.4 collective-permute-start.4
  48.8 0.0 collective-permute-done.1.own_2
  48.9 2.5 %collective-permute-start.5 = (bf16[32,16,128]{2,1,0:T(8,128)(2,1)S(1)}, bf16[32,16,128]{2,1,0:T(8,128)(2,1)S(1)}, u32[]{:S(2)}, u32[]{:S(2)}) collective-permute-start(bf16[32,16,128]{2,1,0:T(8,128)(2,1)S(1)} %collective-permute-done.1.own_2), channel_id=1, source_target_pairs={{0,1},{1,0},{2,3},{3,2},{4,5},{5,4},{6,7},{7,6},{8,9},{9,8},{10,11... | collective-permute-start | bytes 393224 | tf_op jit(solution)/shard_map/ppermute | solution.py:314
  51.4 0.0 collective-permute-done.2.own_3
  51.4 0.6 collective-permute-start.6
  52.0 0.0 collective-permute-done.3.oth_0
  52.0 0.0 collective-permute-done.4.oth_1
  52.0 0.4 collective-permute-done.5.oth_2
  52.4 0.6 collective-permute-done.6.oth_3
  53.0 5.1 %shard_map.77 = (bf16[3,16,256]{2,1,0:T(8,128)(2,1)S(1)}, bf16[3,16,256]{2,1,0:T(8,128)(2,1)S(1)}) custom-call(s32[1]{0:T(128)} %bitcast.chip_ref, s32[1]{0:T(128)} %bitcast.1.core_ref, bf16[32,16,128]{2,1,0:T(8,128)(2,1)S(1)} %get-tuple-element.18.own_0, bf16[32,16,128]{2,1,0:T(8,128)(2,1)S(1)} %collective-permute-done.own_1, ...), custom_call_target="tpu_custom_call" | custom-call | tf_op jit(solution)/shard_map/pallas_call | solution.py:39
  58.1 0.4 collective-permute-start.7
  58.5 0.8 %collective-permute-done.7.got_ref = bf16[3,16,256]{2,1,0:T(8,128)(2,1)S(1)} collective-permute-done((bf16[3,16,256]{2,1,0:T(8,128)(2,1)S(1)}, bf16[3,16,256]{2,1,0:T(8,128)(2,1)S(1)}, u32[]{:S(2)}, u32[]{:S(2)}) %collective-permute-start.7) | collective-permute-done | bytes 24608 | tf_op jit(solution)/shard_map/ppermute | solution.py:323
  59.4 2.4 %collective-permute-start.8 = (bf16[2,16,256]{2,1,0:T(8,128)(2,1)S(1)}, bf16[2,16,256]{2,1,0:T(8,128)(2,1)S(1)}, u32[]{:S(2)}, u32[]{:S(2)}) collective-permute-start(bf16[2,16,256]{2,1,0:T(8,128)(2,1)S(1)} %get-tuple-element.28), channel_id=1, source_target_pairs={{0,6},{1,7},{2,4},{3,5},{4,2},{5,3},{6,0},{7,1},{8,14},{9,15},{10,... | collective-permute-start | bytes 49160 | tf_op jit(solution)/shard_map/ppermute | solution.py:326
  61.8 1.5 %collective-permute-done.8.far_ref = bf16[2,16,256]{2,1,0:T(8,128)(2,1)S(1)} collective-permute-done((bf16[2,16,256]{2,1,0:T(8,128)(2,1)S(1)}, bf16[2,16,256]{2,1,0:T(8,128)(2,1)S(1)}, u32[]{:S(2)}, u32[]{:S(2)}) %collective-permute-start.8) | collective-permute-done | bytes 16416 | tf_op jit(solution)/shard_map/ppermute | solution.py:326
  63.3 0.6 shard_map.79
  (11 shorter events, 0.2 us)
Async XLA Ops:
  0.0 0.9 %copy-start = (bf16[2,1,32,1024]{3,2,1,0:T(8,128)(2,1)S(1)}, bf16[2,1,32,1024]{3,2,1,0:T(8,128)(2,1)}, u32[]{:S(2)}) copy-start(bf16[2,1,32,1024]{3,2,1,0:T(8,128)(2,1)} %own_ref.1) | copy-start | bytes 393220
  1.7 12.0 %copy-start.1 = (s32[64]{0:T(128)S(1)}, s32[64]{0:T(128)}, u32[]{:S(2)}) copy-start(s32[64]{0:T(128)} %src_ref.1) | copy-start | bytes 772
  1.7 12.0 %copy-start.2 = (s32[64]{0:T(128)S(1)}, s32[64]{0:T(128)}, u32[]{:S(2)}) copy-start(s32[64]{0:T(128)} %tgt_ref.1) | copy-start | bytes 772
  1.7 12.0 %copy-start.3 = (s32[64]{0:T(128)S(1)}, s32[64]{0:T(128)}, u32[]{:S(2)}) copy-start(s32[64]{0:T(128)} %slot_ref.1) | copy-start | bytes 772
  1.7 21.4 %all-to-all-start = ((bf16[32,16,128]{2,1,0:T(8,128)(2,1)}), bf16[32,16,128]{2,1,0:T(8,128)(2,1)S(1)}, u32[]{:S(2)}, u32[]{:S(2)}) async-start(bf16[32,16,128]{2,1,0:T(8,128)(2,1)} %shard_map.74), calls=%async_computation | async-start | bytes 262144 | tf_op jit(solution)/shard_map/all_to_all | solution.py:302
  24.4 4.0 %copy-start.4 = (bf16[81,16,16]{0,2,1:T(8,128)(2,1)S(1)}, bf16[81,16,16]{0,2,1:T(8,128)(2,1)}, u32[]{:S(2)}) copy-start(bf16[81,16,16]{0,2,1:T(8,128)(2,1)} %param.12) | copy-start | bytes 124420
  24.4 14.6 %all-to-all-start.1 = ((bf16[32,2,16,128]{3,2,1,0:T(8,128)(2,1)}), bf16[32,2,16,128]{3,2,1,0:T(8,128)(2,1)S(1)}, u32[]{:S(2)}, u32[]{:S(2)}) async-start(bf16[32,2,16,128]{3,2,1,0:T(8,128)(2,1)} %shard_map.75), calls=%async_computation.1 | async-start | bytes 524288 | tf_op jit(solution)/shard_map/all_to_all | solution.py:310
  29.6 0.7 %copy-start.5 = (bf16[81,16,1]{0,1,2:T(8,128)(2,1)S(1)}, bf16[81,16,1]{0,1,2:T(8,128)(2,1)}, u32[]{:S(2)}) copy-start(bf16[81,16,1]{0,1,2:T(8,128)(2,1)} %param.11) | copy-start | bytes 7780
  31.0 0.7 %copy-start.6 = (bf16[81,1,16]{0,2,1:T(8,128)(2,1)S(1)}, bf16[81,1,16]{0,2,1:T(8,128)(2,1)}, u32[]{:S(2)}) copy-start(bf16[81,1,16]{0,2,1:T(8,128)(2,1)} %param.13) | copy-start | bytes 7780
  39.0 9.4 %collective-permute-start = (bf16[32,16,128]{2,1,0:T(8,128)(2,1)S(1)}, bf16[32,16,128]{2,1,0:T(8,128)(2,1)S(1)}, u32[]{:S(2)}, u32[]{:S(2)}) collective-permute-start(bf16[32,16,128]{2,1,0:T(8,128)(2,1)S(1)} %get-tuple-element.19), channel_id=1, source_target_pairs={{0,2},{1,3},{2,4},{3,5},{4,6},{5,7},{6,0},{7,1},{8,10},{9,11},{10,... | collective-permute-start | bytes 393224 | tf_op jit(solution)/shard_map/ppermute | solution.py:313
  40.4 8.5 %collective-permute-start.1 = (bf16[32,16,128]{2,1,0:T(8,128)(2,1)S(1)}, bf16[32,16,128]{2,1,0:T(8,128)(2,1)S(1)}, u32[]{:S(2)}, u32[]{:S(2)}) collective-permute-start(bf16[32,16,128]{2,1,0:T(8,128)(2,1)S(1)} %get-tuple-element.20), channel_id=1, source_target_pairs={{0,4},{1,5},{2,6},{3,7},{4,0},{5,1},{6,2},{7,3},{8,12},{9,13},{10,... | collective-permute-start | bytes 393224 | tf_op jit(solution)/shard_map/ppermute | solution.py:313
  43.0 8.4 %collective-permute-start.2 = (bf16[32,16,128]{2,1,0:T(8,128)(2,1)S(1)}, bf16[32,16,128]{2,1,0:T(8,128)(2,1)S(1)}, u32[]{:S(2)}, u32[]{:S(2)}) collective-permute-start(bf16[32,16,128]{2,1,0:T(8,128)(2,1)S(1)} %get-tuple-element.21), channel_id=1, source_target_pairs={{0,6},{1,7},{2,0},{3,1},{4,2},{5,3},{6,4},{7,5},{8,14},{9,15},{10,... | collective-permute-start | bytes 393224 | tf_op jit(solution)/shard_map/ppermute | solution.py:313
  44.1 8.0 %collective-permute-start.3 = (bf16[32,16,128]{2,1,0:T(8,128)(2,1)S(1)}, bf16[32,16,128]{2,1,0:T(8,128)(2,1)S(1)}, u32[]{:S(2)}, u32[]{:S(2)}) collective-permute-start(bf16[32,16,128]{2,1,0:T(8,128)(2,1)S(1)} %get-tuple-element.18.own_0), channel_id=1, source_target_pairs={{0,1},{1,0},{2,3},{3,2},{4,5},{5,4},{6,7},{7,6},{8,9},{9,8},{10,11... | collective-permute-start | bytes 393224 | tf_op jit(solution)/shard_map/ppermute | solution.py:314
  48.4 3.6 %collective-permute-start.4 = (bf16[32,16,128]{2,1,0:T(8,128)(2,1)S(1)}, bf16[32,16,128]{2,1,0:T(8,128)(2,1)S(1)}, u32[]{:S(2)}, u32[]{:S(2)}) collective-permute-start(bf16[32,16,128]{2,1,0:T(8,128)(2,1)S(1)} %collective-permute-done.own_1), channel_id=1, source_target_pairs={{0,1},{1,0},{2,3},{3,2},{4,5},{5,4},{6,7},{7,6},{8,9},{9,8},{10,11... | collective-permute-start | bytes 393224 | tf_op jit(solution)/shard_map/ppermute | solution.py:314
  48.9 3.5 %collective-permute-start.5 = (bf16[32,16,128]{2,1,0:T(8,128)(2,1)S(1)}, bf16[32,16,128]{2,1,0:T(8,128)(2,1)S(1)}, u32[]{:S(2)}, u32[]{:S(2)}) collective-permute-start(bf16[32,16,128]{2,1,0:T(8,128)(2,1)S(1)} %collective-permute-done.1.own_2), channel_id=1, source_target_pairs={{0,1},{1,0},{2,3},{3,2},{4,5},{5,4},{6,7},{7,6},{8,9},{9,8},{10,11... | collective-permute-start | bytes 393224 | tf_op jit(solution)/shard_map/ppermute | solution.py:314
  51.4 1.6 %collective-permute-start.6 = (bf16[32,16,128]{2,1,0:T(8,128)(2,1)S(1)}, bf16[32,16,128]{2,1,0:T(8,128)(2,1)S(1)}, u32[]{:S(2)}, u32[]{:S(2)}) collective-permute-start(bf16[32,16,128]{2,1,0:T(8,128)(2,1)S(1)} %collective-permute-done.2.own_3), channel_id=1, source_target_pairs={{0,1},{1,0},{2,3},{3,2},{4,5},{5,4},{6,7},{7,6},{8,9},{9,8},{10,11... | collective-permute-start | bytes 393224 | tf_op jit(solution)/shard_map/ppermute | solution.py:314
  58.1 1.3 %collective-permute-start.7 = (bf16[3,16,256]{2,1,0:T(8,128)(2,1)S(1)}, bf16[3,16,256]{2,1,0:T(8,128)(2,1)S(1)}, u32[]{:S(2)}, u32[]{:S(2)}) collective-permute-start(bf16[3,16,256]{2,1,0:T(8,128)(2,1)S(1)} %get-tuple-element.26), channel_id=1, source_target_pairs={{0,1},{1,0},{2,3},{3,2},{4,5},{5,4},{6,7},{7,6},{8,9},{9,8},{10,11... | collective-permute-start | bytes 73736 | tf_op jit(solution)/shard_map/ppermute | solution.py:323
  59.4 3.9 %collective-permute-start.8 = (bf16[2,16,256]{2,1,0:T(8,128)(2,1)S(1)}, bf16[2,16,256]{2,1,0:T(8,128)(2,1)S(1)}, u32[]{:S(2)}, u32[]{:S(2)}) collective-permute-start(bf16[2,16,256]{2,1,0:T(8,128)(2,1)S(1)} %get-tuple-element.28), channel_id=1, source_target_pairs={{0,6},{1,7},{2,4},{3,5},{4,2},{5,3},{6,0},{7,1},{8,14},{9,15},{10,... | collective-permute-start | bytes 49160 | tf_op jit(solution)/shard_map/ppermute | solution.py:326

commit v5 on v4

--- a/solution.py
+++ b/solution.py
@@ -46,10 +46,27 @@
     )(*scalars, *inputs)
 
 
-def spread_kernel(own_ref, out_ref):
+def spread_kernel(src_hbm, tgt_hbm, slot_hbm, own_hbm, out_ref, slots_ref, src_ref, tgt_ref, slot_ref, rows_ref, sems):
+    loads = [
+        pltpu.make_async_copy(hbm, ref, sems.at[place])
+        for place, (hbm, ref) in enumerate(((src_hbm, src_ref), (tgt_hbm, tgt_ref), (slot_hbm, slot_ref)))
+    ]
+    for load in loads:
+        load.start()
+    rows_load = pltpu.make_async_copy(own_hbm, rows_ref, sems.at[3])
+    rows_load.start()
+    for load in loads:
+        load.wait()
+    batch = 16
+    for first in range(0, src_ref.shape[0], batch):
+        pairs = range(first, first + batch)
+        ids = [ref[pair] for pair in pairs for ref in (src_ref, tgt_ref)]
+        for place, slot in enumerate([slot_ref[image] for image in ids]):
+            slots_ref[2 * first + place] = slot
+    rows_load.wait()
     rows = []
     for image in range(2):
-        cells = own_ref[image, 0].astype(F32)
+        cells = rows_ref[image, 0].astype(F32)
         scale = lax.rsqrt(jnp.sum(cells * cells, axis=-1, keepdims=True) + NORM_EPS)
         rows.append(cells * scale)
     for part in range(4):
@@ -58,24 +75,19 @@
             out_ref[part * 8 + block] = jnp.concatenate([rows[0][at], rows[1][at]], axis=0).astype(BF16)
 
 
-def slots_kernel(src_ref, tgt_ref, slot_ref, slots_ref):
-    for pair in range(src_ref.shape[0]):
-        slots_ref[2 * pair] = slot_ref[src_ref[pair]]
-        slots_ref[2 * pair + 1] = slot_ref[tgt_ref[pair]]
-
-
 def select_kernel(slots_ref, held_ref, out_ref, pieces):
     groups = held_ref.shape[0]
     for group in range(groups):
         both = held_ref[group].astype(F32)
         pieces[2 * group] = both[:8]
         pieces[2 * group + 1] = both[8:]
-    for group in range(groups):
-        for pair in range(2):
-            at = 4 * group + 2 * pair
-            out_ref[group, pair] = jnp.concatenate(
-                [pieces[slots_ref[at]], pieces[slots_ref[at + 1]]], axis=0
-            ).astype(BF16)
+    batch = 4
+    for first in range(0, groups, batch):
+        slots = [slots_ref[4 * first + place] for place in range(4 * batch)]
+        found = [pieces[slot] for slot in slots]
+        for at in range(2 * batch):
+            both = jnp.concatenate([found[2 * at], found[2 * at + 1]], axis=0)
+            out_ref[first + at // 2, at % 2] = both.astype(BF16)
 
 
 def pack_kernel(chip_ref, held_ref, out_0, out_1, out_2, out_3):
@@ -282,6 +294,30 @@
     chip = (place // 2).reshape(1)
     core = (place % 2).reshape(1)
 
+    ids = src_ids.shape
+    tiles, slots = pl.pallas_call(
+        spread_kernel,
+        out_shape=(jax.ShapeDtypeStruct((groups, 16, 128), BF16), jax.ShapeDtypeStruct((2 * ids[0],), jnp.int32)),
+        in_specs=[whole(pl.ANY)] * 4,
+        out_specs=(whole(), whole(pltpu.SMEM)),
+        scratch_shapes=[
+            pltpu.SMEM(ids, jnp.int32),
+            pltpu.SMEM(ids, jnp.int32),
+            pltpu.SMEM(image_slot.shape, jnp.int32),
+            pltpu.VMEM(features.shape, BF16),
+            pltpu.SemaphoreType.DMA((4,)),
+        ],
+    )(src_ids, tgt_ids, image_slot, features)
+    held = lax.all_to_all(tiles, "pair", 0, 0, tiled=True)
+    held, w_first, w_mid, w_last = lax.optimization_barrier((held, w_first, w_mid, w_last))
+    wanted = call(
+        select_kernel,
+        jax.ShapeDtypeStruct((groups, 2, 16, 128), BF16),
+        (held,),
+        (slots,),
+        (pltpu.VMEM((2 * groups, 8, 128), F32),),
+    )
+    routed = lax.all_to_all(wanted, "pair", 0, 0, tiled=True)
     taps = w_first.reshape(3, 3, 3, 3, CONV).transpose(4, 2, 3, 0, 1)
     z1 = jnp.pad(taps, ((0, 0),) * 4 + ((1, COLS_IN - 4),)).reshape(CONV, K_1)
     z1 = jnp.pad(z1, ((0, 0), (0, 512 - K_1)))
@@ -291,23 +327,6 @@
     z3 = w_last.reshape(3, 3, 3, 3, CONV).transpose(0, 2, 3, 1, 4).reshape(27, 3 * CONV)
     z3 = jnp.pad(z3, ((0, 0), (0, 256 - 3 * CONV)))
 
-    tiles = call(spread_kernel, jax.ShapeDtypeStruct((groups, 16, 128), BF16), (features,))
-    slots = call(
-        slots_kernel,
-        jax.ShapeDtypeStruct((2 * src_ids.shape[0],), jnp.int32),
-        (),
-        (src_ids, tgt_ids, image_slot),
-        out_specs=whole(pltpu.SMEM),
-    )
-    held = lax.all_to_all(tiles, "pair", 0, 0, tiled=True)
-    wanted = call(
-        select_kernel,
-        jax.ShapeDtypeStruct((groups, 2, 16, 128), BF16),
-        (held,),
-        (slots,),
-        (pltpu.VMEM((2 * groups, 8, 128), F32),),
-    )
-    routed = lax.all_to_all(wanted, "pair", 0, 0, tiled=True)
     routed, z1, z2, z3 = lax.optimization_barrier((routed, z1, z2, z3))
     sends = call(pack_kernel, (jax.ShapeDtypeStruct((groups, 16, 128), BF16),) * 4, (routed,), (chip,))
     own = [sends[0]] + [lax.ppermute(sends[k], "row", row_moves(k, 0)) for k in range(1, CHIPS)]

time: 64.2 us -> 64.9 us (1.011)
  blocking collectives: 0 us -> 21.2 us
  starting transfers between devices: 31.8 us -> 19.8 us
  waiting for transfers between devices: 18.4 us -> 10.3 us
    all_to_all x0 -> x1, blocking collectives: none -> 21.2 us  [local(): held = lax.all_to_all(tiles, 'pair', 0, 0, tiled=True)]
    all_to_all x1 -> x0, starting transfers between devices: 12 us -> none  [local(): held = lax.all_to_all(tiles, 'pair', 0, 0, tiled=True)]
    all_to_all x1 -> x0, waiting for transfers between devices: 8.02 us -> none  [local(): held = lax.all_to_all(tiles, 'pair', 0, 0, tiled=True)]
    pallas_call x7 -> x5, Pallas kernels: 9.14 us -> 7.1 us  [call(): pl.pallas_call(kernel, out_shape=out_shape, in_specs=[whole(pltpu.SMEM)]...]
    pallas_call x0 -> x1, Pallas kernels: none -> 1.74 us  [local(): pl.pallas_call(spread_kernel, out_shape=(jax.ShapeDtypeStruct((groups, 16...]
    unnamed x19 -> x10, local copies, waits for them, and re-layouts: 3.27 us -> 2.45 us
  transfers between devices with their start and end apart: 11 -> 10, of which waited for: 6 -> 5; matrix products, arithmetic and copies ran while one was open for 3% -> 3% of each run, Pallas kernels for 2% -> 0%
where the time goes in v5:
time: 64.9 us; the launch traced here: 64.5 us
  blocking collectives  21.2 us (33%)
  starting transfers between devices  19.8 us (31%)
  waiting for transfers between devices  10.3 us (16%)
  Pallas kernels  8.84 us (14%)
  local copies, waits for them, and re-layouts  4.14 us (6%)
    all_to_all x1, blocking collectives, local(): held = lax.all_to_all(tiles, 'pair', 0, 0, tiled=True)  21.2 us
    ppermute x4, starting transfers between devices, local(): other = [lax.ppermute(block, 'row', row_moves(0, 1)) for block in own]  7.94 us
    pallas_call x5, Pallas kernels, call(): pl.pallas_call(kernel, out_shape=out_shape, in_specs=[whole(pltpu.SMEM)]...  7.1 us
    all_to_all x1, waiting for transfers between devices, local(): routed = lax.all_to_all(wanted, 'pair', 0, 0, tiled=True)  6.98 us
    ppermute x3, starting transfers between devices, local(): lax.ppermute(sends[k], 'row', row_moves(k, 0))  5.06 us
    all_to_all x1, starting transfers between devices, local(): routed = lax.all_to_all(wanted, 'pair', 0, 0, tiled=True)  4 us
    unnamed x10, local copies, waits for them, and re-layouts  2.45 us
    ppermute x1, starting transfers between devices, local(): lax.ppermute(far, 'row', [(2 * y + c, 2 * (CHIPS - 1 - y) + c) for y in r...  2.36 us
  transfers between devices with their start and end apart: 10, of which 5 were waited for; matrix products, arithmetic and copies ran while one was open for 3% of the time, Pallas kernels for 0%

profile of v5, /device:TPU:1, one launch (start us, length us, event | category | flops | bytes accessed | tf_op | source)
XLA Modules:
  0.0 64.5 jit_solution(13409240493242764116)
XLA Ops:
  0.0 1.7 %shard_map.73 = (bf16[32,16,128]{2,1,0:T(8,128)(2,1)}, s32[128]{0:T(128)}) custom-call(s32[64]{0:T(128)} %src_hbm.1, s32[64]{0:T(128)} %tgt_hbm.1, s32[64]{0:T(128)} %slot_hbm.1, bf16[2,1,32,1024]{3,2,1,0:T(8,128)(2,1)} %own_hbm.1), custom_call_target="tpu_custom_call" | custom-call | tf_op jit(solution)/shard_map/pallas_call | solution.py:298
  1.7 21.2 %all_to_all.10.held_ref = bf16[32,16,128]{2,1,0:T(8,128)(2,1)S(1)} all-to-all(bf16[32,16,128]{2,1,0:T(8,128)(2,1)} %get-tuple-element.24), channel_id=1, replica_groups=mesh['pair'=32,'row'=8] {'pair'}, dimensions={0} | all-to-all | bytes 262144 | tf_op jit(solution)/shard_map/all_to_all | solution.py:311
  23.0 0.0 copy-start
  23.0 0.7 %copy-done = s32[128]{0:T(128)S(1)} copy-done((s32[128]{0:T(128)S(1)}, s32[128]{0:T(128)}, u32[]{:S(2)}) %copy-start) | copy-done | bytes 536
  23.6 1.4 %shard_map.74 = bf16[32,2,16,128]{3,2,1,0:T(8,128)(2,1)} custom-call(s32[128]{0:T(128)S(1)} %copy-done, bf16[32,16,128]{2,1,0:T(8,128)(2,1)S(1)} %all_to_all.10.held_ref), custom_call_target="tpu_custom_call" | custom-call | tf_op jit(solution)/shard_map/pallas_call | solution.py:39
  25.0 0.0 copy-start.1
  25.0 4.0 %all-to-all-start.1 = ((bf16[32,2,16,128]{3,2,1,0:T(8,128)(2,1)}), bf16[32,2,16,128]{3,2,1,0:T(8,128)(2,1)S(1)}, u32[]{:S(2)}, u32[]{:S(2)}) async-start(bf16[32,2,16,128]{3,2,1,0:T(8,128)(2,1)} %shard_map.74), calls=%async_computation.1 | async-start | bytes 524288 | tf_op jit(solution)/shard_map/all_to_all | solution.py:320
  29.0 0.0 copy-done.1
  29.0 0.3 copy.13
  29.3 0.2 copy.21
  29.5 0.2 pad.22.clone
  29.8 0.4 reshape.32
  30.2 0.0 copy-start.2
  30.2 0.7 %copy-done.2 = bf16[81,16,1]{0,1,2:T(8,128)(2,1)S(1)} copy-done((bf16[81,16,1]{0,1,2:T(8,128)(2,1)S(1)}, bf16[81,16,1]{0,1,2:T(8,128)(2,1)}, u32[]{:S(2)}) %copy-start.2) | copy-done | bytes 2616
  30.9 0.1 copy.11
  31.0 0.3 copy.20
  31.3 0.2 pad.20.clone
  31.5 0.1 reshape.27
  31.6 0.0 copy-start.3
  31.6 0.7 %copy-done.3 = bf16[81,1,16]{0,2,1:T(8,128)(2,1)S(1)} copy-done((bf16[81,1,16]{0,2,1:T(8,128)(2,1)S(1)}, bf16[81,1,16]{0,2,1:T(8,128)(2,1)}, u32[]{:S(2)}) %copy-start.3) | copy-done | bytes 2616
  32.3 0.1 copy.16
  32.5 0.1 reshape.31
  32.6 7.0 %all-to-all-done.1.held_ref = bf16[32,2,16,128]{3,2,1,0:T(8,128)(2,1)S(1)} async-done(((bf16[32,2,16,128]{3,2,1,0:T(8,128)(2,1)}), bf16[32,2,16,128]{3,2,1,0:T(8,128)(2,1)S(1)}, u32[]{:S(2)}, u32[]{:S(2)}) %all-to-all-start.1) | async-done | bytes 262176 | tf_op jit(solution)/shard_map/all_to_all | solution.py:320
  39.6 1.4 %collective-permute-start = (bf16[32,16,128]{2,1,0:T(8,128)(2,1)S(1)}, bf16[32,16,128]{2,1,0:T(8,128)(2,1)S(1)}, u32[]{:S(2)}, u32[]{:S(2)}) collective-permute-start(bf16[32,16,128]{2,1,0:T(8,128)(2,1)S(1)} %get-tuple-element.31), channel_id=1, source_target_pairs={{0,2},{1,3},{2,4},{3,5},{4,6},{5,7},{6,0},{7,1},{8,10},{9,11},{10,... | collective-permute-start | bytes 393224 | tf_op jit(solution)/shard_map/ppermute | solution.py:332
  41.0 2.6 %collective-permute-start.1 = (bf16[32,16,128]{2,1,0:T(8,128)(2,1)S(1)}, bf16[32,16,128]{2,1,0:T(8,128)(2,1)S(1)}, u32[]{:S(2)}, u32[]{:S(2)}) collective-permute-start(bf16[32,16,128]{2,1,0:T(8,128)(2,1)S(1)} %get-tuple-element.32), channel_id=1, source_target_pairs={{0,4},{1,5},{2,6},{3,7},{4,0},{5,1},{6,2},{7,3},{8,12},{9,13},{10,... | collective-permute-start | bytes 393224 | tf_op jit(solution)/shard_map/ppermute | solution.py:332
  43.6 1.1 %collective-permute-start.2 = (bf16[32,16,128]{2,1,0:T(8,128)(2,1)S(1)}, bf16[32,16,128]{2,1,0:T(8,128)(2,1)S(1)}, u32[]{:S(2)}, u32[]{:S(2)}) collective-permute-start(bf16[32,16,128]{2,1,0:T(8,128)(2,1)S(1)} %get-tuple-element.33), channel_id=1, source_target_pairs={{0,6},{1,7},{2,0},{3,1},{4,2},{5,3},{6,4},{7,5},{8,14},{9,15},{10,... | collective-permute-start | bytes 393224 | tf_op jit(solution)/shard_map/ppermute | solution.py:332
  44.7 4.3 %collective-permute-start.3 = (bf16[32,16,128]{2,1,0:T(8,128)(2,1)S(1)}, bf16[32,16,128]{2,1,0:T(8,128)(2,1)S(1)}, u32[]{:S(2)}, u32[]{:S(2)}) collective-permute-start(bf16[32,16,128]{2,1,0:T(8,128)(2,1)S(1)} %get-tuple-element.30.own_0), channel_id=1, source_target_pairs={{0,1},{1,0},{2,3},{3,2},{4,5},{5,4},{6,7},{7,6},{8,9},{9,8},{10,11... | collective-permute-start | bytes 393224 | tf_op jit(solution)/shard_map/ppermute | solution.py:333
  49.0 0.0 collective-permute-done.own_1
  49.0 0.4 collective-permute-start.4
  49.5 0.0 collective-permute-done.1.own_2
  49.5 2.5 %collective-permute-start.5 = (bf16[32,16,128]{2,1,0:T(8,128)(2,1)S(1)}, bf16[32,16,128]{2,1,0:T(8,128)(2,1)S(1)}, u32[]{:S(2)}, u32[]{:S(2)}) collective-permute-start(bf16[32,16,128]{2,1,0:T(8,128)(2,1)S(1)} %collective-permute-done.1.own_2), channel_id=1, source_target_pairs={{0,1},{1,0},{2,3},{3,2},{4,5},{5,4},{6,7},{7,6},{8,9},{9,8},{10,11... | collective-permute-start | bytes 393224 | tf_op jit(solution)/shard_map/ppermute | solution.py:333
  52.0 0.0 collective-permute-done.2.own_3
  52.0 0.6 collective-permute-start.6
  52.6 0.0 collective-permute-done.3.oth_0
  52.6 0.0 collective-permute-done.4.oth_1
  52.6 0.4 collective-permute-done.5.oth_2
  53.0 0.6 collective-permute-done.6.oth_3
  53.6 5.1 %shard_map.76 = (bf16[3,16,256]{2,1,0:T(8,128)(2,1)S(1)}, bf16[3,16,256]{2,1,0:T(8,128)(2,1)S(1)}) custom-call(s32[1]{0:T(128)} %bitcast.chip_ref, s32[1]{0:T(128)} %bitcast.1.core_ref, bf16[32,16,128]{2,1,0:T(8,128)(2,1)S(1)} %get-tuple-element.30.own_0, bf16[32,16,128]{2,1,0:T(8,128)(2,1)S(1)} %collective-permute-done.own_1, ...), custom_call_target="tpu_custom_call" | custom-call | tf_op jit(solution)/shard_map/pallas_call | solution.py:39
  58.7 0.4 collective-permute-start.7
  59.1 0.8 %collective-permute-done.7.got_ref = bf16[3,16,256]{2,1,0:T(8,128)(2,1)S(1)} collective-permute-done((bf16[3,16,256]{2,1,0:T(8,128)(2,1)S(1)}, bf16[3,16,256]{2,1,0:T(8,128)(2,1)S(1)}, u32[]{:S(2)}, u32[]{:S(2)}) %collective-permute-start.7) | collective-permute-done | bytes 24608 | tf_op jit(solution)/shard_map/ppermute | solution.py:342
  60.0 2.4 %collective-permute-start.8 = (bf16[2,16,256]{2,1,0:T(8,128)(2,1)S(1)}, bf16[2,16,256]{2,1,0:T(8,128)(2,1)S(1)}, u32[]{:S(2)}, u32[]{:S(2)}) collective-permute-start(bf16[2,16,256]{2,1,0:T(8,128)(2,1)S(1)} %get-tuple-element.40), channel_id=1, source_target_pairs={{0,6},{1,7},{2,4},{3,5},{4,2},{5,3},{6,0},{7,1},{8,14},{9,15},{10,... | collective-permute-start | bytes 49160 | tf_op jit(solution)/shard_map/ppermute | solution.py:345
  62.4 1.5 %collective-permute-done.8.far_ref = bf16[2,16,256]{2,1,0:T(8,128)(2,1)S(1)} collective-permute-done((bf16[2,16,256]{2,1,0:T(8,128)(2,1)S(1)}, bf16[2,16,256]{2,1,0:T(8,128)(2,1)S(1)}, u32[]{:S(2)}, u32[]{:S(2)}) %collective-permute-start.8) | collective-permute-done | bytes 16416 | tf_op jit(solution)/shard_map/ppermute | solution.py:345
  63.9 0.6 shard_map.78
  (8 shorter events, 0.2 us)
Async XLA Ops:
  23.0 0.7 %copy-start = (s32[128]{0:T(128)S(1)}, s32[128]{0:T(128)}, u32[]{:S(2)}) copy-start(s32[128]{0:T(128)} %get-tuple-element.23.slots_ref) | copy-start | bytes 1540
  25.0 4.0 %copy-start.1 = (bf16[81,16,16]{0,2,1:T(8,128)(2,1)S(1)}, bf16[81,16,16]{0,2,1:T(8,128)(2,1)}, u32[]{:S(2)}) copy-start(bf16[81,16,16]{0,2,1:T(8,128)(2,1)} %param.12) | copy-start | bytes 124420
  25.0 14.6 %all-to-all-start.1 = ((bf16[32,2,16,128]{3,2,1,0:T(8,128)(2,1)}), bf16[32,2,16,128]{3,2,1,0:T(8,128)(2,1)S(1)}, u32[]{:S(2)}, u32[]{:S(2)}) async-start(bf16[32,2,16,128]{3,2,1,0:T(8,128)(2,1)} %shard_map.74), calls=%async_computation.1 | async-start | bytes 524288 | tf_op jit(solution)/shard_map/all_to_all | solution.py:320
  30.2 0.7 %copy-start.2 = (bf16[81,16,1]{0,1,2:T(8,128)(2,1)S(1)}, bf16[81,16,1]{0,1,2:T(8,128)(2,1)}, u32[]{:S(2)}) copy-start(bf16[81,16,1]{0,1,2:T(8,128)(2,1)} %param.11) | copy-start | bytes 7780
  31.6 0.7 %copy-start.3 = (bf16[81,1,16]{0,2,1:T(8,128)(2,1)S(1)}, bf16[81,1,16]{0,2,1:T(8,128)(2,1)}, u32[]{:S(2)}) copy-start(bf16[81,1,16]{0,2,1:T(8,128)(2,1)} %param.13) | copy-start | bytes 7780
  39.6 9.4 %collective-permute-start = (bf16[32,16,128]{2,1,0:T(8,128)(2,1)S(1)}, bf16[32,16,128]{2,1,0:T(8,128)(2,1)S(1)}, u32[]{:S(2)}, u32[]{:S(2)}) collective-permute-start(bf16[32,16,128]{2,1,0:T(8,128)(2,1)S(1)} %get-tuple-element.31), channel_id=1, source_target_pairs={{0,2},{1,3},{2,4},{3,5},{4,6},{5,7},{6,0},{7,1},{8,10},{9,11},{10,... | collective-permute-start | bytes 393224 | tf_op jit(solution)/shard_map/ppermute | solution.py:332
  41.0 8.5 %collective-permute-start.1 = (bf16[32,16,128]{2,1,0:T(8,128)(2,1)S(1)}, bf16[32,16,128]{2,1,0:T(8,128)(2,1)S(1)}, u32[]{:S(2)}, u32[]{:S(2)}) collective-permute-start(bf16[32,16,128]{2,1,0:T(8,128)(2,1)S(1)} %get-tuple-element.32), channel_id=1, source_target_pairs={{0,4},{1,5},{2,6},{3,7},{4,0},{5,1},{6,2},{7,3},{8,12},{9,13},{10,... | collective-permute-start | bytes 393224 | tf_op jit(solution)/shard_map/ppermute | solution.py:332
  43.6 8.4 %collective-permute-start.2 = (bf16[32,16,128]{2,1,0:T(8,128)(2,1)S(1)}, bf16[32,16,128]{2,1,0:T(8,128)(2,1)S(1)}, u32[]{:S(2)}, u32[]{:S(2)}) collective-permute-start(bf16[32,16,128]{2,1,0:T(8,128)(2,1)S(1)} %get-tuple-element.33), channel_id=1, source_target_pairs={{0,6},{1,7},{2,0},{3,1},{4,2},{5,3},{6,4},{7,5},{8,14},{9,15},{10,... | collective-permute-start | bytes 393224 | tf_op jit(solution)/shard_map/ppermute | solution.py:332
  44.7 8.0 %collective-permute-start.3 = (bf16[32,16,128]{2,1,0:T(8,128)(2,1)S(1)}, bf16[32,16,128]{2,1,0:T(8,128)(2,1)S(1)}, u32[]{:S(2)}, u32[]{:S(2)}) collective-permute-start(bf16[32,16,128]{2,1,0:T(8,128)(2,1)S(1)} %get-tuple-element.30.own_0), channel_id=1, source_target_pairs={{0,1},{1,0},{2,3},{3,2},{4,5},{5,4},{6,7},{7,6},{8,9},{9,8},{10,11... | collective-permute-start | bytes 393224 | tf_op jit(solution)/shard_map/ppermute | solution.py:333
  49.0 3.6 %collective-permute-start.4 = (bf16[32,16,128]{2,1,0:T(8,128)(2,1)S(1)}, bf16[32,16,128]{2,1,0:T(8,128)(2,1)S(1)}, u32[]{:S(2)}, u32[]{:S(2)}) collective-permute-start(bf16[32,16,128]{2,1,0:T(8,128)(2,1)S(1)} %collective-permute-done.own_1), channel_id=1, source_target_pairs={{0,1},{1,0},{2,3},{3,2},{4,5},{5,4},{6,7},{7,6},{8,9},{9,8},{10,11... | collective-permute-start | bytes 393224 | tf_op jit(solution)/shard_map/ppermute | solution.py:333
  49.5 3.5 %collective-permute-start.5 = (bf16[32,16,128]{2,1,0:T(8,128)(2,1)S(1)}, bf16[32,16,128]{2,1,0:T(8,128)(2,1)S(1)}, u32[]{:S(2)}, u32[]{:S(2)}) collective-permute-start(bf16[32,16,128]{2,1,0:T(8,128)(2,1)S(1)} %collective-permute-done.1.own_2), channel_id=1, source_target_pairs={{0,1},{1,0},{2,3},{3,2},{4,5},{5,4},{6,7},{7,6},{8,9},{9,8},{10,11... | collective-permute-start | bytes 393224 | tf_op jit(solution)/shard_map/ppermute | solution.py:333
  52.0 1.6 %collective-permute-start.6 = (bf16[32,16,128]{2,1,0:T(8,128)(2,1)S(1)}, bf16[32,16,128]{2,1,0:T(8,128)(2,1)S(1)}, u32[]{:S(2)}, u32[]{:S(2)}) collective-permute-start(bf16[32,16,128]{2,1,0:T(8,128)(2,1)S(1)} %collective-permute-done.2.own_3), channel_id=1, source_target_pairs={{0,1},{1,0},{2,3},{3,2},{4,5},{5,4},{6,7},{7,6},{8,9},{9,8},{10,11... | collective-permute-start | bytes 393224 | tf_op jit(solution)/shard_map/ppermute | solution.py:333
  58.7 1.3 %collective-permute-start.7 = (bf16[3,16,256]{2,1,0:T(8,128)(2,1)S(1)}, bf16[3,16,256]{2,1,0:T(8,128)(2,1)S(1)}, u32[]{:S(2)}, u32[]{:S(2)}) collective-permute-start(bf16[3,16,256]{2,1,0:T(8,128)(2,1)S(1)} %get-tuple-element.38), channel_id=1, source_target_pairs={{0,1},{1,0},{2,3},{3,2},{4,5},{5,4},{6,7},{7,6},{8,9},{9,8},{10,11... | collective-permute-start | bytes 73736 | tf_op jit(solution)/shard_map/ppermute | solution.py:342
  60.0 3.9 %collective-permute-start.8 = (bf16[2,16,256]{2,1,0:T(8,128)(2,1)S(1)}, bf16[2,16,256]{2,1,0:T(8,128)(2,1)S(1)}, u32[]{:S(2)}, u32[]{:S(2)}) collective-permute-start(bf16[2,16,256]{2,1,0:T(8,128)(2,1)S(1)} %get-tuple-element.40), channel_id=1, source_target_pairs={{0,6},{1,7},{2,4},{3,5},{4,2},{5,3},{6,0},{7,1},{8,14},{9,15},{10,... | collective-permute-start | bytes 49160 | tf_op jit(solution)/shard_map/ppermute | solution.py:345

commit v6 on v4

--- a/solution.py
+++ b/solution.py
@@ -282,6 +282,27 @@
     chip = (place // 2).reshape(1)
     core = (place % 2).reshape(1)
 
+    tiles = call(spread_kernel, jax.ShapeDtypeStruct((groups, 16, 128), BF16), (features,))
+    slots = call(
+        slots_kernel,
+        jax.ShapeDtypeStruct((2 * src_ids.shape[0],), jnp.int32),
+        (),
+        (src_ids, tgt_ids, image_slot),
+        out_specs=whole(pltpu.SMEM),
+    )
+    held = lax.all_to_all(tiles, "pair", 0, 0, tiled=True)
+    held, chip, core = lax.optimization_barrier((held, chip, core))
+    wanted = call(
+        select_kernel,
+        jax.ShapeDtypeStruct((groups, 2, 16, 128), BF16),
+        (held,),
+        (slots,),
+        (pltpu.VMEM((2 * groups, 8, 128), F32),),
+    )
+    routed = lax.all_to_all(wanted, "pair", 0, 0, tiled=True)
+    routed, w_first, w_mid, w_last = lax.optimization_barrier((routed, w_first, w_mid, w_last))
+    sends = call(pack_kernel, (jax.ShapeDtypeStruct((groups, 16, 128), BF16),) * 4, (routed,), (chip,))
+    own = [sends[0]] + [lax.ppermute(sends[k], "row", row_moves(k, 0)) for k in range(1, CHIPS)]
     taps = w_first.reshape(3, 3, 3, 3, CONV).transpose(4, 2, 3, 0, 1)
     z1 = jnp.pad(taps, ((0, 0),) * 4 + ((1, COLS_IN - 4),)).reshape(CONV, K_1)
     z1 = jnp.pad(z1, ((0, 0), (0, 512 - K_1)))
@@ -290,27 +311,7 @@
     z2 = jnp.pad(z2, ((0, 0), (0, 256 - K_2)))
     z3 = w_last.reshape(3, 3, 3, 3, CONV).transpose(0, 2, 3, 1, 4).reshape(27, 3 * CONV)
     z3 = jnp.pad(z3, ((0, 0), (0, 256 - 3 * CONV)))
-
-    tiles = call(spread_kernel, jax.ShapeDtypeStruct((groups, 16, 128), BF16), (features,))
-    slots = call(
-        slots_kernel,
-        jax.ShapeDtypeStruct((2 * src_ids.shape[0],), jnp.int32),
-        (),
-        (src_ids, tgt_ids, image_slot),
-        out_specs=whole(pltpu.SMEM),
-    )
-    held = lax.all_to_all(tiles, "pair", 0, 0, tiled=True)
-    wanted = call(
-        select_kernel,
-        jax.ShapeDtypeStruct((groups, 2, 16, 128), BF16),
-        (held,),
-        (slots,),
-        (pltpu.VMEM((2 * groups, 8, 128), F32),),
-    )
-    routed = lax.all_to_all(wanted, "pair", 0, 0, tiled=True)
-    routed, z1, z2, z3 = lax.optimization_barrier((routed, z1, z2, z3))
-    sends = call(pack_kernel, (jax.ShapeDtypeStruct((groups, 16, 128), BF16),) * 4, (routed,), (chip,))
-    own = [sends[0]] + [lax.ppermute(sends[k], "row", row_moves(k, 0)) for k in range(1, CHIPS)]
+    own[1], z1, z2, z3 = lax.optimization_barrier((own[1], z1, z2, z3))
     other = [lax.ppermute(block, "row", row_moves(0, 1)) for block in own]
     message = jax.ShapeDtypeStruct((3, 16, POS), BF16)
     keep, give = call(

time: 64.2 us -> 63.7 us (level)
  blocking collectives: 0 us -> 13.7 us
  starting transfers between devices: 31.8 us -> 24.2 us
  waiting for transfers between devices: 18.4 us -> 11.8 us
  Pallas kernels: 9.14 us -> 8.45 us
  local copies, waits for them, and re-layouts: 4.4 us -> 5.05 us
    all_to_all x0 -> x1, blocking collectives: none -> 13.7 us  [local(): routed = lax.all_to_all(wanted, 'pair', 0, 0, tiled=True)]
    all_to_all x1 -> x0, waiting for transfers between devices: 6.97 us -> none  [local(): routed = lax.all_to_all(wanted, 'pair', 0, 0, tiled=True)]
    all_to_all x1 -> x0, starting transfers between devices: 4 us -> none  [local(): routed = lax.all_to_all(wanted, 'pair', 0, 0, tiled=True)]
    ppermute x4, starting transfers between devices: 7.94 us -> 5.47 us  [local(): other = [lax.ppermute(block, 'row', row_moves(0, 1)) for block in own]]
    ppermute x1, waiting for transfers between devices: 1.52 us -> 2.43 us  [local(): lax.ppermute(far, 'row', [(2 * y + c, 2 * (CHIPS - 1 - y) + c) for y in r...]
    ppermute x1, starting transfers between devices: 2.37 us -> 1.45 us  [local(): lax.ppermute(far, 'row', [(2 * y + c, 2 * (CHIPS - 1 - y) + c) for y in r...]
    pallas_call x7, Pallas kernels: 9.14 us -> 8.45 us  [call(): pl.pallas_call(kernel, out_shape=out_shape, in_specs=[whole(pltpu.SMEM)]...]
    all_to_all x1, waiting for transfers between devices: 8.02 us -> 7.35 us  [local(): held = lax.all_to_all(tiles, 'pair', 0, 0, tiled=True)]
  transfers between devices with their start and end apart: 11 -> 10, of which waited for: 6 -> 7; matrix products, arithmetic and copies ran while one was open for 3% -> 3% of each run, Pallas kernels for 2% -> 2%
where the time goes in v6:
time: 63.7 us; the launch traced here: 63.4 us
  starting transfers between devices  24.2 us (38%)
  blocking collectives  13.7 us (22%)
  waiting for transfers between devices  11.8 us (19%)
  Pallas kernels  8.45 us (13%)
  local copies, waits for them, and re-layouts  5.05 us (8%)
    all_to_all x1, blocking collectives, local(): routed = lax.all_to_all(wanted, 'pair', 0, 0, tiled=True)  13.7 us
    all_to_all x1, starting transfers between devices, local(): held = lax.all_to_all(tiles, 'pair', 0, 0, tiled=True)  11.9 us
    pallas_call x7, Pallas kernels, call(): pl.pallas_call(kernel, out_shape=out_shape, in_specs=[whole(pltpu.SMEM)]...  8.45 us
    all_to_all x1, waiting for transfers between devices, local(): held = lax.all_to_all(tiles, 'pair', 0, 0, tiled=True)  7.35 us
    ppermute x4, starting transfers between devices, local(): other = [lax.ppermute(block, 'row', row_moves(0, 1)) for block in own]  5.47 us
    ppermute x3, starting transfers between devices, local(): lax.ppermute(sends[k], 'row', row_moves(k, 0))  5.06 us
    unnamed x16, local copies, waits for them, and re-layouts  3.36 us
    ppermute x1, waiting for transfers between devices, local(): lax.ppermute(far, 'row', [(2 * y + c, 2 * (CHIPS - 1 - y) + c) for y in r...  2.43 us
  transfers between devices with their start and end apart: 10, of which 7 were waited for; matrix products, arithmetic and copies ran while one was open for 3% of the time, Pallas kernels for 2%

profile of v6, /device:TPU:1, one launch (start us, length us, event | category | flops | bytes accessed | tf_op | source)
XLA Modules:
  0.0 63.4 jit_solution(14114528799603774457)
XLA Ops:
  0.0 0.9 %copy-done = bf16[2,1,32,1024]{3,2,1,0:T(8,128)(2,1)S(1)} copy-done((bf16[2,1,32,1024]{3,2,1,0:T(8,128)(2,1)S(1)}, bf16[2,1,32,1024]{3,2,1,0:T(8,128)(2,1)}, u32[]{:S(2)}) %copy-start) | copy-done | bytes 131096
  0.9 0.8 %shard_map.73 = bf16[32,16,128]{2,1,0:T(8,128)(2,1)} custom-call(bf16[2,1,32,1024]{3,2,1,0:T(8,128)(2,1)S(1)} %copy-done), custom_call_target="tpu_custom_call" | custom-call | tf_op jit(solution)/shard_map/pallas_call | solution.py:39
  1.7 11.9 %all-to-all-start = ((bf16[32,16,128]{2,1,0:T(8,128)(2,1)}), bf16[32,16,128]{2,1,0:T(8,128)(2,1)S(1)}, u32[]{:S(2)}, u32[]{:S(2)}) async-start(bf16[32,16,128]{2,1,0:T(8,128)(2,1)} %shard_map.73), calls=%async_computation | async-start | bytes 262144 | tf_op jit(solution)/shard_map/all_to_all | solution.py:293
  13.6 0.0 copy-start.1
  13.6 0.0 copy-start.2
  13.6 0.0 copy-start.3
  13.6 0.6 copy-done.1
  14.2 0.0 copy-done.2
  14.2 0.0 copy-done.3
  14.3 1.3 %shard_map.74.slots_ref = s32[128]{0:T(128)S(1)} custom-call(s32[64]{0:T(128)S(1)} %copy-done.1, s32[64]{0:T(128)S(1)} %copy-done.2, s32[64]{0:T(128)S(1)} %copy-done.3), custom_call_target="tpu_custom_call" | custom-call | tf_op jit(solution)/shard_map/pallas_call | solution.py:39
  15.5 7.3 %all-to-all-done.held_ref = bf16[32,16,128]{2,1,0:T(8,128)(2,1)S(1)} async-done(((bf16[32,16,128]{2,1,0:T(8,128)(2,1)}), bf16[32,16,128]{2,1,0:T(8,128)(2,1)S(1)}, u32[]{:S(2)}, u32[]{:S(2)}) %all-to-all-start) | async-done | bytes 131104 | tf_op jit(solution)/shard_map/all_to_all | solution.py:293
  22.9 0.7 %shard_map.75 = bf16[32,2,16,128]{3,2,1,0:T(8,128)(2,1)S(1)} custom-call(s32[128]{0:T(128)S(1)} %shard_map.74.slots_ref, bf16[32,16,128]{2,1,0:T(8,128)(2,1)S(1)} %all-to-all-done.held_ref), custom_call_target="tpu_custom_call" | custom-call | tf_op jit(solution)/shard_map/pallas_call | solution.py:39
  23.6 13.7 %all_to_all.10.held_ref = bf16[32,2,16,128]{3,2,1,0:T(8,128)(2,1)S(1)} all-to-all(bf16[32,2,16,128]{3,2,1,0:T(8,128)(2,1)S(1)} %shard_map.75), channel_id=1, replica_groups=mesh['pair'=32,'row'=8] {'pair'}, dimensions={0} | all-to-all | bytes 524288 | tf_op jit(solution)/shard_map/all_to_all | solution.py:302
  37.3 1.4 %collective-permute-start = (bf16[32,16,128]{2,1,0:T(8,128)(2,1)S(1)}, bf16[32,16,128]{2,1,0:T(8,128)(2,1)S(1)}, u32[]{:S(2)}, u32[]{:S(2)}) collective-permute-start(bf16[32,16,128]{2,1,0:T(8,128)(2,1)S(1)} %get-tuple-element.29), channel_id=1, source_target_pairs={{0,2},{1,3},{2,4},{3,5},{4,6},{5,7},{6,0},{7,1},{8,10},{9,11},{10,... | collective-permute-start | bytes 393224 | tf_op jit(solution)/shard_map/ppermute | solution.py:305
  38.7 2.6 %collective-permute-start.1 = (bf16[32,16,128]{2,1,0:T(8,128)(2,1)S(1)}, bf16[32,16,128]{2,1,0:T(8,128)(2,1)S(1)}, u32[]{:S(2)}, u32[]{:S(2)}) collective-permute-start(bf16[32,16,128]{2,1,0:T(8,128)(2,1)S(1)} %get-tuple-element.34), channel_id=1, source_target_pairs={{0,4},{1,5},{2,6},{3,7},{4,0},{5,1},{6,2},{7,3},{8,12},{9,13},{10,... | collective-permute-start | bytes 393224 | tf_op jit(solution)/shard_map/ppermute | solution.py:305
  41.3 1.1 %collective-permute-start.2 = (bf16[32,16,128]{2,1,0:T(8,128)(2,1)S(1)}, bf16[32,16,128]{2,1,0:T(8,128)(2,1)S(1)}, u32[]{:S(2)}, u32[]{:S(2)}) collective-permute-start(bf16[32,16,128]{2,1,0:T(8,128)(2,1)S(1)} %get-tuple-element.35), channel_id=1, source_target_pairs={{0,6},{1,7},{2,0},{3,1},{4,2},{5,3},{6,4},{7,5},{8,14},{9,15},{10,... | collective-permute-start | bytes 393224 | tf_op jit(solution)/shard_map/ppermute | solution.py:305
  42.4 0.0 copy-done.4
  42.4 0.3 copy.13
  42.7 0.2 copy.21
  42.9 0.2 pad.22.clone
  43.1 0.4 reshape.32
  43.5 0.0 copy-start.5
  43.6 0.7 %copy-done.5 = bf16[81,16,1]{0,1,2:T(8,128)(2,1)S(1)} copy-done((bf16[81,16,1]{0,1,2:T(8,128)(2,1)S(1)}, bf16[81,16,1]{0,1,2:T(8,128)(2,1)}, u32[]{:S(2)}) %copy-start.5) | copy-done | bytes 2616
  44.2 0.1 copy.11
  44.4 0.3 copy.20
  44.7 0.2 pad.20.clone
  44.8 0.1 reshape.27
  45.0 0.0 copy-start.6
  45.0 0.7 %copy-done.6 = bf16[81,1,16]{0,2,1:T(8,128)(2,1)S(1)} copy-done((bf16[81,1,16]{0,2,1:T(8,128)(2,1)S(1)}, bf16[81,1,16]{0,2,1:T(8,128)(2,1)}, u32[]{:S(2)}) %copy-start.6) | copy-done | bytes 2616
  45.7 0.1 copy.16
  45.8 0.1 reshape.31
  45.9 4.7 %collective-permute-start.3 = (bf16[32,16,128]{2,1,0:T(8,128)(2,1)S(1)}, bf16[32,16,128]{2,1,0:T(8,128)(2,1)S(1)}, u32[]{:S(2)}, u32[]{:S(2)}) collective-permute-start(bf16[32,16,128]{2,1,0:T(8,128)(2,1)S(1)} %get-tuple-element.28.own_0), channel_id=1, source_target_pairs={{0,1},{1,0},{2,3},{3,2},{4,5},{5,4},{6,7},{7,6},{8,9},{9,8},{10,11... | collective-permute-start | bytes 393224 | tf_op jit(solution)/shard_map/ppermute | solution.py:315
  50.6 0.0 collective-permute-done.own_1
  50.6 0.1 collective-permute-start.4
  50.7 0.0 collective-permute-done.1.own_2
  50.7 0.4 collective-permute-start.5
  51.1 0.0 collective-permute-done.2.own_3
  51.1 0.3 collective-permute-start.6
  51.4 0.2 collective-permute-done.3.oth_0
  51.6 0.4 collective-permute-done.4.oth_1
  52.0 0.2 collective-permute-done.5.oth_2
  52.2 0.3 collective-permute-done.6.oth_3
  52.5 5.1 %shard_map.77 = (bf16[3,16,256]{2,1,0:T(8,128)(2,1)S(1)}, bf16[3,16,256]{2,1,0:T(8,128)(2,1)S(1)}) custom-call(s32[1]{0:T(128)} %bitcast.chip_ref, s32[1]{0:T(128)} %bitcast.1.core_ref, bf16[32,16,128]{2,1,0:T(8,128)(2,1)S(1)} %get-tuple-element.28.own_0, bf16[32,16,128]{2,1,0:T(8,128)(2,1)S(1)} %collective-permute-done.own_1, ...), custom_call_target="tpu_custom_call" | custom-call | tf_op jit(solution)/shard_map/pallas_call | solution.py:39
  57.6 0.4 collective-permute-start.7
  57.9 0.9 %collective-permute-done.7.got_ref = bf16[3,16,256]{2,1,0:T(8,128)(2,1)S(1)} collective-permute-done((bf16[3,16,256]{2,1,0:T(8,128)(2,1)S(1)}, bf16[3,16,256]{2,1,0:T(8,128)(2,1)S(1)}, u32[]{:S(2)}, u32[]{:S(2)}) %collective-permute-start.7) | collective-permute-done | bytes 24608 | tf_op jit(solution)/shard_map/ppermute | solution.py:324
  58.9 1.5 %collective-permute-start.8 = (bf16[2,16,256]{2,1,0:T(8,128)(2,1)S(1)}, bf16[2,16,256]{2,1,0:T(8,128)(2,1)S(1)}, u32[]{:S(2)}, u32[]{:S(2)}) collective-permute-start(bf16[2,16,256]{2,1,0:T(8,128)(2,1)S(1)} %get-tuple-element.42), channel_id=1, source_target_pairs={{0,6},{1,7},{2,4},{3,5},{4,2},{5,3},{6,0},{7,1},{8,14},{9,15},{10,... | collective-permute-start | bytes 49160 | tf_op jit(solution)/shard_map/ppermute | solution.py:327
  60.3 2.4 %collective-permute-done.8.far_ref = bf16[2,16,256]{2,1,0:T(8,128)(2,1)S(1)} collective-permute-done((bf16[2,16,256]{2,1,0:T(8,128)(2,1)S(1)}, bf16[2,16,256]{2,1,0:T(8,128)(2,1)S(1)}, u32[]{:S(2)}, u32[]{:S(2)}) %collective-permute-start.8) | collective-permute-done | bytes 16416 | tf_op jit(solution)/shard_map/ppermute | solution.py:327
  62.8 0.6 shard_map.79
  (10 shorter events, 0.2 us)
Async XLA Ops:
  0.0 0.9 %copy-start = (bf16[2,1,32,1024]{3,2,1,0:T(8,128)(2,1)S(1)}, bf16[2,1,32,1024]{3,2,1,0:T(8,128)(2,1)}, u32[]{:S(2)}) copy-start(bf16[2,1,32,1024]{3,2,1,0:T(8,128)(2,1)} %own_ref.1) | copy-start | bytes 393220
  1.7 21.2 %all-to-all-start = ((bf16[32,16,128]{2,1,0:T(8,128)(2,1)}), bf16[32,16,128]{2,1,0:T(8,128)(2,1)S(1)}, u32[]{:S(2)}, u32[]{:S(2)}) async-start(bf16[32,16,128]{2,1,0:T(8,128)(2,1)} %shard_map.73), calls=%async_computation | async-start | bytes 262144 | tf_op jit(solution)/shard_map/all_to_all | solution.py:293
  13.6 0.7 %copy-start.1 = (s32[64]{0:T(128)S(1)}, s32[64]{0:T(128)}, u32[]{:S(2)}) copy-start(s32[64]{0:T(128)} %src_ref.1) | copy-start | bytes 772
  13.6 0.7 %copy-start.2 = (s32[64]{0:T(128)S(1)}, s32[64]{0:T(128)}, u32[]{:S(2)}) copy-start(s32[64]{0:T(128)} %tgt_ref.1) | copy-start | bytes 772
  13.6 0.7 %copy-start.3 = (s32[64]{0:T(128)S(1)}, s32[64]{0:T(128)}, u32[]{:S(2)}) copy-start(s32[64]{0:T(128)} %slot_ref.1) | copy-start | bytes 772
  37.3 5.1 %copy-start.4 = (bf16[81,16,16]{0,2,1:T(8,128)(2,1)S(1)}, bf16[81,16,16]{0,2,1:T(8,128)(2,1)}, u32[]{:S(2)}) copy-start(bf16[81,16,16]{0,2,1:T(8,128)(2,1)} %param.12) | copy-start | bytes 124420
  37.3 13.3 %collective-permute-start = (bf16[32,16,128]{2,1,0:T(8,128)(2,1)S(1)}, bf16[32,16,128]{2,1,0:T(8,128)(2,1)S(1)}, u32[]{:S(2)}, u32[]{:S(2)}) collective-permute-start(bf16[32,16,128]{2,1,0:T(8,128)(2,1)S(1)} %get-tuple-element.29), channel_id=1, source_target_pairs={{0,2},{1,3},{2,4},{3,5},{4,6},{5,7},{6,0},{7,1},{8,10},{9,11},{10,... | collective-permute-start | bytes 393224 | tf_op jit(solution)/shard_map/ppermute | solution.py:305
  38.7 12.1 %collective-permute-start.1 = (bf16[32,16,128]{2,1,0:T(8,128)(2,1)S(1)}, bf16[32,16,128]{2,1,0:T(8,128)(2,1)S(1)}, u32[]{:S(2)}, u32[]{:S(2)}) collective-permute-start(bf16[32,16,128]{2,1,0:T(8,128)(2,1)S(1)} %get-tuple-element.34), channel_id=1, source_target_pairs={{0,4},{1,5},{2,6},{3,7},{4,0},{5,1},{6,2},{7,3},{8,12},{9,13},{10,... | collective-permute-start | bytes 393224 | tf_op jit(solution)/shard_map/ppermute | solution.py:305
  41.3 9.9 %collective-permute-start.2 = (bf16[32,16,128]{2,1,0:T(8,128)(2,1)S(1)}, bf16[32,16,128]{2,1,0:T(8,128)(2,1)S(1)}, u32[]{:S(2)}, u32[]{:S(2)}) collective-permute-start(bf16[32,16,128]{2,1,0:T(8,128)(2,1)S(1)} %get-tuple-element.35), channel_id=1, source_target_pairs={{0,6},{1,7},{2,0},{3,1},{4,2},{5,3},{6,4},{7,5},{8,14},{9,15},{10,... | collective-permute-start | bytes 393224 | tf_op jit(solution)/shard_map/ppermute | solution.py:305
  43.5 0.7 %copy-start.5 = (bf16[81,16,1]{0,1,2:T(8,128)(2,1)S(1)}, bf16[81,16,1]{0,1,2:T(8,128)(2,1)}, u32[]{:S(2)}) copy-start(bf16[81,16,1]{0,1,2:T(8,128)(2,1)} %param.11) | copy-start | bytes 7780
  45.0 0.7 %copy-start.6 = (bf16[81,1,16]{0,2,1:T(8,128)(2,1)S(1)}, bf16[81,1,16]{0,2,1:T(8,128)(2,1)}, u32[]{:S(2)}) copy-start(bf16[81,1,16]{0,2,1:T(8,128)(2,1)} %param.13) | copy-start | bytes 7780
  45.9 5.7 %collective-permute-start.3 = (bf16[32,16,128]{2,1,0:T(8,128)(2,1)S(1)}, bf16[32,16,128]{2,1,0:T(8,128)(2,1)S(1)}, u32[]{:S(2)}, u32[]{:S(2)}) collective-permute-start(bf16[32,16,128]{2,1,0:T(8,128)(2,1)S(1)} %get-tuple-element.28.own_0), channel_id=1, source_target_pairs={{0,1},{1,0},{2,3},{3,2},{4,5},{5,4},{6,7},{7,6},{8,9},{9,8},{10,11... | collective-permute-start | bytes 393224 | tf_op jit(solution)/shard_map/ppermute | solution.py:315
  50.6 1.3 %collective-permute-start.4 = (bf16[32,16,128]{2,1,0:T(8,128)(2,1)S(1)}, bf16[32,16,128]{2,1,0:T(8,128)(2,1)S(1)}, u32[]{:S(2)}, u32[]{:S(2)}) collective-permute-start(bf16[32,16,128]{2,1,0:T(8,128)(2,1)S(1)} %collective-permute-done.own_1), channel_id=1, source_target_pairs={{0,1},{1,0},{2,3},{3,2},{4,5},{5,4},{6,7},{7,6},{8,9},{9,8},{10,11... | collective-permute-start | bytes 393224 | tf_op jit(solution)/shard_map/ppermute | solution.py:315
  50.7 1.4 %collective-permute-start.5 = (bf16[32,16,128]{2,1,0:T(8,128)(2,1)S(1)}, bf16[32,16,128]{2,1,0:T(8,128)(2,1)S(1)}, u32[]{:S(2)}, u32[]{:S(2)}) collective-permute-start(bf16[32,16,128]{2,1,0:T(8,128)(2,1)S(1)} %collective-permute-done.1.own_2), channel_id=1, source_target_pairs={{0,1},{1,0},{2,3},{3,2},{4,5},{5,4},{6,7},{7,6},{8,9},{9,8},{10,11... | collective-permute-start | bytes 393224 | tf_op jit(solution)/shard_map/ppermute | solution.py:315
  51.1 1.3 %collective-permute-start.6 = (bf16[32,16,128]{2,1,0:T(8,128)(2,1)S(1)}, bf16[32,16,128]{2,1,0:T(8,128)(2,1)S(1)}, u32[]{:S(2)}, u32[]{:S(2)}) collective-permute-start(bf16[32,16,128]{2,1,0:T(8,128)(2,1)S(1)} %collective-permute-done.2.own_3), channel_id=1, source_target_pairs={{0,1},{1,0},{2,3},{3,2},{4,5},{5,4},{6,7},{7,6},{8,9},{9,8},{10,11... | collective-permute-start | bytes 393224 | tf_op jit(solution)/shard_map/ppermute | solution.py:315
  57.6 1.3 %collective-permute-start.7 = (bf16[3,16,256]{2,1,0:T(8,128)(2,1)S(1)}, bf16[3,16,256]{2,1,0:T(8,128)(2,1)S(1)}, u32[]{:S(2)}, u32[]{:S(2)}) collective-permute-start(bf16[3,16,256]{2,1,0:T(8,128)(2,1)S(1)} %get-tuple-element.40), channel_id=1, source_target_pairs={{0,1},{1,0},{2,3},{3,2},{4,5},{5,4},{6,7},{7,6},{8,9},{9,8},{10,11... | collective-permute-start | bytes 73736 | tf_op jit(solution)/shard_map/ppermute | solution.py:324
  58.9 3.9 %collective-permute-start.8 = (bf16[2,16,256]{2,1,0:T(8,128)(2,1)S(1)}, bf16[2,16,256]{2,1,0:T(8,128)(2,1)S(1)}, u32[]{:S(2)}, u32[]{:S(2)}) collective-permute-start(bf16[2,16,256]{2,1,0:T(8,128)(2,1)S(1)} %get-tuple-element.42), channel_id=1, source_target_pairs={{0,6},{1,7},{2,4},{3,5},{4,2},{5,3},{6,0},{7,1},{8,14},{9,15},{10,... | collective-permute-start | bytes 49160 | tf_op jit(solution)/shard_map/ppermute | solution.py:327

commit v7 on v6

--- a/solution.py
+++ b/solution.py
@@ -52,7 +52,7 @@
         cells = own_ref[image, 0].astype(F32)
         scale = lax.rsqrt(jnp.sum(cells * cells, axis=-1, keepdims=True) + NORM_EPS)
         rows.append(cells * scale)
-    for part in range(4):
+    for part in range(2):
         for block in range(8):
             at = slice(part * 8, part * 8 + 8), slice(block * 128, block * 128 + 128)
             out_ref[part * 8 + block] = jnp.concatenate([rows[0][at], rows[1][at]], axis=0).astype(BF16)
@@ -282,7 +282,13 @@
     chip = (place // 2).reshape(1)
     core = (place % 2).reshape(1)
 
-    tiles = call(spread_kernel, jax.ShapeDtypeStruct((groups, 16, 128), BF16), (features,))
+    tiles = pl.pallas_call(
+        spread_kernel,
+        grid=(2,),
+        out_shape=jax.ShapeDtypeStruct((groups, 16, 128), BF16),
+        in_specs=[pl.BlockSpec((2, 1, WID // 2, channels), lambda half: (0, 0, half, 0))],
+        out_specs=pl.BlockSpec((16, 16, 128), lambda half: (half, 0, 0)),
+    )(features)
     slots = call(
         slots_kernel,
         jax.ShapeDtypeStruct((2 * src_ids.shape[0],), jnp.int32),

time: 63.7 us -> 63.7 us (level)
  Pallas kernels: 8.45 us -> 9.36 us
  local copies, waits for them, and re-layouts: 5.05 us -> 4.15 us
    pallas_call x0 -> x1, Pallas kernels: none -> 1.68 us  [local(): pl.pallas_call(spread_kernel, grid=(2,), out_shape=jax.ShapeDtypeStruct((...]
    unnamed x16 -> x14, local copies, waits for them, and re-layouts: 3.36 us -> 2.45 us
    pallas_call x7 -> x6, Pallas kernels: 8.45 us -> 7.68 us  [call(): pl.pallas_call(kernel, out_shape=out_shape, in_specs=[whole(pltpu.SMEM)]...]
where the time goes in v7:
time: 63.7 us; the launch traced here: 63.4 us
  starting transfers between devices  24.2 us (38%)
  blocking collectives  13.7 us (22%)
  waiting for transfers between devices  11.8 us (19%)
  Pallas kernels  9.36 us (15%)
  local copies, waits for them, and re-layouts  4.15 us (7%)
    all_to_all x1, blocking collectives, local(): routed = lax.all_to_all(wanted, 'pair', 0, 0, tiled=True)  13.7 us
    all_to_all x1, starting transfers between devices, local(): held = lax.all_to_all(tiles, 'pair', 0, 0, tiled=True)  11.9 us
    pallas_call x6, Pallas kernels, call(): pl.pallas_call(kernel, out_shape=out_shape, in_specs=[whole(pltpu.SMEM)]...  7.68 us
    all_to_all x1, waiting for transfers between devices, local(): held = lax.all_to_all(tiles, 'pair', 0, 0, tiled=True)  7.35 us
    ppermute x4, starting transfers between devices, local(): other = [lax.ppermute(block, 'row', row_moves(0, 1)) for block in own]  5.47 us
    ppermute x3, starting transfers between devices, local(): lax.ppermute(sends[k], 'row', row_moves(k, 0))  5.06 us
    unnamed x14, local copies, waits for them, and re-layouts  2.45 us
    ppermute x1, waiting for transfers between devices, local(): lax.ppermute(far, 'row', [(2 * y + c, 2 * (CHIPS - 1 - y) + c) for y in r...  2.43 us
  transfers between devices with their start and end apart: 10, of which 7 were waited for; matrix products, arithmetic and copies ran while one was open for 3% of the time, Pallas kernels for 2%

profile of v7, /device:TPU:1, one launch (start us, length us, event | category | flops | bytes accessed | tf_op | source)
XLA Modules:
  0.0 63.4 jit_solution(15104096950841158711)
XLA Ops:
  0.0 1.7 %shard_map.73 = bf16[32,16,128]{2,1,0:T(8,128)(2,1)} custom-call(bf16[2,1,32,1024]{3,2,1,0:T(8,128)(2,1)} %own_ref.1), custom_call_target="tpu_custom_call" | custom-call | tf_op jit(solution)/shard_map/pallas_call | solution.py:285
  1.7 11.9 %all-to-all-start = ((bf16[32,16,128]{2,1,0:T(8,128)(2,1)}), bf16[32,16,128]{2,1,0:T(8,128)(2,1)S(1)}, u32[]{:S(2)}, u32[]{:S(2)}) async-start(bf16[32,16,128]{2,1,0:T(8,128)(2,1)} %shard_map.73), calls=%async_computation | async-start | bytes 262144 | tf_op jit(solution)/shard_map/all_to_all | solution.py:299
  13.6 0.0 copy-start
  13.6 0.0 copy-start.1
  13.6 0.0 copy-start.2
  13.6 0.6 copy-done
  14.2 0.0 copy-done.1
  14.2 0.0 copy-done.2
  14.3 1.3 %shard_map.74.slots_ref = s32[128]{0:T(128)S(1)} custom-call(s32[64]{0:T(128)S(1)} %copy-done, s32[64]{0:T(128)S(1)} %copy-done.1, s32[64]{0:T(128)S(1)} %copy-done.2), custom_call_target="tpu_custom_call" | custom-call | tf_op jit(solution)/shard_map/pallas_call | solution.py:39
  15.6 7.3 %all-to-all-done.held_ref = bf16[32,16,128]{2,1,0:T(8,128)(2,1)S(1)} async-done(((bf16[32,16,128]{2,1,0:T(8,128)(2,1)}), bf16[32,16,128]{2,1,0:T(8,128)(2,1)S(1)}, u32[]{:S(2)}, u32[]{:S(2)}) %all-to-all-start) | async-done | bytes 131104 | tf_op jit(solution)/shard_map/all_to_all | solution.py:299
  22.9 0.7 %shard_map.75 = bf16[32,2,16,128]{3,2,1,0:T(8,128)(2,1)S(1)} custom-call(s32[128]{0:T(128)S(1)} %shard_map.74.slots_ref, bf16[32,16,128]{2,1,0:T(8,128)(2,1)S(1)} %all-to-all-done.held_ref), custom_call_target="tpu_custom_call" | custom-call | tf_op jit(solution)/shard_map/pallas_call | solution.py:39
  23.6 13.7 %all_to_all.10.held_ref = bf16[32,2,16,128]{3,2,1,0:T(8,128)(2,1)S(1)} all-to-all(bf16[32,2,16,128]{3,2,1,0:T(8,128)(2,1)S(1)} %shard_map.75), channel_id=1, replica_groups=mesh['pair'=32,'row'=8] {'pair'}, dimensions={0} | all-to-all | bytes 524288 | tf_op jit(solution)/shard_map/all_to_all | solution.py:308
  37.3 0.0 copy-start.3
  37.3 1.4 %collective-permute-start = (bf16[32,16,128]{2,1,0:T(8,128)(2,1)S(1)}, bf16[32,16,128]{2,1,0:T(8,128)(2,1)S(1)}, u32[]{:S(2)}, u32[]{:S(2)}) collective-permute-start(bf16[32,16,128]{2,1,0:T(8,128)(2,1)S(1)} %get-tuple-element.29), channel_id=1, source_target_pairs={{0,2},{1,3},{2,4},{3,5},{4,6},{5,7},{6,0},{7,1},{8,10},{9,11},{10,... | collective-permute-start | bytes 393224 | tf_op jit(solution)/shard_map/ppermute | solution.py:311
  38.7 2.6 %collective-permute-start.1 = (bf16[32,16,128]{2,1,0:T(8,128)(2,1)S(1)}, bf16[32,16,128]{2,1,0:T(8,128)(2,1)S(1)}, u32[]{:S(2)}, u32[]{:S(2)}) collective-permute-start(bf16[32,16,128]{2,1,0:T(8,128)(2,1)S(1)} %get-tuple-element.34), channel_id=1, source_target_pairs={{0,4},{1,5},{2,6},{3,7},{4,0},{5,1},{6,2},{7,3},{8,12},{9,13},{10,... | collective-permute-start | bytes 393224 | tf_op jit(solution)/shard_map/ppermute | solution.py:311
  41.3 1.1 %collective-permute-start.2 = (bf16[32,16,128]{2,1,0:T(8,128)(2,1)S(1)}, bf16[32,16,128]{2,1,0:T(8,128)(2,1)S(1)}, u32[]{:S(2)}, u32[]{:S(2)}) collective-permute-start(bf16[32,16,128]{2,1,0:T(8,128)(2,1)S(1)} %get-tuple-element.35), channel_id=1, source_target_pairs={{0,6},{1,7},{2,0},{3,1},{4,2},{5,3},{6,4},{7,5},{8,14},{9,15},{10,... | collective-permute-start | bytes 393224 | tf_op jit(solution)/shard_map/ppermute | solution.py:311
  42.4 0.0 copy-done.3
  42.4 0.3 copy.13
  42.7 0.2 copy.21
  42.9 0.2 pad.22.clone
  43.1 0.4 reshape.32
  43.6 0.0 copy-start.4
  43.6 0.7 %copy-done.4 = bf16[81,16,1]{0,1,2:T(8,128)(2,1)S(1)} copy-done((bf16[81,16,1]{0,1,2:T(8,128)(2,1)S(1)}, bf16[81,16,1]{0,1,2:T(8,128)(2,1)}, u32[]{:S(2)}) %copy-start.4) | copy-done | bytes 2616
  44.2 0.1 copy.11
  44.4 0.3 copy.20
  44.7 0.2 pad.20.clone
  44.8 0.1 reshape.27
  45.0 0.0 copy-start.5
  45.0 0.7 %copy-done.5 = bf16[81,1,16]{0,2,1:T(8,128)(2,1)S(1)} copy-done((bf16[81,1,16]{0,2,1:T(8,128)(2,1)S(1)}, bf16[81,1,16]{0,2,1:T(8,128)(2,1)}, u32[]{:S(2)}) %copy-start.5) | copy-done | bytes 2616
  45.7 0.1 copy.16
  45.8 0.1 reshape.31
  45.9 4.7 %collective-permute-start.3 = (bf16[32,16,128]{2,1,0:T(8,128)(2,1)S(1)}, bf16[32,16,128]{2,1,0:T(8,128)(2,1)S(1)}, u32[]{:S(2)}, u32[]{:S(2)}) collective-permute-start(bf16[32,16,128]{2,1,0:T(8,128)(2,1)S(1)} %get-tuple-element.28.own_0), channel_id=1, source_target_pairs={{0,1},{1,0},{2,3},{3,2},{4,5},{5,4},{6,7},{7,6},{8,9},{9,8},{10,11... | collective-permute-start | bytes 393224 | tf_op jit(solution)/shard_map/ppermute | solution.py:321
  50.6 0.0 collective-permute-done.own_1
  50.6 0.1 collective-permute-start.4
  50.7 0.0 collective-permute-done.1.own_2
  50.7 0.4 collective-permute-start.5
  51.1 0.0 collective-permute-done.2.own_3
  51.2 0.3 collective-permute-start.6
  51.4 0.2 collective-permute-done.3.oth_0
  51.6 0.4 collective-permute-done.4.oth_1
  52.0 0.2 collective-permute-done.5.oth_2
  52.2 0.3 collective-permute-done.6.oth_3
  52.5 5.1 %shard_map.77 = (bf16[3,16,256]{2,1,0:T(8,128)(2,1)S(1)}, bf16[3,16,256]{2,1,0:T(8,128)(2,1)S(1)}) custom-call(s32[1]{0:T(128)} %bitcast.chip_ref, s32[1]{0:T(128)} %bitcast.1.core_ref, bf16[32,16,128]{2,1,0:T(8,128)(2,1)S(1)} %get-tuple-element.28.own_0, bf16[32,16,128]{2,1,0:T(8,128)(2,1)S(1)} %collective-permute-done.own_1, ...), custom_call_target="tpu_custom_call" | custom-call | tf_op jit(solution)/shard_map/pallas_call | solution.py:39
  57.6 0.4 collective-permute-start.7
  57.9 0.9 %collective-permute-done.7.got_ref = bf16[3,16,256]{2,1,0:T(8,128)(2,1)S(1)} collective-permute-done((bf16[3,16,256]{2,1,0:T(8,128)(2,1)S(1)}, bf16[3,16,256]{2,1,0:T(8,128)(2,1)S(1)}, u32[]{:S(2)}, u32[]{:S(2)}) %collective-permute-start.7) | collective-permute-done | bytes 24608 | tf_op jit(solution)/shard_map/ppermute | solution.py:330
  58.9 1.5 %collective-permute-start.8 = (bf16[2,16,256]{2,1,0:T(8,128)(2,1)S(1)}, bf16[2,16,256]{2,1,0:T(8,128)(2,1)S(1)}, u32[]{:S(2)}, u32[]{:S(2)}) collective-permute-start(bf16[2,16,256]{2,1,0:T(8,128)(2,1)S(1)} %get-tuple-element.42), channel_id=1, source_target_pairs={{0,6},{1,7},{2,4},{3,5},{4,2},{5,3},{6,0},{7,1},{8,14},{9,15},{10,... | collective-permute-start | bytes 49160 | tf_op jit(solution)/shard_map/ppermute | solution.py:333
  60.3 2.4 %collective-permute-done.8.far_ref = bf16[2,16,256]{2,1,0:T(8,128)(2,1)S(1)} collective-permute-done((bf16[2,16,256]{2,1,0:T(8,128)(2,1)S(1)}, bf16[2,16,256]{2,1,0:T(8,128)(2,1)S(1)}, u32[]{:S(2)}, u32[]{:S(2)}) %collective-permute-start.8) | collective-permute-done | bytes 16416 | tf_op jit(solution)/shard_map/ppermute | solution.py:333
  62.8 0.6 shard_map.79
  (8 shorter events, 0.2 us)
Async XLA Ops:
  1.7 21.2 %all-to-all-start = ((bf16[32,16,128]{2,1,0:T(8,128)(2,1)}), bf16[32,16,128]{2,1,0:T(8,128)(2,1)S(1)}, u32[]{:S(2)}, u32[]{:S(2)}) async-start(bf16[32,16,128]{2,1,0:T(8,128)(2,1)} %shard_map.73), calls=%async_computation | async-start | bytes 262144 | tf_op jit(solution)/shard_map/all_to_all | solution.py:299
  13.6 0.7 %copy-start = (s32[64]{0:T(128)S(1)}, s32[64]{0:T(128)}, u32[]{:S(2)}) copy-start(s32[64]{0:T(128)} %src_ref.1) | copy-start | bytes 772
  13.6 0.7 %copy-start.1 = (s32[64]{0:T(128)S(1)}, s32[64]{0:T(128)}, u32[]{:S(2)}) copy-start(s32[64]{0:T(128)} %tgt_ref.1) | copy-start | bytes 772
  13.6 0.7 %copy-start.2 = (s32[64]{0:T(128)S(1)}, s32[64]{0:T(128)}, u32[]{:S(2)}) copy-start(s32[64]{0:T(128)} %slot_ref.1) | copy-start | bytes 772
  37.3 5.1 %copy-start.3 = (bf16[81,16,16]{0,2,1:T(8,128)(2,1)S(1)}, bf16[81,16,16]{0,2,1:T(8,128)(2,1)}, u32[]{:S(2)}) copy-start(bf16[81,16,16]{0,2,1:T(8,128)(2,1)} %param.12) | copy-start | bytes 124420
  37.3 13.3 %collective-permute-start = (bf16[32,16,128]{2,1,0:T(8,128)(2,1)S(1)}, bf16[32,16,128]{2,1,0:T(8,128)(2,1)S(1)}, u32[]{:S(2)}, u32[]{:S(2)}) collective-permute-start(bf16[32,16,128]{2,1,0:T(8,128)(2,1)S(1)} %get-tuple-element.29), channel_id=1, source_target_pairs={{0,2},{1,3},{2,4},{3,5},{4,6},{5,7},{6,0},{7,1},{8,10},{9,11},{10,... | collective-permute-start | bytes 393224 | tf_op jit(solution)/shard_map/ppermute | solution.py:311
  38.7 12.1 %collective-permute-start.1 = (bf16[32,16,128]{2,1,0:T(8,128)(2,1)S(1)}, bf16[32,16,128]{2,1,0:T(8,128)(2,1)S(1)}, u32[]{:S(2)}, u32[]{:S(2)}) collective-permute-start(bf16[32,16,128]{2,1,0:T(8,128)(2,1)S(1)} %get-tuple-element.34), channel_id=1, source_target_pairs={{0,4},{1,5},{2,6},{3,7},{4,0},{5,1},{6,2},{7,3},{8,12},{9,13},{10,... | collective-permute-start | bytes 393224 | tf_op jit(solution)/shard_map/ppermute | solution.py:311
  41.3 9.9 %collective-permute-start.2 = (bf16[32,16,128]{2,1,0:T(8,128)(2,1)S(1)}, bf16[32,16,128]{2,1,0:T(8,128)(2,1)S(1)}, u32[]{:S(2)}, u32[]{:S(2)}) collective-permute-start(bf16[32,16,128]{2,1,0:T(8,128)(2,1)S(1)} %get-tuple-element.35), channel_id=1, source_target_pairs={{0,6},{1,7},{2,0},{3,1},{4,2},{5,3},{6,4},{7,5},{8,14},{9,15},{10,... | collective-permute-start | bytes 393224 | tf_op jit(solution)/shard_map/ppermute | solution.py:311
  43.6 0.7 %copy-start.4 = (bf16[81,16,1]{0,1,2:T(8,128)(2,1)S(1)}, bf16[81,16,1]{0,1,2:T(8,128)(2,1)}, u32[]{:S(2)}) copy-start(bf16[81,16,1]{0,1,2:T(8,128)(2,1)} %param.11) | copy-start | bytes 7780
  45.0 0.7 %copy-start.5 = (bf16[81,1,16]{0,2,1:T(8,128)(2,1)S(1)}, bf16[81,1,16]{0,2,1:T(8,128)(2,1)}, u32[]{:S(2)}) copy-start(bf16[81,1,16]{0,2,1:T(8,128)(2,1)} %param.13) | copy-start | bytes 7780
  45.9 5.7 %collective-permute-start.3 = (bf16[32,16,128]{2,1,0:T(8,128)(2,1)S(1)}, bf16[32,16,128]{2,1,0:T(8,128)(2,1)S(1)}, u32[]{:S(2)}, u32[]{:S(2)}) collective-permute-start(bf16[32,16,128]{2,1,0:T(8,128)(2,1)S(1)} %get-tuple-element.28.own_0), channel_id=1, source_target_pairs={{0,1},{1,0},{2,3},{3,2},{4,5},{5,4},{6,7},{7,6},{8,9},{9,8},{10,11... | collective-permute-start | bytes 393224 | tf_op jit(solution)/shard_map/ppermute | solution.py:321
  50.6 1.3 %collective-permute-start.4 = (bf16[32,16,128]{2,1,0:T(8,128)(2,1)S(1)}, bf16[32,16,128]{2,1,0:T(8,128)(2,1)S(1)}, u32[]{:S(2)}, u32[]{:S(2)}) collective-permute-start(bf16[32,16,128]{2,1,0:T(8,128)(2,1)S(1)} %collective-permute-done.own_1), channel_id=1, source_target_pairs={{0,1},{1,0},{2,3},{3,2},{4,5},{5,4},{6,7},{7,6},{8,9},{9,8},{10,11... | collective-permute-start | bytes 393224 | tf_op jit(solution)/shard_map/ppermute | solution.py:321
  50.7 1.4 %collective-permute-start.5 = (bf16[32,16,128]{2,1,0:T(8,128)(2,1)S(1)}, bf16[32,16,128]{2,1,0:T(8,128)(2,1)S(1)}, u32[]{:S(2)}, u32[]{:S(2)}) collective-permute-start(bf16[32,16,128]{2,1,0:T(8,128)(2,1)S(1)} %collective-permute-done.1.own_2), channel_id=1, source_target_pairs={{0,1},{1,0},{2,3},{3,2},{4,5},{5,4},{6,7},{7,6},{8,9},{9,8},{10,11... | collective-permute-start | bytes 393224 | tf_op jit(solution)/shard_map/ppermute | solution.py:321
  51.2 1.3 %collective-permute-start.6 = (bf16[32,16,128]{2,1,0:T(8,128)(2,1)S(1)}, bf16[32,16,128]{2,1,0:T(8,128)(2,1)S(1)}, u32[]{:S(2)}, u32[]{:S(2)}) collective-permute-start(bf16[32,16,128]{2,1,0:T(8,128)(2,1)S(1)} %collective-permute-done.2.own_3), channel_id=1, source_target_pairs={{0,1},{1,0},{2,3},{3,2},{4,5},{5,4},{6,7},{7,6},{8,9},{9,8},{10,11... | collective-permute-start | bytes 393224 | tf_op jit(solution)/shard_map/ppermute | solution.py:321
  57.6 1.3 %collective-permute-start.7 = (bf16[3,16,256]{2,1,0:T(8,128)(2,1)S(1)}, bf16[3,16,256]{2,1,0:T(8,128)(2,1)S(1)}, u32[]{:S(2)}, u32[]{:S(2)}) collective-permute-start(bf16[3,16,256]{2,1,0:T(8,128)(2,1)S(1)} %get-tuple-element.40), channel_id=1, source_target_pairs={{0,1},{1,0},{2,3},{3,2},{4,5},{5,4},{6,7},{7,6},{8,9},{9,8},{10,11... | collective-permute-start | bytes 73736 | tf_op jit(solution)/shard_map/ppermute | solution.py:330
  58.9 3.9 %collective-permute-start.8 = (bf16[2,16,256]{2,1,0:T(8,128)(2,1)S(1)}, bf16[2,16,256]{2,1,0:T(8,128)(2,1)S(1)}, u32[]{:S(2)}, u32[]{:S(2)}) collective-permute-start(bf16[2,16,256]{2,1,0:T(8,128)(2,1)S(1)} %get-tuple-element.42), channel_id=1, source_target_pairs={{0,6},{1,7},{2,4},{3,5},{4,2},{5,3},{6,0},{7,1},{8,14},{9,15},{10,... | collective-permute-start | bytes 49160 | tf_op jit(solution)/shard_map/ppermute | solution.py:333

commit v8 on v7

--- a/solution.py
+++ b/solution.py
@@ -59,9 +59,12 @@
 
 
 def slots_kernel(src_ref, tgt_ref, slot_ref, slots_ref):
-    for pair in range(src_ref.shape[0]):
-        slots_ref[2 * pair] = slot_ref[src_ref[pair]]
-        slots_ref[2 * pair + 1] = slot_ref[tgt_ref[pair]]
+    batch = 16
+    for first in range(0, src_ref.shape[0], batch):
+        pairs = range(first, first + batch)
+        ids = [ref[pair] for pair in pairs for ref in (src_ref, tgt_ref)]
+        for place, slot in enumerate([slot_ref[image] for image in ids]):
+            slots_ref[2 * first + place] = slot
 
 
 def select_kernel(slots_ref, held_ref, out_ref, pieces):
@@ -297,7 +300,12 @@
         out_specs=whole(pltpu.SMEM),
     )
     held = lax.all_to_all(tiles, "pair", 0, 0, tiled=True)
-    held, chip, core = lax.optimization_barrier((held, chip, core))
+    taps = w_first.reshape(3, 3, 3, 3, CONV).transpose(4, 2, 3, 0, 1)
+    z1 = jnp.pad(taps, ((0, 0),) * 4 + ((1, COLS_IN - 4),)).reshape(CONV, K_1)
+    z1 = jnp.pad(z1, ((0, 0), (0, 512 - K_1)))
+    z3 = w_last.reshape(3, 3, 3, 3, CONV).transpose(0, 2, 3, 1, 4).reshape(27, 3 * CONV)
+    z3 = jnp.pad(z3, ((0, 0), (0, 256 - 3 * CONV)))
+    held, chip, core, z1, z3 = lax.optimization_barrier((held, chip, core, z1, z3))
     wanted = call(
         select_kernel,
         jax.ShapeDtypeStruct((groups, 2, 16, 128), BF16),
@@ -306,18 +314,13 @@
         (pltpu.VMEM((2 * groups, 8, 128), F32),),
     )
     routed = lax.all_to_all(wanted, "pair", 0, 0, tiled=True)
-    routed, w_first, w_mid, w_last = lax.optimization_barrier((routed, w_first, w_mid, w_last))
+    routed, w_mid = lax.optimization_barrier((routed, w_mid))
     sends = call(pack_kernel, (jax.ShapeDtypeStruct((groups, 16, 128), BF16),) * 4, (routed,), (chip,))
     own = [sends[0]] + [lax.ppermute(sends[k], "row", row_moves(k, 0)) for k in range(1, CHIPS)]
-    taps = w_first.reshape(3, 3, 3, 3, CONV).transpose(4, 2, 3, 0, 1)
-    z1 = jnp.pad(taps, ((0, 0),) * 4 + ((1, COLS_IN - 4),)).reshape(CONV, K_1)
-    z1 = jnp.pad(z1, ((0, 0), (0, 512 - K_1)))
     taps = w_mid.reshape(3, 3, 3, 3, CONV, CONV).transpose(0, 2, 4, 3, 1, 5)
     z2 = jnp.pad(taps, ((0, 0),) * 4 + ((0, PART_2 - 1), (0, 0))).reshape(9 * CONV, K_2)
     z2 = jnp.pad(z2, ((0, 0), (0, 256 - K_2)))
-    z3 = w_last.reshape(3, 3, 3, 3, CONV).transpose(0, 2, 3, 1, 4).reshape(27, 3 * CONV)
-    z3 = jnp.pad(z3, ((0, 0), (0, 256 - 3 * CONV)))
-    own[1], z1, z2, z3 = lax.optimization_barrier((own[1], z1, z2, z3))
+    own[1], z2 = lax.optimization_barrier((own[1], z2))
     other = [lax.ppermute(block, "row", row_moves(0, 1)) for block in own]
     message = jax.ShapeDtypeStruct((3, 16, POS), BF16)
     keep, give = call(

time: 63.7 us -> 63.3 us (level)
  waiting for transfers between devices: 11.8 us -> 8.29 us
  starting transfers between devices: 24.2 us -> 26.3 us
  blocking collectives: 13.7 us -> 14.7 us
    all_to_all x1, waiting for transfers between devices: 7.35 us -> 4.92 us  [local(): held = lax.all_to_all(tiles, 'pair', 0, 0, tiled=True)]
    ppermute x4, starting transfers between devices: 5.47 us -> 6.54 us  [local(): other = [lax.ppermute(block, 'row', row_moves(0, 1)) for block in own]]
    all_to_all x1, blocking collectives: 13.7 us -> 14.7 us  [local(): routed = lax.all_to_all(wanted, 'pair', 0, 0, tiled=True)]
    ppermute x1, waiting for transfers between devices: 2.43 us -> 1.52 us  [local(): lax.ppermute(far, 'row', [(2 * y + c, 2 * (CHIPS - 1 - y) + c) for y in r...]
    ppermute x1, starting transfers between devices: 1.45 us -> 2.36 us  [local(): lax.ppermute(far, 'row', [(2 * y + c, 2 * (CHIPS - 1 - y) + c) for y in r...]
    unnamed x14 -> x16, local copies, waits for them, and re-layouts: 2.45 us -> 2.7 us
  transfers between devices with their start and end apart: 10 -> 10, of which waited for: 7 -> 5; matrix products, arithmetic and copies ran while one was open for 3% -> 3% of each run, Pallas kernels for 2% -> 2%
where the time goes in v8:
time: 63.3 us; the launch traced here: 63 us
  starting transfers between devices  26.3 us (42%)
  blocking collectives  14.7 us (23%)
  Pallas kernels  9.39 us (15%)
  waiting for transfers between devices  8.29 us (13%)
  local copies, waits for them, and re-layouts  4.16 us (7%)
    all_to_all x1, blocking collectives, local(): routed = lax.all_to_all(wanted, 'pair', 0, 0, tiled=True)  14.7 us
    all_to_all x1, starting transfers between devices, local(): held = lax.all_to_all(tiles, 'pair', 0, 0, tiled=True)  11.9 us
    pallas_call x6, Pallas kernels, call(): pl.pallas_call(kernel, out_shape=out_shape, in_specs=[whole(pltpu.SMEM)]...  7.71 us
    ppermute x4, starting transfers between devices, local(): other = [lax.ppermute(block, 'row', row_moves(0, 1)) for block in own]  6.54 us
    ppermute x3, starting transfers between devices, local(): lax.ppermute(sends[k], 'row', row_moves(k, 0))  5.06 us
    all_to_all x1, waiting for transfers between devices, local(): held = lax.all_to_all(tiles, 'pair', 0, 0, tiled=True)  4.92 us
    unnamed x16, local copies, waits for them, and re-layouts  2.7 us
    ppermute x1, starting transfers between devices, local(): lax.ppermute(far, 'row', [(2 * y + c, 2 * (CHIPS - 1 - y) + c) for y in r...  2.36 us
  transfers between devices with their start and end apart: 10, of which 5 were waited for; matrix products, arithmetic and copies ran while one was open for 3% of the time, Pallas kernels for 2%

profile of v8, /device:TPU:1, one launch (start us, length us, event | category | flops | bytes accessed | tf_op | source)
XLA Modules:
  0.0 63.0 jit_solution(17747380652148986686)
XLA Ops:
  0.0 1.7 %shard_map.73 = bf16[32,16,128]{2,1,0:T(8,128)(2,1)} custom-call(bf16[2,1,32,1024]{3,2,1,0:T(8,128)(2,1)} %own_ref.1), custom_call_target="tpu_custom_call" | custom-call | tf_op jit(solution)/shard_map/pallas_call | solution.py:288
  1.7 11.9 %all-to-all-start = ((bf16[32,16,128]{2,1,0:T(8,128)(2,1)}), bf16[32,16,128]{2,1,0:T(8,128)(2,1)S(1)}, u32[]{:S(2)}, u32[]{:S(2)}) async-start(bf16[32,16,128]{2,1,0:T(8,128)(2,1)} %shard_map.73), calls=%async_computation | async-start | bytes 262144 | tf_op jit(solution)/shard_map/all_to_all | solution.py:302
  13.6 0.0 copy-start.4
  13.6 0.7 %copy-done.4 = bf16[81,16,1]{0,1,2:T(8,128)(2,1)S(1)} copy-done((bf16[81,16,1]{0,1,2:T(8,128)(2,1)S(1)}, bf16[81,16,1]{0,1,2:T(8,128)(2,1)}, u32[]{:S(2)}) %copy-start.4) | copy-done | bytes 2616
  14.3 0.1 copy.11
  14.4 0.3 copy.20
  14.7 0.2 pad.20.clone
  14.9 0.1 reshape.27
  15.0 0.0 copy-start.5
  15.0 0.7 %copy-done.5 = bf16[81,1,16]{0,2,1:T(8,128)(2,1)S(1)} copy-done((bf16[81,1,16]{0,2,1:T(8,128)(2,1)S(1)}, bf16[81,1,16]{0,2,1:T(8,128)(2,1)}, u32[]{:S(2)}) %copy-start.5) | copy-done | bytes 2616
  15.7 0.1 copy.13
  15.9 0.1 reshape.29
  16.0 0.0 copy-start
  16.0 0.0 copy-start.1
  16.0 0.0 copy-start.2
  16.0 0.6 copy-done
  16.6 0.0 copy-done.1
  16.6 0.0 copy-done.2
  16.7 1.3 %shard_map.74.slots_ref = s32[128]{0:T(128)S(1)} custom-call(s32[64]{0:T(128)S(1)} %copy-done, s32[64]{0:T(128)S(1)} %copy-done.1, s32[64]{0:T(128)S(1)} %copy-done.2), custom_call_target="tpu_custom_call" | custom-call | tf_op jit(solution)/shard_map/pallas_call | solution.py:39
  18.0 4.9 %all-to-all-done.held_ref = bf16[32,16,128]{2,1,0:T(8,128)(2,1)S(1)} async-done(((bf16[32,16,128]{2,1,0:T(8,128)(2,1)}), bf16[32,16,128]{2,1,0:T(8,128)(2,1)S(1)}, u32[]{:S(2)}, u32[]{:S(2)}) %all-to-all-start) | async-done | bytes 131104 | tf_op jit(solution)/shard_map/all_to_all | solution.py:302
  22.9 0.7 %shard_map.75 = bf16[32,2,16,128]{3,2,1,0:T(8,128)(2,1)S(1)} custom-call(s32[128]{0:T(128)S(1)} %shard_map.74.slots_ref, bf16[32,16,128]{2,1,0:T(8,128)(2,1)S(1)} %all-to-all-done.held_ref), custom_call_target="tpu_custom_call" | custom-call | tf_op jit(solution)/shard_map/pallas_call | solution.py:39
  23.6 14.7 %all_to_all.10.held_ref = bf16[32,2,16,128]{3,2,1,0:T(8,128)(2,1)S(1)} all-to-all(bf16[32,2,16,128]{3,2,1,0:T(8,128)(2,1)S(1)} %shard_map.75), channel_id=1, replica_groups=mesh['pair'=32,'row'=8] {'pair'}, dimensions={0} | all-to-all | bytes 524288 | tf_op jit(solution)/shard_map/all_to_all | solution.py:316
  38.2 0.0 copy-start.3
  38.3 1.4 %collective-permute-start = (bf16[32,16,128]{2,1,0:T(8,128)(2,1)S(1)}, bf16[32,16,128]{2,1,0:T(8,128)(2,1)S(1)}, u32[]{:S(2)}, u32[]{:S(2)}) collective-permute-start(bf16[32,16,128]{2,1,0:T(8,128)(2,1)S(1)} %get-tuple-element.27), channel_id=1, source_target_pairs={{0,2},{1,3},{2,4},{3,5},{4,6},{5,7},{6,0},{7,1},{8,10},{9,11},{10,... | collective-permute-start | bytes 393224 | tf_op jit(solution)/shard_map/ppermute | solution.py:319
  39.6 2.6 %collective-permute-start.1 = (bf16[32,16,128]{2,1,0:T(8,128)(2,1)S(1)}, bf16[32,16,128]{2,1,0:T(8,128)(2,1)S(1)}, u32[]{:S(2)}, u32[]{:S(2)}) collective-permute-start(bf16[32,16,128]{2,1,0:T(8,128)(2,1)S(1)} %get-tuple-element.30), channel_id=1, source_target_pairs={{0,4},{1,5},{2,6},{3,7},{4,0},{5,1},{6,2},{7,3},{8,12},{9,13},{10,... | collective-permute-start | bytes 393224 | tf_op jit(solution)/shard_map/ppermute | solution.py:319
  42.3 1.1 %collective-permute-start.2 = (bf16[32,16,128]{2,1,0:T(8,128)(2,1)S(1)}, bf16[32,16,128]{2,1,0:T(8,128)(2,1)S(1)}, u32[]{:S(2)}, u32[]{:S(2)}) collective-permute-start(bf16[32,16,128]{2,1,0:T(8,128)(2,1)S(1)} %get-tuple-element.31), channel_id=1, source_target_pairs={{0,6},{1,7},{2,0},{3,1},{4,2},{5,3},{6,4},{7,5},{8,14},{9,15},{10,... | collective-permute-start | bytes 393224 | tf_op jit(solution)/shard_map/ppermute | solution.py:319
  43.3 0.0 copy-done.3
  43.3 0.3 copy.15
  43.7 0.2 copy.21
  43.9 0.2 pad.23.clone
  44.1 0.4 reshape.32
  44.5 4.2 %collective-permute-start.3 = (bf16[32,16,128]{2,1,0:T(8,128)(2,1)S(1)}, bf16[32,16,128]{2,1,0:T(8,128)(2,1)S(1)}, u32[]{:S(2)}, u32[]{:S(2)}) collective-permute-start(bf16[32,16,128]{2,1,0:T(8,128)(2,1)S(1)} %get-tuple-element.26.own_0), channel_id=1, source_target_pairs={{0,1},{1,0},{2,3},{3,2},{4,5},{5,4},{6,7},{7,6},{8,9},{9,8},{10,11... | collective-permute-start | bytes 393224 | tf_op jit(solution)/shard_map/ppermute | solution.py:324
  48.8 0.0 collective-permute-done.own_1
  48.8 0.1 collective-permute-start.4
  48.9 0.0 collective-permute-done.1.own_2
  48.9 1.6 %collective-permute-start.5 = (bf16[32,16,128]{2,1,0:T(8,128)(2,1)S(1)}, bf16[32,16,128]{2,1,0:T(8,128)(2,1)S(1)}, u32[]{:S(2)}, u32[]{:S(2)}) collective-permute-start(bf16[32,16,128]{2,1,0:T(8,128)(2,1)S(1)} %collective-permute-done.1.own_2), channel_id=1, source_target_pairs={{0,1},{1,0},{2,3},{3,2},{4,5},{5,4},{6,7},{7,6},{8,9},{9,8},{10,11... | collective-permute-start | bytes 393224 | tf_op jit(solution)/shard_map/ppermute | solution.py:324
  50.5 0.0 collective-permute-done.2.own_3
  50.5 0.6 collective-permute-start.6
  51.1 0.0 collective-permute-done.3.oth_0
  51.1 0.0 collective-permute-done.4.oth_1
  51.1 0.4 collective-permute-done.5.oth_2
  51.5 0.6 collective-permute-done.6.oth_3
  52.1 5.1 %shard_map.77 = (bf16[3,16,256]{2,1,0:T(8,128)(2,1)S(1)}, bf16[3,16,256]{2,1,0:T(8,128)(2,1)S(1)}) custom-call(s32[1]{0:T(128)} %bitcast.chip_ref, s32[1]{0:T(128)} %bitcast.1.core_ref, bf16[32,16,128]{2,1,0:T(8,128)(2,1)S(1)} %get-tuple-element.26.own_0, bf16[32,16,128]{2,1,0:T(8,128)(2,1)S(1)} %collective-permute-done.own_1, ...), custom_call_target="tpu_custom_call" | custom-call | tf_op jit(solution)/shard_map/pallas_call | solution.py:39
  57.2 0.4 collective-permute-start.7
  57.6 0.8 %collective-permute-done.7.got_ref = bf16[3,16,256]{2,1,0:T(8,128)(2,1)S(1)} collective-permute-done((bf16[3,16,256]{2,1,0:T(8,128)(2,1)S(1)}, bf16[3,16,256]{2,1,0:T(8,128)(2,1)S(1)}, u32[]{:S(2)}, u32[]{:S(2)}) %collective-permute-start.7) | collective-permute-done | bytes 24608 | tf_op jit(solution)/shard_map/ppermute | solution.py:333
  58.5 2.4 %collective-permute-start.8 = (bf16[2,16,256]{2,1,0:T(8,128)(2,1)S(1)}, bf16[2,16,256]{2,1,0:T(8,128)(2,1)S(1)}, u32[]{:S(2)}, u32[]{:S(2)}) collective-permute-start(bf16[2,16,256]{2,1,0:T(8,128)(2,1)S(1)} %get-tuple-element.38), channel_id=1, source_target_pairs={{0,6},{1,7},{2,4},{3,5},{4,2},{5,3},{6,0},{7,1},{8,14},{9,15},{10,... | collective-permute-start | bytes 49160 | tf_op jit(solution)/shard_map/ppermute | solution.py:336
  60.8 1.5 %collective-permute-done.8.far_ref = bf16[2,16,256]{2,1,0:T(8,128)(2,1)S(1)} collective-permute-done((bf16[2,16,256]{2,1,0:T(8,128)(2,1)S(1)}, bf16[2,16,256]{2,1,0:T(8,128)(2,1)S(1)}, u32[]{:S(2)}, u32[]{:S(2)}) %collective-permute-start.8) | collective-permute-done | bytes 16416 | tf_op jit(solution)/shard_map/ppermute | solution.py:336
  62.4 0.6 shard_map.79
  (8 shorter events, 0.2 us)
Async XLA Ops:
  1.7 21.2 %all-to-all-start = ((bf16[32,16,128]{2,1,0:T(8,128)(2,1)}), bf16[32,16,128]{2,1,0:T(8,128)(2,1)S(1)}, u32[]{:S(2)}, u32[]{:S(2)}) async-start(bf16[32,16,128]{2,1,0:T(8,128)(2,1)} %shard_map.73), calls=%async_computation | async-start | bytes 262144 | tf_op jit(solution)/shard_map/all_to_all | solution.py:302
  13.6 0.7 %copy-start.4 = (bf16[81,16,1]{0,1,2:T(8,128)(2,1)S(1)}, bf16[81,16,1]{0,1,2:T(8,128)(2,1)}, u32[]{:S(2)}) copy-start(bf16[81,16,1]{0,1,2:T(8,128)(2,1)} %param.11) | copy-start | bytes 7780
  15.0 0.7 %copy-start.5 = (bf16[81,1,16]{0,2,1:T(8,128)(2,1)S(1)}, bf16[81,1,16]{0,2,1:T(8,128)(2,1)}, u32[]{:S(2)}) copy-start(bf16[81,1,16]{0,2,1:T(8,128)(2,1)} %param.13) | copy-start | bytes 7780
  16.0 0.7 %copy-start = (s32[64]{0:T(128)S(1)}, s32[64]{0:T(128)}, u32[]{:S(2)}) copy-start(s32[64]{0:T(128)} %src_ref.1) | copy-start | bytes 772
  16.0 0.7 %copy-start.1 = (s32[64]{0:T(128)S(1)}, s32[64]{0:T(128)}, u32[]{:S(2)}) copy-start(s32[64]{0:T(128)} %tgt_ref.1) | copy-start | bytes 772
  16.0 0.7 %copy-start.2 = (s32[64]{0:T(128)S(1)}, s32[64]{0:T(128)}, u32[]{:S(2)}) copy-start(s32[64]{0:T(128)} %slot_ref.1) | copy-start | bytes 772
  38.2 5.1 %copy-start.3 = (bf16[81,16,16]{0,2,1:T(8,128)(2,1)S(1)}, bf16[81,16,16]{0,2,1:T(8,128)(2,1)}, u32[]{:S(2)}) copy-start(bf16[81,16,16]{0,2,1:T(8,128)(2,1)} %param.12) | copy-start | bytes 124420
  38.3 10.5 %collective-permute-start = (bf16[32,16,128]{2,1,0:T(8,128)(2,1)S(1)}, bf16[32,16,128]{2,1,0:T(8,128)(2,1)S(1)}, u32[]{:S(2)}, u32[]{:S(2)}) collective-permute-start(bf16[32,16,128]{2,1,0:T(8,128)(2,1)S(1)} %get-tuple-element.27), channel_id=1, source_target_pairs={{0,2},{1,3},{2,4},{3,5},{4,6},{5,7},{6,0},{7,1},{8,10},{9,11},{10,... | collective-permute-start | bytes 393224 | tf_op jit(solution)/shard_map/ppermute | solution.py:319
  39.6 9.2 %collective-permute-start.1 = (bf16[32,16,128]{2,1,0:T(8,128)(2,1)S(1)}, bf16[32,16,128]{2,1,0:T(8,128)(2,1)S(1)}, u32[]{:S(2)}, u32[]{:S(2)}) collective-permute-start(bf16[32,16,128]{2,1,0:T(8,128)(2,1)S(1)} %get-tuple-element.30), channel_id=1, source_target_pairs={{0,4},{1,5},{2,6},{3,7},{4,0},{5,1},{6,2},{7,3},{8,12},{9,13},{10,... | collective-permute-start | bytes 393224 | tf_op jit(solution)/shard_map/ppermute | solution.py:319
  42.3 8.2 %collective-permute-start.2 = (bf16[32,16,128]{2,1,0:T(8,128)(2,1)S(1)}, bf16[32,16,128]{2,1,0:T(8,128)(2,1)S(1)}, u32[]{:S(2)}, u32[]{:S(2)}) collective-permute-start(bf16[32,16,128]{2,1,0:T(8,128)(2,1)S(1)} %get-tuple-element.31), channel_id=1, source_target_pairs={{0,6},{1,7},{2,0},{3,1},{4,2},{5,3},{6,4},{7,5},{8,14},{9,15},{10,... | collective-permute-start | bytes 393224 | tf_op jit(solution)/shard_map/ppermute | solution.py:319
  44.5 6.6 %collective-permute-start.3 = (bf16[32,16,128]{2,1,0:T(8,128)(2,1)S(1)}, bf16[32,16,128]{2,1,0:T(8,128)(2,1)S(1)}, u32[]{:S(2)}, u32[]{:S(2)}) collective-permute-start(bf16[32,16,128]{2,1,0:T(8,128)(2,1)S(1)} %get-tuple-element.26.own_0), channel_id=1, source_target_pairs={{0,1},{1,0},{2,3},{3,2},{4,5},{5,4},{6,7},{7,6},{8,9},{9,8},{10,11... | collective-permute-start | bytes 393224 | tf_op jit(solution)/shard_map/ppermute | solution.py:324
  48.8 2.3 %collective-permute-start.4 = (bf16[32,16,128]{2,1,0:T(8,128)(2,1)S(1)}, bf16[32,16,128]{2,1,0:T(8,128)(2,1)S(1)}, u32[]{:S(2)}, u32[]{:S(2)}) collective-permute-start(bf16[32,16,128]{2,1,0:T(8,128)(2,1)S(1)} %collective-permute-done.own_1), channel_id=1, source_target_pairs={{0,1},{1,0},{2,3},{3,2},{4,5},{5,4},{6,7},{7,6},{8,9},{9,8},{10,11... | collective-permute-start | bytes 393224 | tf_op jit(solution)/shard_map/ppermute | solution.py:324
  48.9 2.6 %collective-permute-start.5 = (bf16[32,16,128]{2,1,0:T(8,128)(2,1)S(1)}, bf16[32,16,128]{2,1,0:T(8,128)(2,1)S(1)}, u32[]{:S(2)}, u32[]{:S(2)}) collective-permute-start(bf16[32,16,128]{2,1,0:T(8,128)(2,1)S(1)} %collective-permute-done.1.own_2), channel_id=1, source_target_pairs={{0,1},{1,0},{2,3},{3,2},{4,5},{5,4},{6,7},{7,6},{8,9},{9,8},{10,11... | collective-permute-start | bytes 393224 | tf_op jit(solution)/shard_map/ppermute | solution.py:324
  50.5 1.6 %collective-permute-start.6 = (bf16[32,16,128]{2,1,0:T(8,128)(2,1)S(1)}, bf16[32,16,128]{2,1,0:T(8,128)(2,1)S(1)}, u32[]{:S(2)}, u32[]{:S(2)}) collective-permute-start(bf16[32,16,128]{2,1,0:T(8,128)(2,1)S(1)} %collective-permute-done.2.own_3), channel_id=1, source_target_pairs={{0,1},{1,0},{2,3},{3,2},{4,5},{5,4},{6,7},{7,6},{8,9},{9,8},{10,11... | collective-permute-start | bytes 393224 | tf_op jit(solution)/shard_map/ppermute | solution.py:324
  57.2 1.3 %collective-permute-start.7 = (bf16[3,16,256]{2,1,0:T(8,128)(2,1)S(1)}, bf16[3,16,256]{2,1,0:T(8,128)(2,1)S(1)}, u32[]{:S(2)}, u32[]{:S(2)}) collective-permute-start(bf16[3,16,256]{2,1,0:T(8,128)(2,1)S(1)} %get-tuple-element.36), channel_id=1, source_target_pairs={{0,1},{1,0},{2,3},{3,2},{4,5},{5,4},{6,7},{7,6},{8,9},{9,8},{10,11... | collective-permute-start | bytes 73736 | tf_op jit(solution)/shard_map/ppermute | solution.py:333
  58.5 3.9 %collective-permute-start.8 = (bf16[2,16,256]{2,1,0:T(8,128)(2,1)S(1)}, bf16[2,16,256]{2,1,0:T(8,128)(2,1)S(1)}, u32[]{:S(2)}, u32[]{:S(2)}) collective-permute-start(bf16[2,16,256]{2,1,0:T(8,128)(2,1)S(1)} %get-tuple-element.38), channel_id=1, source_target_pairs={{0,6},{1,7},{2,4},{3,5},{4,2},{5,3},{6,0},{7,1},{8,14},{9,15},{10,... | collective-permute-start | bytes 49160 | tf_op jit(solution)/shard_map/ppermute | solution.py:336

commit v9 on v8

--- a/solution.py
+++ b/solution.py
@@ -300,12 +300,9 @@
         out_specs=whole(pltpu.SMEM),
     )
     held = lax.all_to_all(tiles, "pair", 0, 0, tiled=True)
-    taps = w_first.reshape(3, 3, 3, 3, CONV).transpose(4, 2, 3, 0, 1)
-    z1 = jnp.pad(taps, ((0, 0),) * 4 + ((1, COLS_IN - 4),)).reshape(CONV, K_1)
-    z1 = jnp.pad(z1, ((0, 0), (0, 512 - K_1)))
     z3 = w_last.reshape(3, 3, 3, 3, CONV).transpose(0, 2, 3, 1, 4).reshape(27, 3 * CONV)
     z3 = jnp.pad(z3, ((0, 0), (0, 256 - 3 * CONV)))
-    held, chip, core, z1, z3 = lax.optimization_barrier((held, chip, core, z1, z3))
+    held, chip, core, z3 = lax.optimization_barrier((held, chip, core, z3))
     wanted = call(
         select_kernel,
         jax.ShapeDtypeStruct((groups, 2, 16, 128), BF16),
@@ -314,13 +311,16 @@
         (pltpu.VMEM((2 * groups, 8, 128), F32),),
     )
     routed = lax.all_to_all(wanted, "pair", 0, 0, tiled=True)
-    routed, w_mid = lax.optimization_barrier((routed, w_mid))
+    routed, w_first, w_mid = lax.optimization_barrier((routed, w_first, w_mid))
     sends = call(pack_kernel, (jax.ShapeDtypeStruct((groups, 16, 128), BF16),) * 4, (routed,), (chip,))
     own = [sends[0]] + [lax.ppermute(sends[k], "row", row_moves(k, 0)) for k in range(1, CHIPS)]
+    taps = w_first.reshape(3, 3, 3, 3, CONV).transpose(4, 2, 3, 0, 1)
+    z1 = jnp.pad(taps, ((0, 0),) * 4 + ((1, COLS_IN - 4),)).reshape(CONV, K_1)
+    z1 = jnp.pad(z1, ((0, 0), (0, 512 - K_1)))
     taps = w_mid.reshape(3, 3, 3, 3, CONV, CONV).transpose(0, 2, 4, 3, 1, 5)
     z2 = jnp.pad(taps, ((0, 0),) * 4 + ((0, PART_2 - 1), (0, 0))).reshape(9 * CONV, K_2)
     z2 = jnp.pad(z2, ((0, 0), (0, 256 - K_2)))
-    own[1], z2 = lax.optimization_barrier((own[1], z2))
+    own[1], z1, z2 = lax.optimization_barrier((own[1], z1, z2))
     other = [lax.ppermute(block, "row", row_moves(0, 1)) for block in own]
     message = jax.ShapeDtypeStruct((3, 16, POS), BF16)
     keep, give = call(

time: 63.3 us -> 62.8 us (level)
  waiting for transfers between devices: 8.29 us -> 9.73 us
  blocking collectives: 14.7 us -> 13.7 us
  starting transfers between devices: 26.3 us -> 25.3 us
    all_to_all x1, waiting for transfers between devices: 4.92 us -> 6.37 us  [local(): held = lax.all_to_all(tiles, 'pair', 0, 0, tiled=True)]
    all_to_all x1, blocking collectives: 14.7 us -> 13.7 us  [local(): routed = lax.all_to_all(wanted, 'pair', 0, 0, tiled=True)]
    ppermute x4, starting transfers between devices: 6.54 us -> 5.58 us  [local(): other = [lax.ppermute(block, 'row', row_moves(0, 1)) for block in own]]
    unnamed x16 -> x15, local copies, waits for them, and re-layouts: 2.7 us -> 2.58 us
  transfers between devices with their start and end apart: 10 -> 10, of which waited for: 5 -> 7; matrix products, arithmetic and copies ran while one was open for 3% -> 3% of each run, Pallas kernels for 2% -> 2%
where the time goes in v9:
time: 62.8 us; the launch traced here: 62.5 us
  starting transfers between devices  25.3 us (40%)
  blocking collectives  13.7 us (22%)
  waiting for transfers between devices  9.73 us (15%)
  Pallas kernels  9.39 us (15%)
  local copies, waits for them, and re-layouts  4.16 us (7%)
    all_to_all x1, blocking collectives, local(): routed = lax.all_to_all(wanted, 'pair', 0, 0, tiled=True)  13.7 us
    all_to_all x1, starting transfers between devices, local(): held = lax.all_to_all(tiles, 'pair', 0, 0, tiled=True)  11.9 us
    pallas_call x6, Pallas kernels, call(): pl.pallas_call(kernel, out_shape=out_shape, in_specs=[whole(pltpu.SMEM)]...  7.7 us
    all_to_all x1, waiting for transfers between devices, local(): held = lax.all_to_all(tiles, 'pair', 0, 0, tiled=True)  6.37 us
    ppermute x4, starting transfers between devices, local(): other = [lax.ppermute(block, 'row', row_moves(0, 1)) for block in own]  5.58 us
    ppermute x3, starting transfers between devices, local(): lax.ppermute(sends[k], 'row', row_moves(k, 0))  5.06 us
    unnamed x15, local copies, waits for them, and re-layouts  2.58 us
    ppermute x1, starting transfers between devices, local(): lax.ppermute(far, 'row', [(2 * y + c, 2 * (CHIPS - 1 - y) + c) for y in r...  2.37 us
  transfers between devices with their start and end apart: 10, of which 7 were waited for; matrix products, arithmetic and copies ran while one was open for 3% of the time, Pallas kernels for 2%

profile of v9, /device:TPU:1, one launch (start us, length us, event | category | flops | bytes accessed | tf_op | source)
XLA Modules:
  0.0 62.5 jit_solution(4923403530506689360)
XLA Ops:
  0.0 1.7 %shard_map.73 = bf16[32,16,128]{2,1,0:T(8,128)(2,1)} custom-call(bf16[2,1,32,1024]{3,2,1,0:T(8,128)(2,1)} %own_ref.1), custom_call_target="tpu_custom_call" | custom-call | tf_op jit(solution)/shard_map/pallas_call | solution.py:288
  1.7 11.9 %all-to-all-start = ((bf16[32,16,128]{2,1,0:T(8,128)(2,1)}), bf16[32,16,128]{2,1,0:T(8,128)(2,1)S(1)}, u32[]{:S(2)}, u32[]{:S(2)}) async-start(bf16[32,16,128]{2,1,0:T(8,128)(2,1)} %shard_map.73), calls=%async_computation | async-start | bytes 262144 | tf_op jit(solution)/shard_map/all_to_all | solution.py:302
  13.6 0.0 copy-start.4
  13.6 0.7 %copy-done.4 = bf16[81,1,16]{0,2,1:T(8,128)(2,1)S(1)} copy-done((bf16[81,1,16]{0,2,1:T(8,128)(2,1)S(1)}, bf16[81,1,16]{0,2,1:T(8,128)(2,1)}, u32[]{:S(2)}) %copy-start.4) | copy-done | bytes 2616
  14.3 0.1 copy.11
  14.4 0.1 reshape.27
  14.5 0.0 copy-start
  14.5 0.0 copy-start.1
  14.5 0.0 copy-start.2
  14.6 0.6 copy-done
  15.2 0.0 copy-done.1
  15.2 0.0 copy-done.2
  15.2 1.3 %shard_map.74.slots_ref = s32[128]{0:T(128)S(1)} custom-call(s32[64]{0:T(128)S(1)} %copy-done, s32[64]{0:T(128)S(1)} %copy-done.1, s32[64]{0:T(128)S(1)} %copy-done.2), custom_call_target="tpu_custom_call" | custom-call | tf_op jit(solution)/shard_map/pallas_call | solution.py:39
  16.5 6.4 %all-to-all-done.held_ref = bf16[32,16,128]{2,1,0:T(8,128)(2,1)S(1)} async-done(((bf16[32,16,128]{2,1,0:T(8,128)(2,1)}), bf16[32,16,128]{2,1,0:T(8,128)(2,1)S(1)}, u32[]{:S(2)}, u32[]{:S(2)}) %all-to-all-start) | async-done | bytes 131104 | tf_op jit(solution)/shard_map/all_to_all | solution.py:302
  22.9 0.7 %shard_map.75 = bf16[32,2,16,128]{3,2,1,0:T(8,128)(2,1)S(1)} custom-call(s32[128]{0:T(128)S(1)} %shard_map.74.slots_ref, bf16[32,16,128]{2,1,0:T(8,128)(2,1)S(1)} %all-to-all-done.held_ref), custom_call_target="tpu_custom_call" | custom-call | tf_op jit(solution)/shard_map/pallas_call | solution.py:39
  23.6 13.7 %all_to_all.10.held_ref = bf16[32,2,16,128]{3,2,1,0:T(8,128)(2,1)S(1)} all-to-all(bf16[32,2,16,128]{3,2,1,0:T(8,128)(2,1)S(1)} %shard_map.75), channel_id=1, replica_groups=mesh['pair'=32,'row'=8] {'pair'}, dimensions={0} | all-to-all | bytes 524288 | tf_op jit(solution)/shard_map/all_to_all | solution.py:313
  37.3 0.0 copy-start.3
  37.3 1.4 %collective-permute-start = (bf16[32,16,128]{2,1,0:T(8,128)(2,1)S(1)}, bf16[32,16,128]{2,1,0:T(8,128)(2,1)S(1)}, u32[]{:S(2)}, u32[]{:S(2)}) collective-permute-start(bf16[32,16,128]{2,1,0:T(8,128)(2,1)S(1)} %get-tuple-element.28), channel_id=1, source_target_pairs={{0,2},{1,3},{2,4},{3,5},{4,6},{5,7},{6,0},{7,1},{8,10},{9,11},{10,... | collective-permute-start | bytes 393224 | tf_op jit(solution)/shard_map/ppermute | solution.py:316
  38.7 2.6 %collective-permute-start.1 = (bf16[32,16,128]{2,1,0:T(8,128)(2,1)S(1)}, bf16[32,16,128]{2,1,0:T(8,128)(2,1)S(1)}, u32[]{:S(2)}, u32[]{:S(2)}) collective-permute-start(bf16[32,16,128]{2,1,0:T(8,128)(2,1)S(1)} %get-tuple-element.32), channel_id=1, source_target_pairs={{0,4},{1,5},{2,6},{3,7},{4,0},{5,1},{6,2},{7,3},{8,12},{9,13},{10,... | collective-permute-start | bytes 393224 | tf_op jit(solution)/shard_map/ppermute | solution.py:316
  41.3 1.1 %collective-permute-start.2 = (bf16[32,16,128]{2,1,0:T(8,128)(2,1)S(1)}, bf16[32,16,128]{2,1,0:T(8,128)(2,1)S(1)}, u32[]{:S(2)}, u32[]{:S(2)}) collective-permute-start(bf16[32,16,128]{2,1,0:T(8,128)(2,1)S(1)} %get-tuple-element.33), channel_id=1, source_target_pairs={{0,6},{1,7},{2,0},{3,1},{4,2},{5,3},{6,4},{7,5},{8,14},{9,15},{10,... | collective-permute-start | bytes 393224 | tf_op jit(solution)/shard_map/ppermute | solution.py:316
  42.4 0.0 copy-done.3
  42.4 0.3 copy.15
  42.7 0.2 copy.21
  42.9 0.2 pad.23.clone
  43.1 0.4 reshape.32
  43.6 0.0 copy-start.5
  43.6 0.7 %copy-done.5 = bf16[81,16,1]{0,1,2:T(8,128)(2,1)S(1)} copy-done((bf16[81,16,1]{0,1,2:T(8,128)(2,1)S(1)}, bf16[81,16,1]{0,1,2:T(8,128)(2,1)}, u32[]{:S(2)}) %copy-start.5) | copy-done | bytes 2616
  44.2 0.1 copy.13
  44.4 0.3 copy.20
  44.7 0.2 pad.21.clone
  44.8 0.1 reshape.29
  45.0 4.7 %collective-permute-start.3 = (bf16[32,16,128]{2,1,0:T(8,128)(2,1)S(1)}, bf16[32,16,128]{2,1,0:T(8,128)(2,1)S(1)}, u32[]{:S(2)}, u32[]{:S(2)}) collective-permute-start(bf16[32,16,128]{2,1,0:T(8,128)(2,1)S(1)} %get-tuple-element.27.own_0), channel_id=1, source_target_pairs={{0,1},{1,0},{2,3},{3,2},{4,5},{5,4},{6,7},{7,6},{8,9},{9,8},{10,11... | collective-permute-start | bytes 393224 | tf_op jit(solution)/shard_map/ppermute | solution.py:324
  49.7 0.0 collective-permute-done.own_1
  49.7 0.1 collective-permute-start.4
  49.8 0.0 collective-permute-done.1.own_2
  49.8 0.4 collective-permute-start.5
  50.2 0.0 collective-permute-done.2.own_3
  50.2 0.4 collective-permute-start.6
  50.6 0.1 collective-permute-done.3.oth_0
  50.7 0.4 collective-permute-done.4.oth_1
  51.0 0.2 collective-permute-done.5.oth_2
  51.2 0.4 collective-permute-done.6.oth_3
  51.6 5.1 %shard_map.77 = (bf16[3,16,256]{2,1,0:T(8,128)(2,1)S(1)}, bf16[3,16,256]{2,1,0:T(8,128)(2,1)S(1)}) custom-call(s32[1]{0:T(128)} %bitcast.chip_ref, s32[1]{0:T(128)} %bitcast.1.core_ref, bf16[32,16,128]{2,1,0:T(8,128)(2,1)S(1)} %get-tuple-element.27.own_0, bf16[32,16,128]{2,1,0:T(8,128)(2,1)S(1)} %collective-permute-done.own_1, ...), custom_call_target="tpu_custom_call" | custom-call | tf_op jit(solution)/shard_map/pallas_call | solution.py:39
  56.6 0.4 collective-permute-start.7
  57.1 0.8 %collective-permute-done.7.got_ref = bf16[3,16,256]{2,1,0:T(8,128)(2,1)S(1)} collective-permute-done((bf16[3,16,256]{2,1,0:T(8,128)(2,1)S(1)}, bf16[3,16,256]{2,1,0:T(8,128)(2,1)S(1)}, u32[]{:S(2)}, u32[]{:S(2)}) %collective-permute-start.7) | collective-permute-done | bytes 24608 | tf_op jit(solution)/shard_map/ppermute | solution.py:333
  58.0 2.4 %collective-permute-start.8 = (bf16[2,16,256]{2,1,0:T(8,128)(2,1)S(1)}, bf16[2,16,256]{2,1,0:T(8,128)(2,1)S(1)}, u32[]{:S(2)}, u32[]{:S(2)}) collective-permute-start(bf16[2,16,256]{2,1,0:T(8,128)(2,1)S(1)} %get-tuple-element.40), channel_id=1, source_target_pairs={{0,6},{1,7},{2,4},{3,5},{4,2},{5,3},{6,0},{7,1},{8,14},{9,15},{10,... | collective-permute-start | bytes 49160 | tf_op jit(solution)/shard_map/ppermute | solution.py:336
  60.3 1.5 %collective-permute-done.8.far_ref = bf16[2,16,256]{2,1,0:T(8,128)(2,1)S(1)} collective-permute-done((bf16[2,16,256]{2,1,0:T(8,128)(2,1)S(1)}, bf16[2,16,256]{2,1,0:T(8,128)(2,1)S(1)}, u32[]{:S(2)}, u32[]{:S(2)}) %collective-permute-start.8) | collective-permute-done | bytes 16416 | tf_op jit(solution)/shard_map/ppermute | solution.py:336
  61.9 0.6 shard_map.79
  (8 shorter events, 0.2 us)
Async XLA Ops:
  1.7 21.2 %all-to-all-start = ((bf16[32,16,128]{2,1,0:T(8,128)(2,1)}), bf16[32,16,128]{2,1,0:T(8,128)(2,1)S(1)}, u32[]{:S(2)}, u32[]{:S(2)}) async-start(bf16[32,16,128]{2,1,0:T(8,128)(2,1)} %shard_map.73), calls=%async_computation | async-start | bytes 262144 | tf_op jit(solution)/shard_map/all_to_all | solution.py:302
  13.6 0.7 %copy-start.4 = (bf16[81,1,16]{0,2,1:T(8,128)(2,1)S(1)}, bf16[81,1,16]{0,2,1:T(8,128)(2,1)}, u32[]{:S(2)}) copy-start(bf16[81,1,16]{0,2,1:T(8,128)(2,1)} %param.13) | copy-start | bytes 7780
  14.5 0.7 %copy-start = (s32[64]{0:T(128)S(1)}, s32[64]{0:T(128)}, u32[]{:S(2)}) copy-start(s32[64]{0:T(128)} %src_ref.1) | copy-start | bytes 772
  14.5 0.7 %copy-start.1 = (s32[64]{0:T(128)S(1)}, s32[64]{0:T(128)}, u32[]{:S(2)}) copy-start(s32[64]{0:T(128)} %tgt_ref.1) | copy-start | bytes 772
  14.5 0.7 %copy-start.2 = (s32[64]{0:T(128)S(1)}, s32[64]{0:T(128)}, u32[]{:S(2)}) copy-start(s32[64]{0:T(128)} %slot_ref.1) | copy-start | bytes 772
  37.3 5.1 %copy-start.3 = (bf16[81,16,16]{0,2,1:T(8,128)(2,1)S(1)}, bf16[81,16,16]{0,2,1:T(8,128)(2,1)}, u32[]{:S(2)}) copy-start(bf16[81,16,16]{0,2,1:T(8,128)(2,1)} %param.12) | copy-start | bytes 124420
  37.3 12.4 %collective-permute-start = (bf16[32,16,128]{2,1,0:T(8,128)(2,1)S(1)}, bf16[32,16,128]{2,1,0:T(8,128)(2,1)S(1)}, u32[]{:S(2)}, u32[]{:S(2)}) collective-permute-start(bf16[32,16,128]{2,1,0:T(8,128)(2,1)S(1)} %get-tuple-element.28), channel_id=1, source_target_pairs={{0,2},{1,3},{2,4},{3,5},{4,6},{5,7},{6,0},{7,1},{8,10},{9,11},{10,... | collective-permute-start | bytes 393224 | tf_op jit(solution)/shard_map/ppermute | solution.py:316
  38.7 11.1 %collective-permute-start.1 = (bf16[32,16,128]{2,1,0:T(8,128)(2,1)S(1)}, bf16[32,16,128]{2,1,0:T(8,128)(2,1)S(1)}, u32[]{:S(2)}, u32[]{:S(2)}) collective-permute-start(bf16[32,16,128]{2,1,0:T(8,128)(2,1)S(1)} %get-tuple-element.32), channel_id=1, source_target_pairs={{0,4},{1,5},{2,6},{3,7},{4,0},{5,1},{6,2},{7,3},{8,12},{9,13},{10,... | collective-permute-start | bytes 393224 | tf_op jit(solution)/shard_map/ppermute | solution.py:316
  41.3 8.9 %collective-permute-start.2 = (bf16[32,16,128]{2,1,0:T(8,128)(2,1)S(1)}, bf16[32,16,128]{2,1,0:T(8,128)(2,1)S(1)}, u32[]{:S(2)}, u32[]{:S(2)}) collective-permute-start(bf16[32,16,128]{2,1,0:T(8,128)(2,1)S(1)} %get-tuple-element.33), channel_id=1, source_target_pairs={{0,6},{1,7},{2,0},{3,1},{4,2},{5,3},{6,4},{7,5},{8,14},{9,15},{10,... | collective-permute-start | bytes 393224 | tf_op jit(solution)/shard_map/ppermute | solution.py:316
  43.6 0.7 %copy-start.5 = (bf16[81,16,1]{0,1,2:T(8,128)(2,1)S(1)}, bf16[81,16,1]{0,1,2:T(8,128)(2,1)}, u32[]{:S(2)}) copy-start(bf16[81,16,1]{0,1,2:T(8,128)(2,1)} %param.11) | copy-start | bytes 7780
  45.0 5.7 %collective-permute-start.3 = (bf16[32,16,128]{2,1,0:T(8,128)(2,1)S(1)}, bf16[32,16,128]{2,1,0:T(8,128)(2,1)S(1)}, u32[]{:S(2)}, u32[]{:S(2)}) collective-permute-start(bf16[32,16,128]{2,1,0:T(8,128)(2,1)S(1)} %get-tuple-element.27.own_0), channel_id=1, source_target_pairs={{0,1},{1,0},{2,3},{3,2},{4,5},{5,4},{6,7},{7,6},{8,9},{9,8},{10,11... | collective-permute-start | bytes 393224 | tf_op jit(solution)/shard_map/ppermute | solution.py:324
  49.7 1.3 %collective-permute-start.4 = (bf16[32,16,128]{2,1,0:T(8,128)(2,1)S(1)}, bf16[32,16,128]{2,1,0:T(8,128)(2,1)S(1)}, u32[]{:S(2)}, u32[]{:S(2)}) collective-permute-start(bf16[32,16,128]{2,1,0:T(8,128)(2,1)S(1)} %collective-permute-done.own_1), channel_id=1, source_target_pairs={{0,1},{1,0},{2,3},{3,2},{4,5},{5,4},{6,7},{7,6},{8,9},{9,8},{10,11... | collective-permute-start | bytes 393224 | tf_op jit(solution)/shard_map/ppermute | solution.py:324
  49.8 1.4 %collective-permute-start.5 = (bf16[32,16,128]{2,1,0:T(8,128)(2,1)S(1)}, bf16[32,16,128]{2,1,0:T(8,128)(2,1)S(1)}, u32[]{:S(2)}, u32[]{:S(2)}) collective-permute-start(bf16[32,16,128]{2,1,0:T(8,128)(2,1)S(1)} %collective-permute-done.1.own_2), channel_id=1, source_target_pairs={{0,1},{1,0},{2,3},{3,2},{4,5},{5,4},{6,7},{7,6},{8,9},{9,8},{10,11... | collective-permute-start | bytes 393224 | tf_op jit(solution)/shard_map/ppermute | solution.py:324
  50.2 1.4 %collective-permute-start.6 = (bf16[32,16,128]{2,1,0:T(8,128)(2,1)S(1)}, bf16[32,16,128]{2,1,0:T(8,128)(2,1)S(1)}, u32[]{:S(2)}, u32[]{:S(2)}) collective-permute-start(bf16[32,16,128]{2,1,0:T(8,128)(2,1)S(1)} %collective-permute-done.2.own_3), channel_id=1, source_target_pairs={{0,1},{1,0},{2,3},{3,2},{4,5},{5,4},{6,7},{7,6},{8,9},{9,8},{10,11... | collective-permute-start | bytes 393224 | tf_op jit(solution)/shard_map/ppermute | solution.py:324
  56.6 1.3 %collective-permute-start.7 = (bf16[3,16,256]{2,1,0:T(8,128)(2,1)S(1)}, bf16[3,16,256]{2,1,0:T(8,128)(2,1)S(1)}, u32[]{:S(2)}, u32[]{:S(2)}) collective-permute-start(bf16[3,16,256]{2,1,0:T(8,128)(2,1)S(1)} %get-tuple-element.38), channel_id=1, source_target_pairs={{0,1},{1,0},{2,3},{3,2},{4,5},{5,4},{6,7},{7,6},{8,9},{9,8},{10,11... | collective-permute-start | bytes 73736 | tf_op jit(solution)/shard_map/ppermute | solution.py:333
  58.0 3.9 %collective-permute-start.8 = (bf16[2,16,256]{2,1,0:T(8,128)(2,1)S(1)}, bf16[2,16,256]{2,1,0:T(8,128)(2,1)S(1)}, u32[]{:S(2)}, u32[]{:S(2)}) collective-permute-start(bf16[2,16,256]{2,1,0:T(8,128)(2,1)S(1)} %get-tuple-element.40), channel_id=1, source_target_pairs={{0,6},{1,7},{2,4},{3,5},{4,2},{5,3},{6,0},{7,1},{8,14},{9,15},{10,... | collective-permute-start | bytes 49160 | tf_op jit(solution)/shard_map/ppermute | solution.py:336

commit v10 on v8

--- a/solution.py
+++ b/solution.py
@@ -267,13 +267,6 @@
     far_ref[...] = lines[1]
 
 
-def place_kernel(chip_ref, near_ref, far_ref, out_ref):
-    pair = chip_ref[0] // (CHIPS // 2)
-    for half in range(2):
-        out_ref[pair, 0, half * BLOCK : half * BLOCK + BLOCK] = near_ref[half]
-        out_ref[1 - pair, 0, half * BLOCK : half * BLOCK + BLOCK] = far_ref[half]
-
-
 def row_moves(chips, cores):
     return [(2 * y + c, 2 * ((y + chips) % CHIPS) + (c ^ cores)) for y in range(CHIPS) for c in range(2)]
 
@@ -334,7 +327,8 @@
     lines = jax.ShapeDtypeStruct((2, BLOCK, POS), BF16)
     near, far = call(finish_kernel, (lines, lines), (keep, got), (core,), (pltpu.VMEM((2, 2, BLOCK, POS), BF16),))
     far = lax.ppermute(far, "row", [(2 * y + c, 2 * (CHIPS - 1 - y) + c) for y in range(CHIPS) for c in range(2)])
-    return call(place_kernel, jax.ShapeDtypeStruct((2, 1, WID, POS), BF16), (near, far), (chip,))
+    first = (chip < CHIPS // 2).reshape(1, 1, 1)
+    return jnp.where(first, jnp.stack([near, far]), jnp.stack([far, near])).reshape(2, 1, WID, POS)
 
 
 def solution(mesh):

time: 63.3 us -> 63.3 us (level)
    pallas_call x6 -> x5, Pallas kernels: 7.71 us -> 7.09 us  [call(): pl.pallas_call(kernel, out_shape=out_shape, in_specs=[whole(pltpu.SMEM)]...]
where the time goes in v10:
time: 63.3 us; the launch traced here: 63 us
  starting transfers between devices  26.3 us (42%)
  blocking collectives  14.7 us (23%)
  Pallas kernels  8.77 us (14%)
  waiting for transfers between devices  8.29 us (13%)
  local copies, waits for them, and re-layouts  4.16 us (7%)
    all_to_all x1, blocking collectives, local(): routed = lax.all_to_all(wanted, 'pair', 0, 0, tiled=True)  14.7 us
    all_to_all x1, starting transfers between devices, local(): held = lax.all_to_all(tiles, 'pair', 0, 0, tiled=True)  11.9 us
    pallas_call x5, Pallas kernels, call(): pl.pallas_call(kernel, out_shape=out_shape, in_specs=[whole(pltpu.SMEM)]...  7.09 us
    ppermute x4, starting transfers between devices, local(): other = [lax.ppermute(block, 'row', row_moves(0, 1)) for block in own]  6.54 us
    ppermute x3, starting transfers between devices, local(): lax.ppermute(sends[k], 'row', row_moves(k, 0))  5.06 us
    all_to_all x1, waiting for transfers between devices, local(): held = lax.all_to_all(tiles, 'pair', 0, 0, tiled=True)  4.92 us
    unnamed x16, local copies, waits for them, and re-layouts  2.7 us
    ppermute x1, starting transfers between devices, local(): lax.ppermute(far, 'row', [(2 * y + c, 2 * (CHIPS - 1 - y) + c) for y in r...  2.36 us
  transfers between devices with their start and end apart: 10, of which 5 were waited for; matrix products, arithmetic and copies ran while one was open for 3% of the time, Pallas kernels for 2%

profile of v10, /device:TPU:1, one launch (start us, length us, event | category | flops | bytes accessed | tf_op | source)
XLA Modules:
  0.0 63.0 jit_solution(13118672877332573842)
XLA Ops:
  0.0 1.7 %shard_map.73 = bf16[32,16,128]{2,1,0:T(8,128)(2,1)} custom-call(bf16[2,1,32,1024]{3,2,1,0:T(8,128)(2,1)} %own_ref.1), custom_call_target="tpu_custom_call" | custom-call | tf_op jit(solution)/shard_map/pallas_call | solution.py:281
  1.7 11.9 %all-to-all-start = ((bf16[32,16,128]{2,1,0:T(8,128)(2,1)}), bf16[32,16,128]{2,1,0:T(8,128)(2,1)S(1)}, u32[]{:S(2)}, u32[]{:S(2)}) async-start(bf16[32,16,128]{2,1,0:T(8,128)(2,1)} %shard_map.73), calls=%async_computation | async-start | bytes 262144 | tf_op jit(solution)/shard_map/all_to_all | solution.py:295
  13.6 0.0 copy-start.4
  13.6 0.7 %copy-done.4 = bf16[81,16,1]{0,1,2:T(8,128)(2,1)S(1)} copy-done((bf16[81,16,1]{0,1,2:T(8,128)(2,1)S(1)}, bf16[81,16,1]{0,1,2:T(8,128)(2,1)}, u32[]{:S(2)}) %copy-start.4) | copy-done | bytes 2616
  14.3 0.1 copy.11
  14.4 0.3 copy.20
  14.7 0.2 pad.20.clone
  14.9 0.1 reshape.89
  15.0 0.0 copy-start.5
  15.0 0.7 %copy-done.5 = bf16[81,1,16]{0,2,1:T(8,128)(2,1)S(1)} copy-done((bf16[81,1,16]{0,2,1:T(8,128)(2,1)S(1)}, bf16[81,1,16]{0,2,1:T(8,128)(2,1)}, u32[]{:S(2)}) %copy-start.5) | copy-done | bytes 2616
  15.7 0.1 copy.13
  15.9 0.1 reshape.91
  16.0 0.0 copy-start
  16.0 0.0 copy-start.1
  16.0 0.0 copy-start.2
  16.0 0.6 copy-done
  16.6 0.0 copy-done.1
  16.6 0.0 copy-done.2
  16.7 1.3 %shard_map.74.slots_ref = s32[128]{0:T(128)S(1)} custom-call(s32[64]{0:T(128)S(1)} %copy-done, s32[64]{0:T(128)S(1)} %copy-done.1, s32[64]{0:T(128)S(1)} %copy-done.2), custom_call_target="tpu_custom_call" | custom-call | tf_op jit(solution)/shard_map/pallas_call | solution.py:39
  18.0 4.9 %all-to-all-done.held_ref = bf16[32,16,128]{2,1,0:T(8,128)(2,1)S(1)} async-done(((bf16[32,16,128]{2,1,0:T(8,128)(2,1)}), bf16[32,16,128]{2,1,0:T(8,128)(2,1)S(1)}, u32[]{:S(2)}, u32[]{:S(2)}) %all-to-all-start) | async-done | bytes 131104 | tf_op jit(solution)/shard_map/all_to_all | solution.py:295
  22.9 0.7 %shard_map.75 = bf16[32,2,16,128]{3,2,1,0:T(8,128)(2,1)S(1)} custom-call(s32[128]{0:T(128)S(1)} %shard_map.74.slots_ref, bf16[32,16,128]{2,1,0:T(8,128)(2,1)S(1)} %all-to-all-done.held_ref), custom_call_target="tpu_custom_call" | custom-call | tf_op jit(solution)/shard_map/pallas_call | solution.py:39
  23.6 14.7 %all_to_all.10.held_ref = bf16[32,2,16,128]{3,2,1,0:T(8,128)(2,1)S(1)} all-to-all(bf16[32,2,16,128]{3,2,1,0:T(8,128)(2,1)S(1)} %shard_map.75), channel_id=1, replica_groups=mesh['pair'=32,'row'=8] {'pair'}, dimensions={0} | all-to-all | bytes 524288 | tf_op jit(solution)/shard_map/all_to_all | solution.py:309
  38.2 0.0 copy-start.3
  38.3 1.4 %collective-permute-start = (bf16[32,16,128]{2,1,0:T(8,128)(2,1)S(1)}, bf16[32,16,128]{2,1,0:T(8,128)(2,1)S(1)}, u32[]{:S(2)}, u32[]{:S(2)}) collective-permute-start(bf16[32,16,128]{2,1,0:T(8,128)(2,1)S(1)} %get-tuple-element.27), channel_id=1, source_target_pairs={{0,2},{1,3},{2,4},{3,5},{4,6},{5,7},{6,0},{7,1},{8,10},{9,11},{10,... | collective-permute-start | bytes 393224 | tf_op jit(solution)/shard_map/ppermute | solution.py:312
  39.6 2.6 %collective-permute-start.1 = (bf16[32,16,128]{2,1,0:T(8,128)(2,1)S(1)}, bf16[32,16,128]{2,1,0:T(8,128)(2,1)S(1)}, u32[]{:S(2)}, u32[]{:S(2)}) collective-permute-start(bf16[32,16,128]{2,1,0:T(8,128)(2,1)S(1)} %get-tuple-element.30), channel_id=1, source_target_pairs={{0,4},{1,5},{2,6},{3,7},{4,0},{5,1},{6,2},{7,3},{8,12},{9,13},{10,... | collective-permute-start | bytes 393224 | tf_op jit(solution)/shard_map/ppermute | solution.py:312
  42.3 1.1 %collective-permute-start.2 = (bf16[32,16,128]{2,1,0:T(8,128)(2,1)S(1)}, bf16[32,16,128]{2,1,0:T(8,128)(2,1)S(1)}, u32[]{:S(2)}, u32[]{:S(2)}) collective-permute-start(bf16[32,16,128]{2,1,0:T(8,128)(2,1)S(1)} %get-tuple-element.31), channel_id=1, source_target_pairs={{0,6},{1,7},{2,0},{3,1},{4,2},{5,3},{6,4},{7,5},{8,14},{9,15},{10,... | collective-permute-start | bytes 393224 | tf_op jit(solution)/shard_map/ppermute | solution.py:312
  43.3 0.0 copy-done.3
  43.3 0.3 copy.15
  43.7 0.2 copy.21
  43.9 0.2 pad.23.clone
  44.1 0.4 reshape.94
  44.5 4.2 %collective-permute-start.3 = (bf16[32,16,128]{2,1,0:T(8,128)(2,1)S(1)}, bf16[32,16,128]{2,1,0:T(8,128)(2,1)S(1)}, u32[]{:S(2)}, u32[]{:S(2)}) collective-permute-start(bf16[32,16,128]{2,1,0:T(8,128)(2,1)S(1)} %get-tuple-element.26.own_0), channel_id=1, source_target_pairs={{0,1},{1,0},{2,3},{3,2},{4,5},{5,4},{6,7},{7,6},{8,9},{9,8},{10,11... | collective-permute-start | bytes 393224 | tf_op jit(solution)/shard_map/ppermute | solution.py:317
  48.8 0.0 collective-permute-done.own_1
  48.8 0.1 collective-permute-start.4
  48.9 0.0 collective-permute-done.1.own_2
  48.9 1.6 %collective-permute-start.5 = (bf16[32,16,128]{2,1,0:T(8,128)(2,1)S(1)}, bf16[32,16,128]{2,1,0:T(8,128)(2,1)S(1)}, u32[]{:S(2)}, u32[]{:S(2)}) collective-permute-start(bf16[32,16,128]{2,1,0:T(8,128)(2,1)S(1)} %collective-permute-done.1.own_2), channel_id=1, source_target_pairs={{0,1},{1,0},{2,3},{3,2},{4,5},{5,4},{6,7},{7,6},{8,9},{9,8},{10,11... | collective-permute-start | bytes 393224 | tf_op jit(solution)/shard_map/ppermute | solution.py:317
  50.5 0.0 collective-permute-done.2.own_3
  50.5 0.6 collective-permute-start.6
  51.1 0.0 collective-permute-done.3.oth_0
  51.1 0.0 collective-permute-done.4.oth_1
  51.1 0.4 collective-permute-done.5.oth_2
  51.5 0.6 collective-permute-done.6.oth_3
  52.1 5.1 %shard_map.77 = (bf16[3,16,256]{2,1,0:T(8,128)(2,1)S(1)}, bf16[3,16,256]{2,1,0:T(8,128)(2,1)S(1)}) custom-call(s32[1]{0:T(128)} %bitcast.chip_ref, s32[1]{0:T(128)} %bitcast.1.core_ref, bf16[32,16,128]{2,1,0:T(8,128)(2,1)S(1)} %get-tuple-element.26.own_0, bf16[32,16,128]{2,1,0:T(8,128)(2,1)S(1)} %collective-permute-done.own_1, ...), custom_call_target="tpu_custom_call" | custom-call | tf_op jit(solution)/shard_map/pallas_call | solution.py:39
  57.2 0.4 collective-permute-start.7
  57.6 0.8 %collective-permute-done.7.got_ref = bf16[3,16,256]{2,1,0:T(8,128)(2,1)S(1)} collective-permute-done((bf16[3,16,256]{2,1,0:T(8,128)(2,1)S(1)}, bf16[3,16,256]{2,1,0:T(8,128)(2,1)S(1)}, u32[]{:S(2)}, u32[]{:S(2)}) %collective-permute-start.7) | collective-permute-done | bytes 24608 | tf_op jit(solution)/shard_map/ppermute | solution.py:326
  58.5 2.4 %collective-permute-start.8 = (bf16[2,16,256]{2,1,0:T(8,128)(2,1)S(1)}, bf16[2,16,256]{2,1,0:T(8,128)(2,1)S(1)}, u32[]{:S(2)}, u32[]{:S(2)}) collective-permute-start(bf16[2,16,256]{2,1,0:T(8,128)(2,1)S(1)} %get-tuple-element.38), channel_id=1, source_target_pairs={{0,6},{1,7},{2,4},{3,5},{4,2},{5,3},{6,0},{7,1},{8,14},{9,15},{10,... | collective-permute-start | bytes 49160 | tf_op jit(solution)/shard_map/ppermute | solution.py:329
  60.8 1.5 %collective-permute-done.8 = bf16[2,16,256]{2,1,0:T(8,128)(2,1)S(1)} collective-permute-done((bf16[2,16,256]{2,1,0:T(8,128)(2,1)S(1)}, bf16[2,16,256]{2,1,0:T(8,128)(2,1)S(1)}, u32[]{:S(2)}, u32[]{:S(2)}) %collective-permute-start.8) | collective-permute-done | bytes 16416 | tf_op jit(solution)/shard_map/ppermute | solution.py:329
  62.4 0.6 maximum_select_fusion
  (8 shorter events, 0.2 us)
Async XLA Ops:
  1.7 21.2 %all-to-all-start = ((bf16[32,16,128]{2,1,0:T(8,128)(2,1)}), bf16[32,16,128]{2,1,0:T(8,128)(2,1)S(1)}, u32[]{:S(2)}, u32[]{:S(2)}) async-start(bf16[32,16,128]{2,1,0:T(8,128)(2,1)} %shard_map.73), calls=%async_computation | async-start | bytes 262144 | tf_op jit(solution)/shard_map/all_to_all | solution.py:295
  13.6 0.7 %copy-start.4 = (bf16[81,16,1]{0,1,2:T(8,128)(2,1)S(1)}, bf16[81,16,1]{0,1,2:T(8,128)(2,1)}, u32[]{:S(2)}) copy-start(bf16[81,16,1]{0,1,2:T(8,128)(2,1)} %param.11) | copy-start | bytes 7780
  15.0 0.7 %copy-start.5 = (bf16[81,1,16]{0,2,1:T(8,128)(2,1)S(1)}, bf16[81,1,16]{0,2,1:T(8,128)(2,1)}, u32[]{:S(2)}) copy-start(bf16[81,1,16]{0,2,1:T(8,128)(2,1)} %param.13) | copy-start | bytes 7780
  16.0 0.7 %copy-start = (s32[64]{0:T(128)S(1)}, s32[64]{0:T(128)}, u32[]{:S(2)}) copy-start(s32[64]{0:T(128)} %src_ref.1) | copy-start | bytes 772
  16.0 0.7 %copy-start.1 = (s32[64]{0:T(128)S(1)}, s32[64]{0:T(128)}, u32[]{:S(2)}) copy-start(s32[64]{0:T(128)} %tgt_ref.1) | copy-start | bytes 772
  16.0 0.7 %copy-start.2 = (s32[64]{0:T(128)S(1)}, s32[64]{0:T(128)}, u32[]{:S(2)}) copy-start(s32[64]{0:T(128)} %slot_ref.1) | copy-start | bytes 772
  38.2 5.1 %copy-start.3 = (bf16[81,16,16]{0,2,1:T(8,128)(2,1)S(1)}, bf16[81,16,16]{0,2,1:T(8,128)(2,1)}, u32[]{:S(2)}) copy-start(bf16[81,16,16]{0,2,1:T(8,128)(2,1)} %param.12) | copy-start | bytes 124420
  38.3 10.5 %collective-permute-start = (bf16[32,16,128]{2,1,0:T(8,128)(2,1)S(1)}, bf16[32,16,128]{2,1,0:T(8,128)(2,1)S(1)}, u32[]{:S(2)}, u32[]{:S(2)}) collective-permute-start(bf16[32,16,128]{2,1,0:T(8,128)(2,1)S(1)} %get-tuple-element.27), channel_id=1, source_target_pairs={{0,2},{1,3},{2,4},{3,5},{4,6},{5,7},{6,0},{7,1},{8,10},{9,11},{10,... | collective-permute-start | bytes 393224 | tf_op jit(solution)/shard_map/ppermute | solution.py:312
  39.6 9.2 %collective-permute-start.1 = (bf16[32,16,128]{2,1,0:T(8,128)(2,1)S(1)}, bf16[32,16,128]{2,1,0:T(8,128)(2,1)S(1)}, u32[]{:S(2)}, u32[]{:S(2)}) collective-permute-start(bf16[32,16,128]{2,1,0:T(8,128)(2,1)S(1)} %get-tuple-element.30), channel_id=1, source_target_pairs={{0,4},{1,5},{2,6},{3,7},{4,0},{5,1},{6,2},{7,3},{8,12},{9,13},{10,... | collective-permute-start | bytes 393224 | tf_op jit(solution)/shard_map/ppermute | solution.py:312
  42.3 8.2 %collective-permute-start.2 = (bf16[32,16,128]{2,1,0:T(8,128)(2,1)S(1)}, bf16[32,16,128]{2,1,0:T(8,128)(2,1)S(1)}, u32[]{:S(2)}, u32[]{:S(2)}) collective-permute-start(bf16[32,16,128]{2,1,0:T(8,128)(2,1)S(1)} %get-tuple-element.31), channel_id=1, source_target_pairs={{0,6},{1,7},{2,0},{3,1},{4,2},{5,3},{6,4},{7,5},{8,14},{9,15},{10,... | collective-permute-start | bytes 393224 | tf_op jit(solution)/shard_map/ppermute | solution.py:312
  44.5 6.6 %collective-permute-start.3 = (bf16[32,16,128]{2,1,0:T(8,128)(2,1)S(1)}, bf16[32,16,128]{2,1,0:T(8,128)(2,1)S(1)}, u32[]{:S(2)}, u32[]{:S(2)}) collective-permute-start(bf16[32,16,128]{2,1,0:T(8,128)(2,1)S(1)} %get-tuple-element.26.own_0), channel_id=1, source_target_pairs={{0,1},{1,0},{2,3},{3,2},{4,5},{5,4},{6,7},{7,6},{8,9},{9,8},{10,11... | collective-permute-start | bytes 393224 | tf_op jit(solution)/shard_map/ppermute | solution.py:317
  48.8 2.3 %collective-permute-start.4 = (bf16[32,16,128]{2,1,0:T(8,128)(2,1)S(1)}, bf16[32,16,128]{2,1,0:T(8,128)(2,1)S(1)}, u32[]{:S(2)}, u32[]{:S(2)}) collective-permute-start(bf16[32,16,128]{2,1,0:T(8,128)(2,1)S(1)} %collective-permute-done.own_1), channel_id=1, source_target_pairs={{0,1},{1,0},{2,3},{3,2},{4,5},{5,4},{6,7},{7,6},{8,9},{9,8},{10,11... | collective-permute-start | bytes 393224 | tf_op jit(solution)/shard_map/ppermute | solution.py:317
  48.9 2.6 %collective-permute-start.5 = (bf16[32,16,128]{2,1,0:T(8,128)(2,1)S(1)}, bf16[32,16,128]{2,1,0:T(8,128)(2,1)S(1)}, u32[]{:S(2)}, u32[]{:S(2)}) collective-permute-start(bf16[32,16,128]{2,1,0:T(8,128)(2,1)S(1)} %collective-permute-done.1.own_2), channel_id=1, source_target_pairs={{0,1},{1,0},{2,3},{3,2},{4,5},{5,4},{6,7},{7,6},{8,9},{9,8},{10,11... | collective-permute-start | bytes 393224 | tf_op jit(solution)/shard_map/ppermute | solution.py:317
  50.5 1.6 %collective-permute-start.6 = (bf16[32,16,128]{2,1,0:T(8,128)(2,1)S(1)}, bf16[32,16,128]{2,1,0:T(8,128)(2,1)S(1)}, u32[]{:S(2)}, u32[]{:S(2)}) collective-permute-start(bf16[32,16,128]{2,1,0:T(8,128)(2,1)S(1)} %collective-permute-done.2.own_3), channel_id=1, source_target_pairs={{0,1},{1,0},{2,3},{3,2},{4,5},{5,4},{6,7},{7,6},{8,9},{9,8},{10,11... | collective-permute-start | bytes 393224 | tf_op jit(solution)/shard_map/ppermute | solution.py:317
  57.2 1.3 %collective-permute-start.7 = (bf16[3,16,256]{2,1,0:T(8,128)(2,1)S(1)}, bf16[3,16,256]{2,1,0:T(8,128)(2,1)S(1)}, u32[]{:S(2)}, u32[]{:S(2)}) collective-permute-start(bf16[3,16,256]{2,1,0:T(8,128)(2,1)S(1)} %get-tuple-element.36), channel_id=1, source_target_pairs={{0,1},{1,0},{2,3},{3,2},{4,5},{5,4},{6,7},{7,6},{8,9},{9,8},{10,11... | collective-permute-start | bytes 73736 | tf_op jit(solution)/shard_map/ppermute | solution.py:326
  58.5 3.9 %collective-permute-start.8 = (bf16[2,16,256]{2,1,0:T(8,128)(2,1)S(1)}, bf16[2,16,256]{2,1,0:T(8,128)(2,1)S(1)}, u32[]{:S(2)}, u32[]{:S(2)}) collective-permute-start(bf16[2,16,256]{2,1,0:T(8,128)(2,1)S(1)} %get-tuple-element.38), channel_id=1, source_target_pairs={{0,6},{1,7},{2,4},{3,5},{4,2},{5,3},{6,0},{7,1},{8,14},{9,15},{10,... | collective-permute-start | bytes 49160 | tf_op jit(solution)/shard_map/ppermute | solution.py:329
